TPU v7x, 768 devices: a whole 4x8x12 slice. The times are simulated.
768 devices in a mesh: pair: 12 (over z_lo, x), grow: 8 (over y), gcol: 8 (over z_hi, core).
Axes of the slice: x: 4, y: 8, z: 12 (z_hi: 4, z_lo: 3; z = z_hi * 3 + z_lo), core: 2. Of those that a mesh axis runs over, the one named last changes fastest.
Arguments:
- valence: bfloat16 [48, 32768], replicated, may hold values from -6 to 6
- conduction: bfloat16 [192, 32768], P('pair'), may hold values from -6 to 6
- valence_energy: float32 [48], replicated, may hold values from -12 to -1
- conduction_energy: float32 [192], P('pair'), may hold values from 0.5 to 8
- pair_valence: int32 [1536], P(('pair', 'grow', 'gcol')), may hold values from 0 to 47
- pair_conduction: int32 [1536], P(('pair', 'grow', 'gcol')), may hold values from 0 to 15
- pair_count: int32 [768], P(('pair', 'grow', 'gcol')), may hold values from 1 to 2, as said below
- g_index: int32 [9216], replicated, may hold values from 1 to 32767, as said below
Outputs:
- chi: float32 [9216, 9216], P(('pair', 'grow'), 'gcol')
Inputs may be any that keep to these rules, and one draw needn't show every extreme that they name: `pair_count`: every device has at least one live slot, and some device has exactly 2. `g_index`: distinct cells; with centred frequencies (an index v stands for v - 32 when v >= 16) they are the 9216 cells of smallest |G| other than G = 0 and the planes at frequency -16, closed under G -> -G, in no particular order.
All inputs are finite; a program needn't handle non-finite values.
Results may differ from a plain program's by a relative error of at most 0.0037.
Values may be sent and summed in bfloat16 or wider, within the bound.
No kernel may reach another device: no remote copies, remote signals or barrier semaphores. Data moves between devices by JAX's collectives and lax.ppermute only.
A program may use at most 128 MiB of HBM per device.

v0:
```python
import math

import jax
import jax.numpy as jnp
from jax import lax
from jax.sharding import PartitionSpec as P

GRID = 32


def dft_tables(length):
    points = jnp.arange(length, dtype=jnp.int32)
    phases = points[:, None] * points[None, :] % length
    angles = phases.astype(jnp.float32) * (2.0 * math.pi / length)
    return (jnp.cos(angles), jnp.sin(angles))


def transform(density):
    cosine_table, sine_table = dft_tables(density.shape[-1])
    highest = lax.Precision.HIGHEST
    real_part = jnp.einsum("pabn,nk->pabk", density, cosine_table, precision=highest)
    imag_part = -jnp.einsum("pabn,nk->pabk", density, sine_table, precision=highest)
    real_next = jnp.einsum(
        "panc,nk->pakc", real_part, cosine_table, precision=highest
    ) + jnp.einsum("panc,nk->pakc", imag_part, sine_table, precision=highest)
    imag_next = jnp.einsum(
        "panc,nk->pakc", imag_part, cosine_table, precision=highest
    ) - jnp.einsum("panc,nk->pakc", real_part, sine_table, precision=highest)
    real_last = jnp.einsum(
        "pnbc,nk->pkbc", real_next, cosine_table, precision=highest
    ) + jnp.einsum("pnbc,nk->pkbc", imag_next, sine_table, precision=highest)
    imag_last = jnp.einsum(
        "pnbc,nk->pkbc", imag_next, cosine_table, precision=highest
    ) - jnp.einsum("pnbc,nk->pkbc", real_next, sine_table, precision=highest)
    return (real_last, imag_last)


def local(
    valence,
    conduction,
    valence_energy,
    conduction_energy,
    pair_valence,
    pair_conduction,
    pair_count,
    g_index,
):
    slot_count = pair_valence.shape[0]
    total_g = g_index.shape[0]
    n_pair = lax.axis_size("pair")
    n_grow = lax.axis_size("grow")
    n_gcol = lax.axis_size("gcol")
    phi_valence = jnp.take(valence, pair_valence, axis=0).astype(jnp.float32)
    phi_conduction = jnp.take(conduction, pair_conduction, axis=0).astype(jnp.float32)
    density = (phi_valence * phi_conduction).reshape(slot_count, GRID, GRID, GRID)
    real_grid, imag_grid = transform(density)
    real_sel = jnp.take(real_grid.reshape(slot_count, -1), g_index, axis=1)
    imag_sel = jnp.take(imag_grid.reshape(slot_count, -1), g_index, axis=1)
    valence_pick = (
        pair_valence[:, None] == jnp.arange(valence_energy.shape[0], dtype=jnp.int32)[None, :]
    ).astype(jnp.float32)
    conduction_pick = (
        pair_conduction[:, None] == jnp.arange(conduction_energy.shape[0], dtype=jnp.int32)[None, :]
    ).astype(jnp.float32)
    energy_gap = jnp.sum(conduction_pick * conduction_energy[None, :], axis=1) - jnp.sum(
        valence_pick * valence_energy[None, :], axis=1
    )
    live_slots = (jnp.arange(slot_count, dtype=jnp.int32) < pair_count[0]).astype(jnp.float32)
    factor = live_slots * jnp.sqrt(4.0 / energy_gap) / jnp.sqrt(jnp.float32(GRID**3))
    amplitudes = jnp.concatenate(
        [real_sel * factor[:, None], imag_sel * factor[:, None]], axis=0
    ).astype(jnp.bfloat16)
    doubled = amplitudes.shape[0]
    sub_rows = total_g // (n_pair * n_grow)
    col_width = total_g // n_gcol
    by_rows = amplitudes.reshape(doubled, n_pair, n_grow, sub_rows)
    row_panel = lax.all_to_all(by_rows, "grow", split_axis=2, concat_axis=0, tiled=True)
    row_panel = row_panel.reshape(1, n_grow, doubled, n_pair * sub_rows)
    by_columns = amplitudes.reshape(doubled, n_gcol, col_width)
    col_panel = lax.all_to_all(by_columns, "gcol", split_axis=1, concat_axis=0, tiled=True)
    col_panel = lax.all_gather(
        col_panel.reshape(1, n_gcol, doubled, col_width), "grow", axis=0, tiled=True
    )
    all_rows = lax.all_gather(row_panel, "gcol", axis=0, tiled=True)
    partial_value = jnp.einsum(
        "crsa,rcsb->ab", all_rows, col_panel, preferred_element_type=jnp.float32
    )
    summed = lax.psum_scatter(partial_value, "pair", scatter_dimension=0, tiled=True)
    total_slots = slot_count * n_pair * n_grow * n_gcol
    return -summed / jnp.sqrt(jnp.float32(total_slots))


def solution(mesh):
    return jax.shard_map(
        local,
        mesh=mesh,
        in_specs=(
            P(),
            P("pair", None),
            P(),
            P("pair"),
            P(("pair", "grow", "gcol")),
            P(("pair", "grow", "gcol")),
            P(("pair", "grow", "gcol")),
            P(),
        ),
        out_specs=P(("pair", "grow"), "gcol"),
        check_vma=False,
    )
```

profile of v0, /device:TPU:192, one launch (start us, length us, event | category | flops | bytes accessed | tf_op | source)
XLA Modules:
  0.0 303.1 jit_solution(5822242822440442890)
XLA Ops:
  6.5 0.0 copy-start
  6.5 0.0 copy-start.3
  6.5 0.8 compare_select_fusion.2
  7.3 0.8 compare_and_fusion.1
  8.2 0.7 compare_select_fusion.1
  8.9 0.0 copy-done
  8.9 0.7 gather_fusion
  9.6 0.3 gather.16
  9.9 2.2 gather_fusion.1
  12.1 0.3 gather.18
  12.3 1.1 convolution_negate_fusion
  13.5 1.1 fusion.6
  14.6 0.0 copy-done.3
  14.7 1.1 fusion.25
  15.7 1.1 fusion.28
  16.8 1.1 fusion.4
  17.9 1.6 fusion.7
  19.5 1.1 fusion.5
  20.6 2.6 fusion.11
  23.2 1.8 fusion.2
  25.0 0.0 copy-start.2
  25.0 9.2 %copy.74 = f32[2,32,32,32]{0,3,2,1:T(8,128)} copy(f32[2,32,32,32]{3,1,2,0:T(8,128)S(1)} %fusion.2) | data formatting | bytes 524288 | tf_op jit(solution)/shard_map/reshape | solution.py:58
  34.2 0.0 copy-done.2
  34.2 1.6 fusion.3
  35.8 0.0 copy-start.4
  35.9 0.0 copy-start.6
  35.9 0.0 copy-start.5
  35.9 0.0 copy-start.7
  35.9 9.3 %copy.73 = f32[2,32,32,32]{0,3,2,1:T(8,128)} copy(f32[2,32,32,32]{3,1,2,0:T(8,128)S(1)} %fusion.3) | data formatting | bytes 524288 | tf_op jit(solution)/shard_map/reshape | solution.py:57
  45.2 36.9 %gather_fusion.3 = f32[9216,2]{1,0:T(8,128)} fusion(f32[2,32768]{0,1:T(8,128)} %bitcast.76, s32[9216]{0:T(1024)S(1)} %fusion.14), kind=kCustom, calls=%fused_computation.1.clone | custom fusion | bytes 184320 | tf_op jit(solution)/shard_map/jit(_take)/gather | solution.py:58
  82.1 37.0 %gather_fusion.2 = f32[9216,2]{1,0:T(8,128)} fusion(f32[2,32768]{0,1:T(8,128)} %bitcast.77, s32[9216]{0:T(1024)S(1)} %fusion.14), kind=kCustom, calls=%fused_computation.clone | custom fusion | bytes 184320 | tf_op jit(solution)/shard_map/jit(_take)/gather | solution.py:57
  119.7 0.0 copy-done.4
  119.7 0.0 copy-done.6
  119.7 0.2 fusion.45
  119.9 0.0 copy-done.5
  119.9 0.0 copy-done.7
  119.9 0.2 fusion.46
  120.1 8.4 %fusion.1 = (bf16[2,9216]{0,1:T(8,128)(2,1)}, bf16[2,9216]{0,1:T(8,128)(2,1)S(1)}) fusion(f32[9216,2]{1,0:T(8,128)} %gather_fusion.2, f32[2]{0:T(128)S(1)} %fusion.47, pred[9216]{0:T(1024)(128)(4,1)S(1)} %compare_and_fusion, f32[9216,2]{1,0:T(8,128)} %gather_fusion.3), kind=kLoop, calls=%fused_computation.8 | loop fusion | flops 110592 | bytes 230408 | tf_op jit(solution)/shard_map/convert.7
  128.5 2.2 copy.59
  130.7 1.1 copy.60
  131.8 0.8 pad_maximum_fusion
  132.5 7.1 %all-to-all-start = ((bf16[4,12,8,96]{3,0,1,2:T(4,128)(2,1)}), bf16[4,12,8,96]{3,0,1,2:T(4,128)(2,1)S(1)}, u32[]{:S(2)}, u32[]{:S(2)}) async-start(bf16[4,12,8,96]{3,0,1,2:T(4,128)(2,1)} %pad_maximum_fusion), calls=%async_computation | async-start | bytes 196608 | tf_op jit(solution)/shard_map/all_to_all | solution.py:77
  139.6 2.1 copy.62
  141.8 1.0 copy.63
  142.8 0.7 pad_maximum_fusion.1
  143.5 4.8 %all-to-all-done = bf16[4,12,8,96]{3,0,1,2:T(4,128)(2,1)S(1)} async-done(((bf16[4,12,8,96]{3,0,1,2:T(4,128)(2,1)}), bf16[4,12,8,96]{3,0,1,2:T(4,128)(2,1)S(1)}, u32[]{:S(2)}, u32[]{:S(2)}) %all-to-all-start) | async-done | bytes 73760 | tf_op jit(solution)/shard_map/all_to_all | solution.py:77
  148.4 12.3 %all-to-all-start.1 = ((bf16[4,8,1152]{2,0,1:T(4,128)(2,1)}), bf16[4,8,1152]{2,0,1:T(4,128)(2,1)S(1)}, u32[]{:S(2)}, u32[]{:S(2)}) async-start(bf16[4,8,1152]{2,0,1:T(4,128)(2,1)} %pad_maximum_fusion.1), calls=%async_computation.1 | async-start | bytes 147456 | tf_op jit(solution)/shard_map/all_to_all | solution.py:80
  160.7 0.0 reduce-scatter.2.cloned.1.call-start
  160.7 0.1 reshape.71
  160.9 21.6 %all_gather.6 = bf16[8,8,4,1152]{3,1,2,0:T(8,128)(2,1)} all-gather(bf16[1,8,4,1152]{3,1,2,0:T(8,128)(2,1)S(1)} %reshape.71), channel_id=1, replica_groups=mesh['pair'=12,'grow'=8,'gcol'=8] {'gcol'}, dimensions={0}, use_global_device_ids=true | all-gather | bytes 663552 | tf_op jit(solution)/shard_map/all_gather | solution.py:84
  182.4 0.0 all-to-all-done.1
  182.4 25.5 %all-gather = bf16[64,4,1,1152]{3,0,1,2:T(8,128)(2,1)S(1)} all-gather(bf16[8,4,1,1152]{3,0,1,2:T(8,128)(2,1)S(1)} %bitcast.80), channel_id=2, replica_groups=mesh['pair'=12,'grow'=8,'gcol'=8] {'grow'}, dimensions={0}, use_global_device_ids=true | all-gather | bytes 663552 | tf_op jit(solution)/shard_map/all_gather | solution.py:81
  207.9 0.0 copy-start.1
  207.9 4.5 %convolution_bitcast_fusion = f32[1152,1152]{1,0:T(8,128)} fusion(bf16[8,8,4,1152]{3,1,2,0:T(8,128)(2,1)} %all_gather.6, bf16[8,8,4,1152]{3,1,0,2:T(8,128)(2,1)S(1)} %bitcast.78), kind=kOutput, calls=%fused_computation.4 | convolution fusion | flops 679477248 | bytes 6488064 | tf_op jit(solution)/shard_map/crsa,rcsb->ab/dot_general | solution.py:85
  212.4 0.0 reduce-scatter.2.cloned.1.call-update
  212.5 82.0 %reduce-scatter.2.cloned.1.call-done = f32[96,1152]{1,0:T(8,128)} async-done(((f32[1152,1152]{1,0:T(8,128)}), f32[96,1152]{1,0:T(8,128)}) %reduce-scatter.2.cloned.1.call-update) | async-done | bytes 442384 | tf_op jit(solution)/shard_map/reduce_scatter | solution.py:88
  294.4 1.8 negate_multiply_fusion
  296.2 0.0 copy-done.1
  (7 shorter events, 0.1 us)
Async XLA Ops:
  6.5 2.3 copy-start
  6.5 8.1 %copy-start.3 = (s32[9216]{0:T(1024)S(1)}, s32[9216]{0:T(1024)}, u32[]{:S(2)}) copy-start(s32[9216]{0:T(1024)} %param.17) | copy-start | bytes 110596
  25.0 9.2 %copy-start.2 = (f32[32,2,32,32]{3,0,2,1:T(8,128)S(1)}, f32[32,2,32,32]{3,0,2,1:T(8,128)}, u32[]{:S(2)}) copy-start(f32[32,2,32,32]{3,0,2,1:T(8,128)} %fusion.11) | copy-start | bytes 786436
  35.8 83.9 %copy-start.4 = (s32[2]{0:T(128)S(1)}, s32[2]{0:T(128)}, u32[]{:S(2)}) copy-start(s32[2]{0:T(128)} %param.15) | copy-start | bytes 28
  35.9 83.9 %copy-start.6 = (f32[16]{0:T(128)S(1)}, f32[16]{0:T(128)}, u32[]{:S(2)}) copy-start(f32[16]{0:T(128)} %param.13) | copy-start | bytes 196
  35.9 84.0 %copy-start.5 = (s32[2]{0:T(128)S(1)}, s32[2]{0:T(128)}, u32[]{:S(2)}) copy-start(s32[2]{0:T(128)} %param.14) | copy-start | bytes 28
  35.9 84.0 %copy-start.7 = (f32[48]{0:T(128)S(1)}, f32[48]{0:T(128)}, u32[]{:S(2)}) copy-start(f32[48]{0:T(128)} %param.12) | copy-start | bytes 580
  132.5 15.8 %all-to-all-start = ((bf16[4,12,8,96]{3,0,1,2:T(4,128)(2,1)}), bf16[4,12,8,96]{3,0,1,2:T(4,128)(2,1)S(1)}, u32[]{:S(2)}, u32[]{:S(2)}) async-start(bf16[4,12,8,96]{3,0,1,2:T(4,128)(2,1)} %pad_maximum_fusion), calls=%async_computation | async-start | bytes 196608 | tf_op jit(solution)/shard_map/all_to_all | solution.py:77
  148.4 34.1 %all-to-all-start.1 = ((bf16[4,8,1152]{2,0,1:T(4,128)(2,1)}), bf16[4,8,1152]{2,0,1:T(4,128)(2,1)S(1)}, u32[]{:S(2)}, u32[]{:S(2)}) async-start(bf16[4,8,1152]{2,0,1:T(4,128)(2,1)} %pad_maximum_fusion.1), calls=%async_computation.1 | async-start | bytes 147456 | tf_op jit(solution)/shard_map/all_to_all | solution.py:80
  160.7 133.7 %reduce-scatter.2.cloned.1.call-start = ((), (), s32[]{:S(2)}) async-start(), calls=%async_computation.3 | async-start | bytes 5750784 | tf_op jit(solution)/shard_map/reduce_scatter | solution.py:88
  207.9 88.3 %copy-start.1 = (bf16[48,32768]{1,0:T(8,128)(2,1)S(1)}, bf16[48,32768]{1,0:T(8,128)(2,1)}, u32[]{:S(2)}) copy-start(bf16[48,32768]{1,0:T(8,128)(2,1)} %param.10) | copy-start | bytes 9437188
Sparse Core Ops, SparseCore 0:
  212.6 81.7 reduce-scatter.1
where the time goes:
time: 304 us; the launch traced here: 303 us
  local copies, waits for them, and re-layouts  102 us (34%)
  waiting for transfers between devices  86.8 us (29%)
  blocking collectives  47 us (15%)
  starting transfers between devices  19.4 us (6%)
  matrix products  18.7 us (6%)
  other arithmetic  14.4 us (5%)
  between operations  14.3 us (5%)
    reduce_scatter x1, waiting for transfers between devices, local(): lax.psum_scatter(partial_value, 'pair', scatter_dimension=0, tiled=True)  82 us
    gather x1, local copies, waits for them, and re-layouts, local(): real_sel = jnp.take(real_grid.reshape(slot_count, -1), g_index, axis=1)  37 us
    gather x1, local copies, waits for them, and re-layouts, local(): imag_sel = jnp.take(imag_grid.reshape(slot_count, -1), g_index, axis=1)  36.9 us
    all_gather x1, blocking collectives, local(): lax.all_gather(col_panel.reshape(1, n_gcol, doubled, col_width), 'grow',...  25.5 us
    all_gather x1, blocking collectives, local(): all_rows = lax.all_gather(row_panel, 'gcol', axis=0, tiled=True)  21.6 us
    all_to_all x1, starting transfers between devices, local(): lax.all_to_all(by_columns, 'gcol', split_axis=1, concat_axis=0, tiled=True)  12.3 us
    reshape x1, local copies, waits for them, and re-layouts, local(): real_sel = jnp.take(real_grid.reshape(slot_count, -1), g_index, axis=1)  9.27 us
    reshape x1, local copies, waits for them, and re-layouts, local(): imag_sel = jnp.take(imag_grid.reshape(slot_count, -1), g_index, axis=1)  9.23 us
  transfers between devices with their start and end apart: 3, of which 2 were waited for; matrix products, arithmetic and copies ran while one was open for 1% of the time, Pallas kernels for 0%

commit v1 on v0

v1 whole, which is shorter than its diff:
```python
import numpy as np
import ml_dtypes

import jax
import jax.numpy as jnp
from jax import lax
from jax.experimental import pallas as pl
from jax.experimental.pallas import tpu as pltpu
from jax.sharding import PartitionSpec as P

GRID = 32
NX = 4
LANES = 128
ROWS = 256
CHUNK = 384


def split(table):
    high = table.astype(ml_dtypes.bfloat16)
    low = (table - high.astype(np.float64)).astype(ml_dtypes.bfloat16)
    return high, low


def tables():
    turn = 2.0 * np.pi / GRID
    phase = turn * np.outer(np.arange(32), np.arange(16))
    first = np.concatenate(
        [np.kron(np.eye(4), np.cos(phase)), np.kron(np.eye(4), -np.sin(phase))], axis=1
    )
    high, low = split(first)
    both = np.concatenate([high, low], axis=1)
    lane_table = np.concatenate([both, both], axis=0)
    a_half = np.repeat(np.arange(16), 8)
    beta_half = np.tile(np.arange(8), 16)
    i_row = np.repeat(np.arange(32), 8)
    j_row = np.tile(np.arange(8), 32)
    phase = 2.0 * np.pi * (np.outer(a_half, i_row) / 32.0 + np.outer(beta_half, j_row) / 8.0)
    high, low = split(np.concatenate([np.cos(phase), np.sin(phase)], axis=0))
    row_table = np.concatenate([high, high, low], axis=1)
    beta = np.concatenate([beta_half, (8 - beta_half) % 8])
    angle = turn * np.outer(beta, np.repeat(np.arange(4), 16))
    twiddle_same = np.concatenate([np.cos(angle), np.cos(angle)], axis=1).astype(np.float32)
    twiddle_swap = np.concatenate([np.sin(angle), -np.sin(angle)], axis=1).astype(np.float32)
    step = np.outer(np.arange(4), np.arange(4)) % 4
    real = np.array([1, 0, -1, 0])[step]
    imag = np.array([0, -1, 0, 1])[step]
    last = np.block([[np.kron(real, np.eye(16)), np.kron(imag, np.eye(16))],
                     [np.kron(-imag, np.eye(16)), np.kron(real, np.eye(16))]])
    last_table = np.concatenate([last, last], axis=0).astype(ml_dtypes.bfloat16)
    return lane_table, row_table, twiddle_same, twiddle_swap, last_table


def halves(value):
    high = value.astype(jnp.bfloat16)
    low = (value - high.astype(jnp.float32)).astype(jnp.bfloat16)
    return high, low


def dot(left, right):
    return jnp.dot(left, right, preferred_element_type=jnp.float32)


def select(cells, amplitudes):
    first = cells >> 10
    second = (cells >> 5) & 31
    third = cells & 31
    flip = third >= 16
    first = jnp.where(flip, (32 - first) & 31, first)
    second = jnp.where(flip, (32 - second) & 31, second)
    third = jnp.where(flip, 32 - third, third)
    sign = jnp.where(flip, -1.0, 1.0)
    beta = second & 7
    row = jnp.where(
        first > 16, 128 + (32 - first) * 8 + ((8 - beta) & 7), first * 8 + beta
    )
    lane = (second >> 3) * 16 + third
    width = cells.shape[-1]
    hot = (lax.broadcasted_iota(jnp.int32, (ROWS, width), 0) == row).astype(jnp.bfloat16)
    picked = dot(amplitudes, hot)
    mask = lax.broadcasted_iota(jnp.int32, (64, width), 0) == lane
    parts = []
    for part in range(4):
        block = jnp.where(mask, picked[part * 64:part * 64 + 64], 0.0)
        total = jnp.sum(block, axis=0, keepdims=True)
        parts.append(total * sign if part % 2 else total)
    return jnp.concatenate(parts, axis=0).astype(jnp.bfloat16)


def amplitude_kernel(pv_ref, pc_ref, count_ref, ve_ref, ce_ref, valence_ref, conduction_ref,
                     lane_ref, row_ref, same_ref, swap_ref, last_ref, gcol_ref, grow_ref,
                     col_ref, rowout_ref, bands, wide, amp, sems):
    slots = 2
    copies = []
    for slot in range(slots):
        start = pl.multiple_of(pv_ref[slot] // 16 * 16, 16)
        copies.append(pltpu.make_async_copy(
            valence_ref.at[pl.ds(start, 16), :], bands.at[slot], sems.at[slot]))
    copies.append(pltpu.make_async_copy(conduction_ref, bands.at[slots], sems.at[slots]))
    for copy in copies:
        copy.start()
    for copy in copies:
        copy.wait()

    def widen(tile, carry):
        lanes = pl.ds(pl.multiple_of(tile * LANES, LANES), LANES)
        rows = pl.ds(pl.multiple_of(tile * 16, 16), 16)
        for band in range(slots + 1):
            wide[band, rows, :] = bands[band, :, lanes].astype(jnp.float32)
        return carry

    lax.fori_loop(0, ROWS, widen, 0, unroll=8)

    stage = []
    for slot in range(slots):
        left = wide[slot, pl.ds(pv_ref[slot] % 16, ROWS, stride=16), :]
        right = wide[slots, pl.ds(pc_ref[slot], ROWS, stride=16), :]
        high, low = halves(left * right)
        out = dot(jnp.concatenate([high, low], axis=1), lane_ref[...])
        stage.append(out[:, :LANES] + out[:, LANES:])
    high, low = halves(jnp.concatenate(stage, axis=1))
    out = dot(row_ref[...], jnp.concatenate([high, low, high], axis=0))
    lane_id = lax.broadcasted_iota(jnp.int32, (LANES, LANES), 1)
    for slot in range(slots):
        lanes = slice(slot * LANES, slot * LANES + LANES)
        cosine, sine = out[:LANES, lanes], out[LANES:, lanes]
        turned = pltpu.roll(sine, 64, 1)
        turned = jnp.where(lane_id < 64, turned, -turned)
        full = jnp.concatenate([cosine + turned, cosine - turned], axis=0)
        full = full * same_ref[...] + pltpu.roll(full, 64, 1) * swap_ref[...]
        high, low = halves(full)
        spectrum = dot(jnp.concatenate([high, low], axis=1), last_ref[...])
        gap = ce_ref[pc_ref[slot]] - ve_ref[pv_ref[slot]]
        live = jnp.where(slot < count_ref[0], 1.0, 0.0)
        factor = live * jnp.sqrt(4.0 / jnp.full((1, LANES), gap, jnp.float32)) / np.float32(
            np.sqrt(np.float32(GRID**3)))
        amp[slot * LANES:slot * LANES + LANES, :] = (spectrum * factor).T.astype(jnp.bfloat16)

    parts = col_ref.shape[2] // CHUNK

    def pick_columns(block, carry):
        for part in range(parts):
            cells = gcol_ref[pl.ds(block * parts + part, 1), :]
            col_ref[block, :, part * CHUNK:part * CHUNK + CHUNK] = select(cells, amp[...])
        return carry

    def pick_rows(block, carry):
        picked = select(grow_ref[pl.ds(block, 1), :], amp[...])
        rowout_ref[block] = picked[:, :rowout_ref.shape[2]]
        return carry

    lax.fori_loop(0, rowout_ref.shape[0], pick_rows, 0)
    lax.fori_loop(0, col_ref.shape[0], pick_columns, 0)


def amplitudes_of(pv, pc, count, ve, ce, valence, conduction, gcol, grow, col_shape, row_shape):
    smem = pl.BlockSpec(memory_space=pltpu.SMEM)
    vmem = pl.BlockSpec(memory_space=pltpu.VMEM)
    hbm = pl.BlockSpec(memory_space=pl.ANY)
    return pl.pallas_call(
        amplitude_kernel,
        out_shape=(jax.ShapeDtypeStruct(col_shape, jnp.bfloat16),
                   jax.ShapeDtypeStruct(row_shape, jnp.bfloat16)),
        in_specs=[smem] * 5 + [hbm] * 2 + [vmem] * 7,
        out_specs=(vmem, vmem),
        scratch_shapes=[
            pltpu.VMEM((3, 16, GRID**3), jnp.bfloat16),
            pltpu.VMEM((3, 16 * ROWS, LANES), jnp.float32),
            pltpu.VMEM((ROWS, ROWS), jnp.bfloat16),
            pltpu.SemaphoreType.DMA((3,)),
        ],
        compiler_params=pltpu.CompilerParams(vmem_limit_bytes=40 * 1024 * 1024),
        cost_estimate=pl.CostEstimate(flops=4 * 10**9, bytes_accessed=5 * 10**6, transcendentals=0),
    )(pv, pc, count, ve, ce, valence, conduction, *(jnp.asarray(t) for t in tables()), gcol, grow)


def local(valence, conduction, valence_energy, conduction_energy, pair_valence, pair_conduction,
          pair_count, g_index):
    n_pair, n_grow, n_gcol = (lax.axis_size(name) for name in ("pair", "grow", "gcol"))
    n_z = n_pair // NX
    total_g = g_index.shape[0]
    doubled = 2 * pair_valence.shape[0]
    width = total_g // n_gcol
    sub = total_g // (n_pair * n_grow)
    n_xy = NX * n_grow
    x_groups = [[z * NX + x for x in range(NX)] for z in range(n_z)]
    z_groups = [[z * NX + x for z in range(n_z)] for x in range(NX)]
    xy_groups = [[(z * NX + x) * n_grow + y for x in range(NX) for y in range(n_grow)]
                 for z in range(n_z)]
    g_rows = g_index.reshape(n_z, n_xy, sub).transpose(1, 0, 2).reshape(n_xy, n_z * sub)
    g_rows = jnp.pad(g_rows, ((0, 0), (0, CHUNK - n_z * sub)))
    col, row = amplitudes_of(
        pair_valence, pair_conduction, pair_count, valence_energy, conduction_energy,
        valence, conduction, g_index.reshape(total_g // CHUNK, CHUNK), g_rows,
        (n_gcol, doubled, width), (n_xy, doubled, n_z * sub))
    row = lax.all_to_all(row, ("pair", "grow"), 0, 0, tiled=True, axis_index_groups=xy_groups)
    col = lax.all_to_all(col, "gcol", 0, 0, tiled=True)
    row = lax.all_gather(row.reshape(1, n_xy * doubled, n_z * sub), "gcol", axis=0, tiled=True)
    col = lax.all_gather(col.reshape(1, n_gcol * doubled, width), "grow", axis=0, tiled=True)
    col = lax.all_gather(col, "pair", axis=0, tiled=True, axis_index_groups=x_groups)
    row = row.reshape(n_gcol, n_xy, doubled, n_z * sub).transpose(1, 0, 2, 3)
    row = row.reshape(-1, n_z * sub)
    col = col.reshape(-1, width)
    partial = lax.dot_general(row, col, (((0,), (0,)), ((), ())),
                              preferred_element_type=jnp.float32)
    partial = partial.astype(jnp.bfloat16).reshape(n_z, sub, width)
    partial = lax.all_to_all(partial, "pair", 0, 0, tiled=True, axis_index_groups=z_groups)
    summed = jnp.sum(partial.astype(jnp.float32), axis=0)
    total_slots = pair_valence.shape[0] * n_pair * n_grow * n_gcol
    return -summed / jnp.sqrt(jnp.float32(total_slots))


def solution(mesh):
    return jax.shard_map(
        local,
        mesh=mesh,
        in_specs=(
            P(),
            P("pair", None),
            P(),
            P("pair"),
            P(("pair", "grow", "gcol")),
            P(("pair", "grow", "gcol")),
            P(("pair", "grow", "gcol")),
            P(),
        ),
        out_specs=P(("pair", "grow"), "gcol"),
        check_vma=False,
    )
```

time: 304 us -> 154 us (0.51)
  the two profiles are of different devices: /device:TPU:192 before, /device:TPU:1 now
where the time goes in v1:
time: 154 us; the launch traced here: 153 us
  blocking collectives  108 us (70%)
  between operations  14.1 us (9%)
  Pallas kernels  14 us (9%)
  local copies, waits for them, and re-layouts  13.5 us (9%)
  matrix products  2.63 us (2%)
    all_to_all x1, blocking collectives, local(): col = lax.all_to_all(col, 'gcol', 0, 0, tiled=True)  26.2 us
    all_gather x1, blocking collectives, local(): lax.all_gather(row.reshape(1, n_xy * doubled, n_z * sub), 'gcol', axis=0,...  26.2 us
    all_gather x1, blocking collectives, local(): lax.all_gather(col.reshape(1, n_gcol * doubled, width), 'grow', axis=0, t...  23.6 us
    all_to_all x1, blocking collectives, local(): lax.all_to_all(row, ('pair', 'grow'), 0, 0, tiled=True, axis_index_groups...  16.6 us
    all_to_all x1, blocking collectives, local(): lax.all_to_all(partial, 'pair', 0, 0, tiled=True, axis_index_groups=z_gro...  15.4 us
    pallas_call x1, Pallas kernels, amplitudes_of(): pl.pallas_call(amplitude_kernel, out_shape=(jax.ShapeDtypeStruct(col_shap...  14 us
    unnamed x22, local copies, waits for them, and re-layouts  10.3 us
  transfers between devices with their start and end apart: 1, of which 0 were waited for; matrix products, arithmetic and copies ran while one was open for 1% of the time, Pallas kernels for 0%

profile of v1, /device:TPU:1, one launch (start us, length us, event | category | flops | bytes accessed | tf_op | source)
XLA Modules:
  0.0 153.1 jit_solution(3855075833307639258)
XLA Ops:
  6.5 0.0 all-gather.2.cloned.1.call-start
  6.5 0.8 reshape.28
  7.4 0.8 reshape.27.gcol_ref
  8.2 0.1 reshape.29
  9.0 0.0 copy-start
  9.0 1.9 %copy-done = bf16[48,32768]{1,0:T(8,128)(2,1)S(1)} copy-done((bf16[48,32768]{1,0:T(8,128)(2,1)S(1)}, bf16[48,32768]{1,0:T(8,128)(2,1)}, u32[]{:S(2)}) %copy-start) | copy-done | bytes 3145752
  10.9 0.0 copy-start.1
  10.9 1.2 copy-done.1
  12.1 0.0 copy-start.2
  12.1 0.7 copy-done.2
  12.7 0.0 copy-start.3
  12.7 0.7 copy-done.3
  13.4 0.0 copy-start.4
  13.4 0.7 copy-done.4
  14.1 0.0 copy-start.5
  14.1 0.7 copy-done.5
  14.7 0.0 copy-start.6
  14.7 1.0 copy-done.6
  15.7 0.0 copy-start.7
  15.7 0.9 copy-done.7
  16.6 0.0 copy-start.8
  16.6 0.9 copy-done.8
  17.5 0.0 copy-start.9
  17.5 0.9 copy-done.9
  18.4 0.0 copy-start.10
  18.4 0.8 copy-done.10
  19.3 14.0 %shard_map.127 = (bf16[8,4,1152]{2,1,0:T(4,128)(2,1)S(1)}, bf16[32,4,288]{2,1,0:T(4,128)(2,1)S(1)}) custom-call(s32[2]{0:T(128)S(1)} %copy-done.2, s32[2]{0:T(128)S(1)} %copy-done.3, s32[1]{0:T(128)S(6)} %copy.21.count_ref, f32[48]{0:T(128)S(1)} %copy-done.4, f32[16]{0:T(128)S(1)} %copy-done.5, bf16[48,32768]{1,0:T(8,128)(2,1)S(1)} %copy-done, ...), custom_call_target="tpu_custom_call" | custom-call | flops 4000000000 | bytes 5000000 | tf_op jit(solution)/shard_map/pallas_call | solution.py:159
  33.3 26.2 %all_to_all.15 = bf16[8,4,1152]{2,1,0:T(4,128)(2,1)S(1)} all-to-all(bf16[8,4,1152]{2,1,0:T(4,128)(2,1)S(1)} %get-tuple-element.8), channel_id=1, replica_groups=mesh['pair'=12,'grow'=8,'gcol'=8] {'gcol'}, dimensions={0} | all-to-all | bytes 147456 | tf_op jit(solution)/shard_map/all_to_all | solution.py:196
  59.5 23.6 %all_gather.10 = bf16[8,32,1152]{2,1,0:T(8,128)(2,1)} all-gather(bf16[1,32,1152]{2,1,0:T(8,128)(2,1)S(1)} %reshape.33), channel_id=1, replica_groups=mesh['pair'=12,'grow'=8,'gcol'=8] {'grow'}, dimensions={0}, use_global_device_ids=true | all-gather | bytes 663552 | tf_op jit(solution)/shard_map/all_gather | solution.py:198
  83.1 0.0 all-gather.2.cloned.1.call-update
  83.1 16.6 %all_to_all.16 = bf16[32,4,288]{2,1,0:T(4,128)(2,1)S(1)} all-to-all(bf16[32,4,288]{2,1,0:T(4,128)(2,1)S(1)} %get-tuple-element.7), channel_id=1, replica_groups={{0,8,16,24,32,40,48,56,64,72,80,88,96,104,112,120,128,136,144,152,160,1..., dimensions={0} | all-to-all | bytes 147456 | tf_op jit(solution)/shard_map/all_to_all | solution.py:195
  99.7 0.1 reshape.30
  99.8 0.1 copy.18
  99.9 26.2 %all_gather.9 = bf16[8,128,288]{1,2,0:T(8,128)(2,1)S(1)} all-gather(bf16[1,128,288]{1,2,0:T(8,128)(2,1)S(1)} %copy.18), channel_id=1, replica_groups=mesh['pair'=12,'grow'=8,'gcol'=8] {'gcol'}, dimensions={0}, use_global_device_ids=true | all-gather | bytes 663552 | tf_op jit(solution)/shard_map/all_gather | solution.py:197
  126.1 0.5 copy.19
  126.6 0.3 copy.20
  126.9 0.4 reshape.32
  127.3 0.0 all-gather.2.cloned.1.call-done
  127.4 2.6 %convolution_convert_fusion = bf16[288,1152]{1,0:T(8,128)(2,1)S(1)} fusion(bf16[1024,288]{1,0:T(8,128)(2,1)S(1)} %reshape.32, bf16[1024,1152]{1,0:T(8,128)(2,1)} %bitcast.10), kind=kOutput, calls=%fused_computation | convolution fusion | flops 679809024 | bytes 3612672 | tf_op jit(solution)/shard_map/dot_general | solution.py:203
  130.0 15.4 %all_to_all.17 = bf16[3,96,1152]{2,1,0:T(8,128)(2,1)S(1)} all-to-all(bf16[3,96,1152]{2,1,0:T(8,128)(2,1)S(1)} %bitcast.8), channel_id=1, replica_groups={{0,256,512},{64,320,576},{128,384,640},{192,448,704},{1,257,513},{65,32..., dimensions={0} | all-to-all | bytes 1327104 | tf_op jit(solution)/shard_map/all_to_all | solution.py:206
  145.4 0.1 convert_reduce_fusion
  145.5 0.8 negate_multiply_fusion
  (3 shorter events, 0.1 us)
Async XLA Ops:
  6.5 120.8 %all-gather.2.cloned.1.call-start = ((), (), s32[]{:S(2)}) async-start(), calls=%async_computation.3 | async-start | bytes 2949120 | tf_op jit(solution)/shard_map/all_gather | solution.py:199
  9.0 1.9 %copy-start = (bf16[48,32768]{1,0:T(8,128)(2,1)S(1)}, bf16[48,32768]{1,0:T(8,128)(2,1)}, u32[]{:S(2)}) copy-start(bf16[48,32768]{1,0:T(8,128)(2,1)} %valence_ref.1) | copy-start | bytes 9437188
  10.9 1.2 copy-start.1
  12.1 0.7 copy-start.2
  12.7 0.7 copy-start.3
  13.4 0.7 copy-start.4
  14.1 0.7 copy-start.5
  14.7 1.0 copy-start.6
  15.7 0.9 copy-start.7
  16.6 0.9 copy-start.8
  17.5 0.9 copy-start.9
  18.4 0.8 copy-start.10
Sparse Core Ops, SparseCore 0:
  83.2 40.5 all-gather.1

commit v2 on v1

--- a/solution.py
+++ b/solution.py
@@ -83,37 +83,51 @@
         block = jnp.where(mask, picked[part * 64:part * 64 + 64], 0.0)
         total = jnp.sum(block, axis=0, keepdims=True)
         parts.append(total * sign if part % 2 else total)
-    return jnp.concatenate(parts, axis=0).astype(jnp.bfloat16)
-
-
-def amplitude_kernel(pv_ref, pc_ref, count_ref, ve_ref, ce_ref, valence_ref, conduction_ref,
-                     lane_ref, row_ref, same_ref, swap_ref, last_ref, gcol_ref, grow_ref,
-                     col_ref, rowout_ref, bands, wide, amp, sems):
+    return jnp.concatenate(parts, axis=0)
+
+
+def lane_tiles(width):
+    return [(lane, min(LANES, width - lane)) for lane in range(0, width, LANES)]
+
+
+def amplitude_kernel(pv_hbm, pc_hbm, count_hbm, ve_hbm, ce_hbm, valence_hbm, conduction_hbm,
+                     lane_hbm, row_hbm, same_hbm, swap_hbm, last_hbm, g_hbm,
+                     out_ref, pv_ref, pc_ref, count_ref, ve_ref, ce_ref, valence_ref,
+                     conduction_ref, lane_ref, row_ref, same_ref, swap_ref, last_ref, g_ref,
+                     wide, amp, flat, ordered, sems):
     slots = 2
-    copies = []
-    for slot in range(slots):
-        start = pl.multiple_of(pv_ref[slot] // 16 * 16, 16)
-        copies.append(pltpu.make_async_copy(
-            valence_ref.at[pl.ds(start, 16), :], bands.at[slot], sems.at[slot]))
-    copies.append(pltpu.make_async_copy(conduction_ref, bands.at[slots], sems.at[slots]))
+    sub = out_ref.shape[2] // 3
+    n_xy = out_ref.shape[1] // (2 * slots)
+    sources = (pv_hbm, pc_hbm, conduction_hbm, valence_hbm, lane_hbm, row_hbm, same_hbm,
+               swap_hbm, last_hbm, g_hbm, count_hbm, ve_hbm, ce_hbm)
+    targets = (pv_ref, pc_ref, conduction_ref, valence_ref, lane_ref, row_ref, same_ref,
+               swap_ref, last_ref, g_ref, count_ref, ve_ref, ce_ref)
+    copies = [pltpu.make_async_copy(source, target, sems.at[at])
+              for at, (source, target) in enumerate(zip(sources, targets))]
     for copy in copies:
         copy.start()
-    for copy in copies:
+    for copy in copies[:4]:
         copy.wait()
+    picks = [(valence_ref, pv_ref[slot]) for slot in range(slots)]
+    picks += [(conduction_ref, pc_ref[slot]) for slot in range(slots)]
 
     def widen(tile, carry):
         lanes = pl.ds(pl.multiple_of(tile * LANES, LANES), LANES)
-        rows = pl.ds(pl.multiple_of(tile * 16, 16), 16)
-        for band in range(slots + 1):
-            wide[band, rows, :] = bands[band, :, lanes].astype(jnp.float32)
+        rows = pl.ds(pl.multiple_of(tile * 8, 8), 8)
+        for at, (ref, band) in enumerate(picks):
+            start = pl.multiple_of(band // 16 * 16, 16)
+            block = ref[pl.ds(start, 16), lanes].astype(jnp.float32)
+            wide[at, rows, :] = jnp.where(band % 16 >= 8, block[8:], block[:8])
         return carry
 
     lax.fori_loop(0, ROWS, widen, 0, unroll=8)
+    for copy in copies[4:]:
+        copy.wait()
 
     stage = []
     for slot in range(slots):
-        left = wide[slot, pl.ds(pv_ref[slot] % 16, ROWS, stride=16), :]
-        right = wide[slots, pl.ds(pc_ref[slot], ROWS, stride=16), :]
+        left = wide[slot, pl.ds(pv_ref[slot] % 8, ROWS, stride=8), :]
+        right = wide[slots + slot, pl.ds(pc_ref[slot] % 8, ROWS, stride=8), :]
         high, low = halves(left * right)
         out = dot(jnp.concatenate([high, low], axis=1), lane_ref[...])
         stage.append(out[:, :LANES] + out[:, LANES:])
@@ -135,42 +149,121 @@
             np.sqrt(np.float32(GRID**3)))
         amp[slot * LANES:slot * LANES + LANES, :] = (spectrum * factor).T.astype(jnp.bfloat16)
 
-    parts = col_ref.shape[2] // CHUNK
-
-    def pick_columns(block, carry):
-        for part in range(parts):
-            cells = gcol_ref[pl.ds(block * parts + part, 1), :]
-            col_ref[block, :, part * CHUNK:part * CHUNK + CHUNK] = select(cells, amp[...])
+    per = CHUNK // LANES
+
+    def pick(chunk, carry):
+        cells = jnp.concatenate(
+            [g_ref[pl.ds(chunk * per + at, 1), :] for at in range(per)], axis=1)
+        lanes = pl.ds(pl.multiple_of(chunk * CHUNK, CHUNK), CHUNK)
+        flat[0:4, lanes] = select(cells, amp[...])
         return carry
 
-    def pick_rows(block, carry):
-        picked = select(grow_ref[pl.ds(block, 1), :], amp[...])
-        rowout_ref[block] = picked[:, :rowout_ref.shape[2]]
-        return carry
-
-    lax.fori_loop(0, rowout_ref.shape[0], pick_rows, 0)
-    lax.fori_loop(0, col_ref.shape[0], pick_columns, 0)
-
-
-def amplitudes_of(pv, pc, count, ve, ce, valence, conduction, gcol, grow, col_shape, row_shape):
-    smem = pl.BlockSpec(memory_space=pltpu.SMEM)
-    vmem = pl.BlockSpec(memory_space=pltpu.VMEM)
-    hbm = pl.BlockSpec(memory_space=pl.ANY)
+    lax.fori_loop(0, flat.shape[1] // CHUNK, pick, 0, unroll=3)
+    for place in range(n_xy):
+        starts = [(z * n_xy + place) * sub for z in range(3)]
+        block = jnp.concatenate([flat[0:4, at:at + sub] for at in starts], axis=1)
+        for at, (lane, size) in enumerate(lane_tiles(3 * sub)):
+            part = block[:, lane:lane + size]
+            if size < LANES:
+                part = jnp.concatenate(
+                    [part, jnp.zeros((4, LANES - size), jnp.float32)], axis=1)
+            ordered[at, pl.ds(place, 4, stride=n_xy), :] = part
+    for at, (lane, size) in enumerate(lane_tiles(3 * sub)):
+        out_ref[0, :, lane:lane + size] = ordered[at, :, :size].astype(jnp.bfloat16)
+
+
+def amplitudes_of(pv, pc, count, ve, ce, valence, conduction, g_index, n_xy, wide_sub):
+    hbm = pl.BlockSpec(memory_space=pltpu.HBM)
+    consts = [jnp.asarray(table) for table in tables()]
+    g_rows = g_index.reshape(-1, LANES)
+    arrays = [valence, conduction, *consts, g_rows]
+    doubled = 2 * pv.shape[0]
     return pl.pallas_call(
         amplitude_kernel,
-        out_shape=(jax.ShapeDtypeStruct(col_shape, jnp.bfloat16),
-                   jax.ShapeDtypeStruct(row_shape, jnp.bfloat16)),
-        in_specs=[smem] * 5 + [hbm] * 2 + [vmem] * 7,
-        out_specs=(vmem, vmem),
-        scratch_shapes=[
-            pltpu.VMEM((3, 16, GRID**3), jnp.bfloat16),
-            pltpu.VMEM((3, 16 * ROWS, LANES), jnp.float32),
+        out_shape=jax.ShapeDtypeStruct((1, doubled * n_xy, wide_sub), jnp.bfloat16),
+        in_specs=[hbm] * 13,
+        out_specs=pl.BlockSpec(memory_space=pltpu.VMEM),
+        scratch_shapes=[pltpu.SMEM(a.shape, a.dtype) for a in (pv, pc, count, ve, ce)]
+        + [pltpu.VMEM(a.shape, a.dtype) for a in arrays]
+        + [
+            pltpu.VMEM((4, 8 * ROWS, LANES), jnp.float32),
             pltpu.VMEM((ROWS, ROWS), jnp.bfloat16),
-            pltpu.SemaphoreType.DMA((3,)),
+            pltpu.VMEM((8, g_index.shape[0]), jnp.float32),
+            pltpu.VMEM((-(-wide_sub // LANES), doubled * n_xy, LANES), jnp.float32),
+            pltpu.SemaphoreType.DMA((13,)),
         ],
         compiler_params=pltpu.CompilerParams(vmem_limit_bytes=40 * 1024 * 1024),
         cost_estimate=pl.CostEstimate(flops=4 * 10**9, bytes_accessed=5 * 10**6, transcendentals=0),
-    )(pv, pc, count, ve, ce, valence, conduction, *(jnp.asarray(t) for t in tables()), gcol, grow)
+    )(pv, pc, count, ve, ce, *arrays)
+
+
+def deal_kernel(mine_ref, all_ref, rows_ref, col_ref, wide):
+    n_xy, depth, wide_sub = rows_ref.shape
+    sub = wide_sub // 3
+    blocks = col_ref.shape[1] // depth * 3
+    tiles = lane_tiles(wide_sub)
+    for at, (lane, size) in enumerate(tiles):
+        block = all_ref[:, :, lane:lane + size].astype(jnp.float32)
+        wide[at, :, :size] = block.reshape(n_xy * depth, size)
+    for place in range(n_xy):
+        for at, (lane, size) in enumerate(tiles):
+            rows = wide[at, pl.ds(place, depth, stride=n_xy), :]
+            rows_ref[place, :, lane:lane + size] = rows[:, :size].astype(jnp.bfloat16)
+    for chunk in range(blocks // 3):
+        parts = []
+        for at in range(3):
+            block = mine_ref[0] * blocks + chunk * 3 + at
+            layer, place = block // n_xy, block % n_xy
+            rows = jnp.concatenate(
+                [wide[tile, pl.ds(place, depth, stride=n_xy), :] for tile in range(len(tiles))],
+                axis=1)[:, :wide_sub]
+            part = jnp.where(layer == 1, rows[:, sub:2 * sub], rows[:, :sub])
+            parts.append(jnp.where(layer == 2, rows[:, 2 * sub:], part))
+        col_ref[0, chunk * depth:chunk * depth + depth, :] = jnp.concatenate(
+            parts, axis=1).astype(jnp.bfloat16)
+
+
+def deal(mine, gathered, n_xy, width):
+    n_gcol, rows, wide_sub = gathered.shape
+    depth = n_gcol * rows // n_xy
+    vmem = pl.BlockSpec(memory_space=pltpu.VMEM)
+    return pl.pallas_call(
+        deal_kernel,
+        out_shape=(jax.ShapeDtypeStruct((n_xy, depth, wide_sub), jnp.bfloat16),
+                   jax.ShapeDtypeStruct((1, width // wide_sub * depth, wide_sub), jnp.bfloat16)),
+        in_specs=[pl.BlockSpec(memory_space=pltpu.SMEM), vmem],
+        out_specs=(vmem, vmem),
+        scratch_shapes=[pltpu.VMEM((-(-wide_sub // LANES), n_gcol * rows, LANES), jnp.float32)],
+        compiler_params=pltpu.CompilerParams(vmem_limit_bytes=16 * 1024 * 1024),
+        cost_estimate=pl.CostEstimate(flops=10**6, bytes_accessed=2 * 10**6, transcendentals=0),
+    )(mine, gathered)
+
+
+def tile_kernel(row_ref, col_ref, out_ref):
+    n_xy, depth, wide_sub = row_ref.shape
+    left = row_ref[...].reshape(n_xy * depth, wide_sub)
+    parts = []
+    for chunk in range(col_ref.shape[1] // depth):
+        right = col_ref[:, chunk * depth:chunk * depth + depth, :]
+        parts.append(lax.dot_general(
+            left, right.reshape(n_xy * depth, wide_sub), (((0,), (0,)), ((), ())),
+            preferred_element_type=jnp.float32))
+    out_ref[...] = jnp.concatenate(parts, axis=1).astype(jnp.bfloat16)
+
+
+def tile(row, col):
+    n_xy, depth, wide_sub = row.shape
+    width = col.shape[1] // depth * wide_sub
+    vmem = pl.BlockSpec(memory_space=pltpu.VMEM)
+    return pl.pallas_call(
+        tile_kernel,
+        out_shape=jax.ShapeDtypeStruct((wide_sub, width), jnp.bfloat16),
+        in_specs=[vmem, vmem],
+        out_specs=vmem,
+        compiler_params=pltpu.CompilerParams(vmem_limit_bytes=40 * 1024 * 1024),
+        cost_estimate=pl.CostEstimate(
+            flops=2 * n_xy * depth * wide_sub * width, bytes_accessed=5 * 10**6, transcendentals=0),
+    )(row, col)
 
 
 def local(valence, conduction, valence_energy, conduction_energy, pair_valence, pair_conduction,
@@ -178,7 +271,6 @@
     n_pair, n_grow, n_gcol = (lax.axis_size(name) for name in ("pair", "grow", "gcol"))
     n_z = n_pair // NX
     total_g = g_index.shape[0]
-    doubled = 2 * pair_valence.shape[0]
     width = total_g // n_gcol
     sub = total_g // (n_pair * n_grow)
     n_xy = NX * n_grow
@@ -186,23 +278,15 @@
     z_groups = [[z * NX + x for z in range(n_z)] for x in range(NX)]
     xy_groups = [[(z * NX + x) * n_grow + y for x in range(NX) for y in range(n_grow)]
                  for z in range(n_z)]
-    g_rows = g_index.reshape(n_z, n_xy, sub).transpose(1, 0, 2).reshape(n_xy, n_z * sub)
-    g_rows = jnp.pad(g_rows, ((0, 0), (0, CHUNK - n_z * sub)))
-    col, row = amplitudes_of(
+    mine = amplitudes_of(
         pair_valence, pair_conduction, pair_count, valence_energy, conduction_energy,
-        valence, conduction, g_index.reshape(total_g // CHUNK, CHUNK), g_rows,
-        (n_gcol, doubled, width), (n_xy, doubled, n_z * sub))
+        valence, conduction, g_index, n_xy, n_z * sub)
+    mine = lax.all_gather(mine, "gcol", axis=0, tiled=True)
+    row, col = deal(lax.axis_index("gcol").astype(jnp.int32)[None], mine, n_xy, width)
     row = lax.all_to_all(row, ("pair", "grow"), 0, 0, tiled=True, axis_index_groups=xy_groups)
-    col = lax.all_to_all(col, "gcol", 0, 0, tiled=True)
-    row = lax.all_gather(row.reshape(1, n_xy * doubled, n_z * sub), "gcol", axis=0, tiled=True)
-    col = lax.all_gather(col.reshape(1, n_gcol * doubled, width), "grow", axis=0, tiled=True)
+    col = lax.all_gather(col, "grow", axis=0, tiled=True)
     col = lax.all_gather(col, "pair", axis=0, tiled=True, axis_index_groups=x_groups)
-    row = row.reshape(n_gcol, n_xy, doubled, n_z * sub).transpose(1, 0, 2, 3)
-    row = row.reshape(-1, n_z * sub)
-    col = col.reshape(-1, width)
-    partial = lax.dot_general(row, col, (((0,), (0,)), ((), ())),
-                              preferred_element_type=jnp.float32)
-    partial = partial.astype(jnp.bfloat16).reshape(n_z, sub, width)
+    partial = tile(row, col).reshape(n_z, sub, width)
     partial = lax.all_to_all(partial, "pair", 0, 0, tiled=True, axis_index_groups=z_groups)
     summed = jnp.sum(partial.astype(jnp.float32), axis=0)
     total_slots = pair_valence.shape[0] * n_pair * n_grow * n_gcol

time: 154 us -> 158 us (1.026)
  blocking collectives: 108 us -> 66.1 us
  waiting for transfers between devices: 0.04 us -> 39.4 us
  starting transfers between devices: 0.01 us -> 7.7 us
  matrix products: 2.63 us -> 0 us
    all_to_all x2 -> x0, blocking collectives: 42.8 us -> none  [the longest x1 26.2 us: local(): col = lax.all_to_all(col, 'gcol', 0, 0, tiled=True)]
    all_gather x1, waiting for transfers between devices: 0.02 us -> 39.4 us  [local(): lax.all_gather(col, 'pair', axis=0, tiled=True, axis_index_groups=x_groups)]
    all_to_all x0 -> x1, starting transfers between devices: none -> 7.7 us  [local(): lax.all_to_all(row, ('pair', 'grow'), 0, 0, tiled=True, axis_index_groups...]
    all_gather x1 -> x2, local copies, waits for them, and re-layouts: 0.53 us -> 3.64 us  [the longest x1 3.28 us: local(): lax.all_gather(col, 'pair', axis=0, tiled=True, axis_index_groups=x_groups)]
    dot_general x1 -> x0, matrix products: 2.63 us -> none  [local(): lax.dot_general(row, col, (((0,), (0,)), ((), ())), preferred_element_typ...]
    reshape x7 -> x0, local copies, waits for them, and re-layouts: 2.32 us -> none  [the longest x2 0.93 us: local(): g_index.reshape(n_z, n_xy, sub).transpose(1, 0, 2).reshape(n_xy, n_z * sub)]
    pallas_call x1 -> x3, Pallas kernels: 14 us -> 13.1 us  [the longest x1 7.69 us: amplitudes_of(): pl.pallas_call(amplitude_kernel, out_shape=jax.ShapeDtypeStruct((1, doubl...]
    unnamed x22 -> x24, local copies, waits for them, and re-layouts: 10.3 us -> 11 us
  transfers between devices with their start and end apart: 1 -> 2, of which waited for: 0 -> 1; matrix products, arithmetic and copies ran while one was open for 1% -> 2% of each run, Pallas kernels for 0% -> 0%
where the time goes in v2:
time: 158 us; the launch traced here: 156 us
  blocking collectives  66.1 us (42%)
  waiting for transfers between devices  39.4 us (25%)
  local copies, waits for them, and re-layouts  14.9 us (9%)
  between operations  14.1 us (9%)
  Pallas kernels  13.1 us (8%)
  starting transfers between devices  7.7 us (5%)
    all_gather x1, waiting for transfers between devices, local(): lax.all_gather(col, 'pair', axis=0, tiled=True, axis_index_groups=x_groups)  39.4 us
    all_gather x1, blocking collectives, local(): mine = lax.all_gather(mine, 'gcol', axis=0, tiled=True)  29.2 us
    all_gather x1, blocking collectives, local(): col = lax.all_gather(col, 'grow', axis=0, tiled=True)  21.9 us
    all_to_all x1, blocking collectives, local(): lax.all_to_all(partial, 'pair', 0, 0, tiled=True, axis_index_groups=z_gro...  15.1 us
    unnamed x24, local copies, waits for them, and re-layouts  11 us
    all_to_all x1, starting transfers between devices, local(): lax.all_to_all(row, ('pair', 'grow'), 0, 0, tiled=True, axis_index_groups...  7.7 us
    pallas_call x1, Pallas kernels, amplitudes_of(): pl.pallas_call(amplitude_kernel, out_shape=jax.ShapeDtypeStruct((1, doubl...  7.69 us
    all_gather x1, local copies, waits for them, and re-layouts, local(): lax.all_gather(col, 'pair', axis=0, tiled=True, axis_index_groups=x_groups)  3.28 us
  transfers between devices with their start and end apart: 2, of which 1 were waited for; matrix products, arithmetic and copies ran while one was open for 2% of the time, Pallas kernels for 0%

profile of v2, /device:TPU:1, one launch (start us, length us, event | category | flops | bytes accessed | tf_op | source)
XLA Modules:
  0.0 156.3 jit_solution(7037696179741559211)
XLA Ops:
  6.5 0.0 all-gather.2.cloned.1.call-start
  7.2 0.0 copy-start
  7.2 1.9 %copy-done = bf16[48,32768]{1,0:T(8,128)(2,1)S(1)} copy-done((bf16[48,32768]{1,0:T(8,128)(2,1)S(1)}, bf16[48,32768]{1,0:T(8,128)(2,1)}, u32[]{:S(2)}) %copy-start) | copy-done | bytes 3145752
  9.1 0.0 copy-start.1
  9.1 1.2 copy-done.1
  10.3 0.0 copy-start.2
  10.3 0.8 copy-done.2
  11.1 0.0 copy-start.3
  11.1 0.7 copy-done.3
  11.7 0.0 copy-start.4
  11.7 0.7 copy-done.4
  12.4 0.0 copy-start.5
  12.4 0.7 copy-done.5
  13.0 0.0 copy-start.6
  13.0 0.7 copy-done.6
  13.7 0.0 copy-start.7
  13.7 1.0 copy-done.7
  14.7 0.0 copy-start.8
  14.7 0.9 copy-done.8
  15.6 0.0 copy-start.9
  15.6 0.9 copy-done.9
  16.5 0.0 copy-start.10
  16.5 0.9 copy-done.10
  17.4 0.0 copy-start.11
  17.4 0.8 copy-done.11
  18.2 7.7 %shard_map.127 = bf16[1,128,288]{2,1,0:T(8,128)(2,1)S(1)} custom-call(s32[2]{0:T(128)S(1)} %copy-done.3, s32[2]{0:T(128)S(1)} %copy-done.4, s32[1]{0:T(128)S(6)} %copy.18.count_hbm, f32[48]{0:T(128)S(1)} %copy-done.5, f32[16]{0:T(128)S(1)} %copy-done.6, bf16[48,32768]{1,0:T(8,128)(2,1)S(1)} %copy-done, bf16[16,32768]{1,0:T(8,128)(2,1)S(1)} %copy-done.1, ...), custom_call_target="tpu_custom_call" | custom-call | flops 4000000000 | bytes 5000000 | tf_op jit(solution)/shard_map/pallas_call | solution.py:181
  25.9 0.1 copy.14
  26.1 29.2 %all_gather.9 = bf16[8,128,288]{1,2,0:T(8,128)(2,1)S(1)} all-gather(bf16[1,128,288]{1,2,0:T(8,128)(2,1)S(1)} %copy.14), channel_id=1, replica_groups=mesh['pair'=12,'grow'=8,'gcol'=8] {'gcol'}, dimensions={0}, use_global_device_ids=true | all-gather | bytes 663552 | tf_op jit(solution)/shard_map/all_gather | solution.py:284
  55.2 0.4 copy.15.all_ref
  55.6 2.8 %shard_map.128 = (bf16[32,32,288]{2,1,0:T(8,128)(2,1)}, bf16[1,128,288]{2,1,0:T(8,128)(2,1)S(1)}) custom-call(s32[1]{0:T(128)} %bitcast.mine_ref, bf16[8,128,288]{2,1,0:T(8,128)(2,1)S(1)} %copy.15.all_ref), custom_call_target="tpu_custom_call" | custom-call | flops 1000000 | bytes 2000000 | tf_op jit(solution)/shard_map/pallas_call | solution.py:230
  58.4 0.1 copy.16
  58.5 21.9 %all_gather.10 = bf16[8,128,288]{1,2,0:T(8,128)(2,1)} all-gather(bf16[1,128,288]{1,2,0:T(8,128)(2,1)S(1)} %copy.16), channel_id=1, replica_groups=mesh['pair'=12,'grow'=8,'gcol'=8] {'grow'}, dimensions={0}, use_global_device_ids=true | all-gather | bytes 663552 | tf_op jit(solution)/shard_map/all_gather | solution.py:287
  80.4 0.0 all-gather.2.cloned.1.call-update
  80.4 7.7 %all-to-all-start = ((bf16[32,32,288]{2,1,0:T(8,128)(2,1)}), bf16[32,32,288]{2,1,0:T(8,128)(2,1)}, u32[]{:S(2)}, u32[]{:S(2)}) async-start(bf16[32,32,288]{2,1,0:T(8,128)(2,1)} %get-tuple-element.7), calls=%async_computation | async-start | bytes 1572864 | tf_op jit(solution)/shard_map/all_to_all | solution.py:286
  88.1 39.4 %all-gather.2.cloned.1.call-done = bf16[32,128,288]{1,2,0:T(8,128)(2,1)} async-done(((bf16[8,128,288]{1,2,0:T(8,128)(2,1)}), bf16[32,128,288]{1,2,0:T(8,128)(2,1)}) %all-gather.2.cloned.1.call-update) | async-done | bytes 2359312 | tf_op jit(solution)/shard_map/all_gather | solution.py:288
  127.5 3.3 %copy.17.col_ref = bf16[32,128,288]{2,1,0:T(8,128)(2,1)S(1)} copy(bf16[32,128,288]{1,2,0:T(8,128)(2,1)} %all-gather.2.cloned.1.call-done) | data formatting | bytes 4718592 | tf_op jit(solution)/shard_map/all_gather | solution.py:288
  130.8 0.0 all-to-all-done.row_ref
  130.8 2.6 %shard_map.129 = bf16[288,1152]{1,0:T(8,128)(2,1)S(1)} custom-call(bf16[32,32,288]{2,1,0:T(8,128)(2,1)} %all-to-all-done.row_ref, bf16[32,128,288]{2,1,0:T(8,128)(2,1)S(1)} %copy.17.col_ref), custom_call_target="tpu_custom_call" | custom-call | flops 679477248 | bytes 5000000 | tf_op jit(solution)/shard_map/pallas_call | solution.py:258
  133.4 15.1 %all_to_all.10 = bf16[3,96,1152]{2,1,0:T(8,128)(2,1)S(1)} all-to-all(bf16[3,96,1152]{2,1,0:T(8,128)(2,1)S(1)} %bitcast.3), channel_id=1, replica_groups={{0,256,512},{64,320,576},{128,384,640},{192,448,704},{1,257,513},{65,32..., dimensions={0} | all-to-all | bytes 1327104 | tf_op jit(solution)/shard_map/all_to_all | solution.py:290
  148.5 0.1 convert_reduce_fusion
  148.6 0.8 negate_multiply_fusion
Async XLA Ops:
  6.5 121.0 %all-gather.2.cloned.1.call-start = ((), (), s32[]{:S(2)}) async-start(), calls=%async_computation.2 | async-start | bytes 2949120 | tf_op jit(solution)/shard_map/all_gather | solution.py:288
  7.2 1.9 %copy-start = (bf16[48,32768]{1,0:T(8,128)(2,1)S(1)}, bf16[48,32768]{1,0:T(8,128)(2,1)}, u32[]{:S(2)}) copy-start(bf16[48,32768]{1,0:T(8,128)(2,1)} %valence_hbm.1) | copy-start | bytes 9437188
  9.1 1.2 copy-start.1
  10.3 0.8 copy-start.2
  11.1 0.7 copy-start.3
  11.7 0.7 copy-start.4
  12.4 0.7 copy-start.5
  13.0 0.7 copy-start.6
  13.7 1.0 copy-start.7
  14.7 0.9 copy-start.8
  15.6 0.9 copy-start.9
  16.5 0.9 copy-start.10
  17.4 0.8 copy-start.11
  80.4 50.4 %all-to-all-start = ((bf16[32,32,288]{2,1,0:T(8,128)(2,1)}), bf16[32,32,288]{2,1,0:T(8,128)(2,1)}, u32[]{:S(2)}, u32[]{:S(2)}) async-start(bf16[32,32,288]{2,1,0:T(8,128)(2,1)} %get-tuple-element.7), calls=%async_computation | async-start | bytes 1572864 | tf_op jit(solution)/shard_map/all_to_all | solution.py:286
Sparse Core Ops, SparseCore 0:
  80.5 46.9 all-gather.1

commit v3 on v2

--- a/solution.py
+++ b/solution.py
@@ -56,6 +56,10 @@
     return high, low
 
 
+def position(name):
+    return lax.axis_index(name)
+
+
 def dot(left, right):
     return jnp.dot(left, right, preferred_element_type=jnp.float32)
 
@@ -192,15 +196,15 @@
             pltpu.VMEM((-(-wide_sub // LANES), doubled * n_xy, LANES), jnp.float32),
             pltpu.SemaphoreType.DMA((13,)),
         ],
-        compiler_params=pltpu.CompilerParams(vmem_limit_bytes=40 * 1024 * 1024),
+        compiler_params=pltpu.CompilerParams(vmem_limit_bytes=60 * 1024 * 1024),
         cost_estimate=pl.CostEstimate(flops=4 * 10**9, bytes_accessed=5 * 10**6, transcendentals=0),
     )(pv, pc, count, ve, ce, *arrays)
 
 
-def deal_kernel(mine_ref, all_ref, rows_ref, col_ref, wide):
+def deal_kernel(all_ref, rows_ref, col_ref, wide):
     n_xy, depth, wide_sub = rows_ref.shape
     sub = wide_sub // 3
-    blocks = col_ref.shape[1] // depth * 3
+    blocks = col_ref.shape[2] // sub
     tiles = lane_tiles(wide_sub)
     for at, (lane, size) in enumerate(tiles):
         block = all_ref[:, :, lane:lane + size].astype(jnp.float32)
@@ -209,61 +213,74 @@
         for at, (lane, size) in enumerate(tiles):
             rows = wide[at, pl.ds(place, depth, stride=n_xy), :]
             rows_ref[place, :, lane:lane + size] = rows[:, :size].astype(jnp.bfloat16)
-    for chunk in range(blocks // 3):
-        parts = []
-        for at in range(3):
-            block = mine_ref[0] * blocks + chunk * 3 + at
-            layer, place = block // n_xy, block % n_xy
-            rows = jnp.concatenate(
-                [wide[tile, pl.ds(place, depth, stride=n_xy), :] for tile in range(len(tiles))],
-                axis=1)[:, :wide_sub]
-            part = jnp.where(layer == 1, rows[:, sub:2 * sub], rows[:, :sub])
-            parts.append(jnp.where(layer == 2, rows[:, 2 * sub:], part))
-        col_ref[0, chunk * depth:chunk * depth + depth, :] = jnp.concatenate(
-            parts, axis=1).astype(jnp.bfloat16)
-
-
-def deal(mine, gathered, n_xy, width):
+    mine = position("gcol") * blocks
+    parts = []
+    for at in range(blocks):
+        layer, place = (mine + at) // n_xy, (mine + at) % n_xy
+        rows = jnp.concatenate(
+            [wide[tile, pl.ds(place, depth, stride=n_xy), :] for tile in range(len(tiles))],
+            axis=1)[:, :wide_sub]
+        part = jnp.where(layer == 1, rows[:, sub:2 * sub], rows[:, :sub])
+        parts.append(jnp.where(layer == 2, rows[:, 2 * sub:], part))
+    whole = jnp.concatenate(parts, axis=1).astype(jnp.bfloat16)
+    for target in range(col_ref.shape[0]):
+        col_ref[target] = whole
+
+
+def deal(gathered, n_xy, width, n_grow):
     n_gcol, rows, wide_sub = gathered.shape
     depth = n_gcol * rows // n_xy
     vmem = pl.BlockSpec(memory_space=pltpu.VMEM)
     return pl.pallas_call(
         deal_kernel,
         out_shape=(jax.ShapeDtypeStruct((n_xy, depth, wide_sub), jnp.bfloat16),
-                   jax.ShapeDtypeStruct((1, width // wide_sub * depth, wide_sub), jnp.bfloat16)),
-        in_specs=[pl.BlockSpec(memory_space=pltpu.SMEM), vmem],
+                   jax.ShapeDtypeStruct((n_grow, depth, width), jnp.bfloat16)),
+        in_specs=[vmem],
         out_specs=(vmem, vmem),
         scratch_shapes=[pltpu.VMEM((-(-wide_sub // LANES), n_gcol * rows, LANES), jnp.float32)],
-        compiler_params=pltpu.CompilerParams(vmem_limit_bytes=16 * 1024 * 1024),
+        compiler_params=pltpu.CompilerParams(vmem_limit_bytes=24 * 1024 * 1024),
         cost_estimate=pl.CostEstimate(flops=10**6, bytes_accessed=2 * 10**6, transcendentals=0),
-    )(mine, gathered)
-
-
-def tile_kernel(row_ref, col_ref, out_ref):
-    n_xy, depth, wide_sub = row_ref.shape
-    left = row_ref[...].reshape(n_xy * depth, wide_sub)
-    parts = []
-    for chunk in range(col_ref.shape[1] // depth):
-        right = col_ref[:, chunk * depth:chunk * depth + depth, :]
-        parts.append(lax.dot_general(
-            left, right.reshape(n_xy * depth, wide_sub), (((0,), (0,)), ((), ())),
-            preferred_element_type=jnp.float32))
-    out_ref[...] = jnp.concatenate(parts, axis=1).astype(jnp.bfloat16)
-
-
-def tile(row, col):
+    )(gathered)
+
+
+def tile_kernel(row_ref, *refs):
+    col_refs, own_ref, sent_refs, total = refs[:NX], refs[NX], refs[NX + 1:-1], refs[-1]
+    n_grow, depth, width = col_refs[0].shape
+    wide_sub = row_ref.shape[2]
+    mine = position("pair") % NX
+    value = None
+    for step, col_ref in enumerate(col_refs):
+        source = (mine + (NX - step)) % NX
+        left = row_ref[pl.ds(source * n_grow, n_grow)].reshape(n_grow * depth, wide_sub)
+        term = lax.dot_general(
+            left, col_ref[...].reshape(n_grow * depth, width), (((0,), (0,)), ((), ())),
+            preferred_element_type=jnp.float32)
+        value = term if value is None else value + term
+    total[...] = value
+    sub = own_ref.shape[0]
+    layer = position("pair") // NX
+    own_ref[...] = total[pl.ds(pl.multiple_of(layer * sub, 8), sub), :]
+    for at, sent_ref in enumerate(sent_refs):
+        target = (layer + at + 1) % (len(sent_refs) + 1)
+        sent_ref[...] = total[pl.ds(pl.multiple_of(target * sub, 8), sub), :].astype(jnp.bfloat16)
+
+
+def tile(row, cols, n_z):
     n_xy, depth, wide_sub = row.shape
-    width = col.shape[1] // depth * wide_sub
+    width = cols[0].shape[2]
+    sub = wide_sub // n_z
     vmem = pl.BlockSpec(memory_space=pltpu.VMEM)
     return pl.pallas_call(
         tile_kernel,
-        out_shape=jax.ShapeDtypeStruct((wide_sub, width), jnp.bfloat16),
-        in_specs=[vmem, vmem],
-        out_specs=vmem,
+        out_shape=[jax.ShapeDtypeStruct((sub, width), jnp.float32)]
+        + [jax.ShapeDtypeStruct((sub, width), jnp.bfloat16)] * (n_z - 1),
+        in_specs=[vmem] * (1 + NX),
+        out_specs=[vmem] * n_z,
+        scratch_shapes=[pltpu.VMEM((wide_sub, width), jnp.float32)],
         compiler_params=pltpu.CompilerParams(vmem_limit_bytes=40 * 1024 * 1024),
         cost_estimate=pl.CostEstimate(
             flops=2 * n_xy * depth * wide_sub * width, bytes_accessed=5 * 10**6, transcendentals=0),
-    )(row, col)
+    )(row, *cols)
 
 
 def local(valence, conduction, valence_energy, conduction_energy, pair_valence, pair_conduction,
@@ -274,23 +291,25 @@
     width = total_g // n_gcol
     sub = total_g // (n_pair * n_grow)
     n_xy = NX * n_grow
-    x_groups = [[z * NX + x for x in range(NX)] for z in range(n_z)]
-    z_groups = [[z * NX + x for z in range(n_z)] for x in range(NX)]
     xy_groups = [[(z * NX + x) * n_grow + y for x in range(NX) for y in range(n_grow)]
                  for z in range(n_z)]
     mine = amplitudes_of(
         pair_valence, pair_conduction, pair_count, valence_energy, conduction_energy,
         valence, conduction, g_index, n_xy, n_z * sub)
     mine = lax.all_gather(mine, "gcol", axis=0, tiled=True)
-    row, col = deal(lax.axis_index("gcol").astype(jnp.int32)[None], mine, n_xy, width)
+    row, col = deal(mine, n_xy, width, n_grow)
     row = lax.all_to_all(row, ("pair", "grow"), 0, 0, tiled=True, axis_index_groups=xy_groups)
-    col = lax.all_gather(col, "grow", axis=0, tiled=True)
-    col = lax.all_gather(col, "pair", axis=0, tiled=True, axis_index_groups=x_groups)
-    partial = tile(row, col).reshape(n_z, sub, width)
-    partial = lax.all_to_all(partial, "pair", 0, 0, tiled=True, axis_index_groups=z_groups)
-    summed = jnp.sum(partial.astype(jnp.float32), axis=0)
+    col = lax.all_to_all(col, "grow", 0, 0, tiled=True)
+    cols = [col] + [
+        lax.ppermute(col, "pair", [(z * NX + x, z * NX + (x + step) % NX)
+                                   for z in range(n_z) for x in range(NX)])
+        for step in range(1, NX)]
+    own, *sent = tile(row, cols, n_z)
+    for step, block in enumerate(sent, 1):
+        own = own + lax.ppermute(block, "pair", [(z * NX + x, (z + step) % n_z * NX + x)
+                                                 for z in range(n_z) for x in range(NX)])
     total_slots = pair_valence.shape[0] * n_pair * n_grow * n_gcol
-    return -summed / jnp.sqrt(jnp.float32(total_slots))
+    return -own / jnp.sqrt(jnp.float32(total_slots))
 
 
 def solution(mesh):

time: 158 us -> 130 us (0.82); the launches traced: 156 us -> 130 us
  local copies, waits for them, and re-layouts: 14.9 us -> 1.36 us
  blocking collectives: 66.1 us -> 52.7 us
  between operations: 14.1 us -> 0.73 us
  starting transfers between devices: 7.7 us -> 20.3 us
    all_gather x1 -> x0, waiting for transfers between devices: 39.4 us -> none  [local(): lax.all_gather(col, 'pair', axis=0, tiled=True, axis_index_groups=x_groups)]
    ppermute x0 -> x5, waiting for transfers between devices: none -> 30.2 us  [the longest x3 21.5 us: local(): lax.ppermute(col, 'pair', [(z * NX + x, z * NX + (x + step) % NX) for z i...]
    all_gather x1 -> x0, blocking collectives: 21.9 us -> none  [local(): col = lax.all_gather(col, 'grow', axis=0, tiled=True)]
    ppermute x0 -> x5, starting transfers between devices: none -> 15.8 us  [the longest x3 9.33 us: local(): lax.ppermute(col, 'pair', [(z * NX + x, z * NX + (x + step) % NX) for z i...]
    unnamed x24 -> x0, local copies, waits for them, and re-layouts: 11 us -> none
    all_to_all x1, waiting for transfers between devices: 0.01 us -> 10.5 us  [local(): lax.all_to_all(row, ('pair', 'grow'), 0, 0, tiled=True, axis_index_groups...]
    all_to_all x1, blocking collectives: 15.1 us -> 23.7 us  [local(): col = lax.all_to_all(col, 'grow', 0, 0, tiled=True)]
    all_gather x1 -> x0, local copies, waits for them, and re-layouts: 3.28 us -> none  [local(): lax.all_gather(col, 'pair', axis=0, tiled=True, axis_index_groups=x_groups)]
  transfers between devices with their start and end apart: 2 -> 6, of which waited for: 1 -> 6; matrix products, arithmetic and copies ran while one was open for 2% -> 0% of each run, Pallas kernels for 0% -> 0%
where the time goes in v3:
time: 130 us
  blocking collectives  52.7 us (41%)
  waiting for transfers between devices  40.7 us (31%)
  starting transfers between devices  20.3 us (16%)
  Pallas kernels  13.2 us (10%)
  local copies, waits for them, and re-layouts  1.36 us (1%)
    all_gather x1, blocking collectives, local(): mine = lax.all_gather(mine, 'gcol', axis=0, tiled=True)  29 us
    all_to_all x1, blocking collectives, local(): col = lax.all_to_all(col, 'grow', 0, 0, tiled=True)  23.7 us
    ppermute x3, waiting for transfers between devices, local(): lax.ppermute(col, 'pair', [(z * NX + x, z * NX + (x + step) % NX) for z i...  21.5 us
    all_to_all x1, waiting for transfers between devices, local(): lax.all_to_all(row, ('pair', 'grow'), 0, 0, tiled=True, axis_index_groups...  10.5 us
    pallas_call x1, Pallas kernels, amplitudes_of(): pl.pallas_call(amplitude_kernel, out_shape=jax.ShapeDtypeStruct((1, doubl...  9.4 us
    ppermute x3, starting transfers between devices, local(): lax.ppermute(col, 'pair', [(z * NX + x, z * NX + (x + step) % NX) for z i...  9.33 us
    ppermute x2, waiting for transfers between devices, local(): lax.ppermute(block, 'pair', [(z * NX + x, (z + step) % n_z * NX + x) for...  8.68 us
    ppermute x2, starting transfers between devices, local(): lax.ppermute(block, 'pair', [(z * NX + x, (z + step) % n_z * NX + x) for...  6.52 us
  transfers between devices with their start and end apart: 6, of which 6 were waited for; matrix products, arithmetic and copies ran while one was open for 0% of the time, Pallas kernels for 0%

profile of v3, /device:TPU:1, one launch (start us, length us, event | category | flops | bytes accessed | tf_op | source)
XLA Modules:
  0.0 129.9 jit_solution(2487555604833876824)
XLA Ops:
  0.7 9.4 %shard_map.127 = bf16[1,128,288]{2,1,0:T(8,128)(2,1)} custom-call(s32[2]{0:T(128)} %pv_hbm.1, s32[2]{0:T(128)} %pc_hbm.1, s32[1]{0:T(128)S(6)} %copy.16.count_hbm, f32[48]{0:T(128)} %ve_hbm.1, f32[16]{0:T(128)} %ce_hbm.1, bf16[48,32768]{1,0:T(8,128)(2,1)} %valence_hbm.1, bf16[16,32768]{1,0:T(8,128)(2,1)} %conduction_hbm.1, ...), custom_call_target="tpu_custom_call" | custom-call | flops 4000000000 | bytes 5000000 | tf_op jit(solution)/shard_map/pallas_call | solution.py:185
  10.1 1.0 copy.14
  11.1 29.0 %all_gather.3 = bf16[8,128,288]{1,2,0:T(8,128)(2,1)S(1)} all-gather(bf16[1,128,288]{1,2,0:T(8,128)(2,1)S(1)} %copy.14), channel_id=1, replica_groups=mesh['pair'=12,'grow'=8,'gcol'=8] {'gcol'}, dimensions={0}, use_global_device_ids=true | all-gather | bytes 663552 | tf_op jit(solution)/shard_map/all_gather | solution.py:299
  40.1 0.4 copy.15.all_ref
  40.5 2.8 %shard_map.128 = (bf16[32,32,288]{2,1,0:T(8,128)(2,1)}, bf16[8,32,1152]{2,1,0:T(8,128)(2,1)S(1)}) custom-call(bf16[8,128,288]{2,1,0:T(8,128)(2,1)S(1)} %copy.15.all_ref), custom_call_target="tpu_custom_call" | custom-call | flops 1000000 | bytes 2000000 | tf_op jit(solution)/shard_map/pallas_call | solution.py:234
  43.2 23.7 %all_to_all.10.refs_0_ = bf16[8,32,1152]{2,1,0:T(8,128)(2,1)S(1)} all-to-all(bf16[8,32,1152]{2,1,0:T(8,128)(2,1)S(1)} %get-tuple-element.11), channel_id=1, replica_groups=mesh['pair'=12,'grow'=8,'gcol'=8] {'grow'}, dimensions={0} | all-to-all | bytes 1179648 | tf_op jit(solution)/shard_map/all_to_all | solution.py:302
  66.9 4.5 %all-to-all-start = ((bf16[32,32,288]{2,1,0:T(8,128)(2,1)}), bf16[32,32,288]{2,1,0:T(8,128)(2,1)S(1)}, u32[]{:S(2)}, u32[]{:S(2)}) async-start(bf16[32,32,288]{2,1,0:T(8,128)(2,1)} %get-tuple-element.10), calls=%async_computation | async-start | bytes 1572864 | tf_op jit(solution)/shard_map/all_to_all | solution.py:301
  71.4 4.4 %collective-permute-start.2 = (bf16[8,32,1152]{2,1,0:T(8,128)(2,1)S(1)}, bf16[8,32,1152]{2,1,0:T(8,128)(2,1)S(1)}, u32[]{:S(2)}, u32[]{:S(2)}) collective-permute-start(bf16[8,32,1152]{2,1,0:T(8,128)(2,1)S(1)} %all_to_all.10.refs_0_), channel_id=1, source_target_pairs={{0,192},{64,0},{128,64},{192,128},{256,448},{320,256},{384,320},{4... | collective-permute-start | bytes 1769480 | tf_op jit(solution)/shard_map/ppermute | solution.py:304
  75.8 2.4 %collective-permute-start.1 = (bf16[8,32,1152]{2,1,0:T(8,128)(2,1)S(1)}, bf16[8,32,1152]{2,1,0:T(8,128)(2,1)S(1)}, u32[]{:S(2)}, u32[]{:S(2)}) collective-permute-start(bf16[8,32,1152]{2,1,0:T(8,128)(2,1)S(1)} %all_to_all.10.refs_0_), channel_id=1, source_target_pairs={{0,128},{64,192},{128,0},{192,64},{256,384},{320,448},{384,256},{4... | collective-permute-start | bytes 1769480 | tf_op jit(solution)/shard_map/ppermute | solution.py:304
  78.3 2.5 %collective-permute-start = (bf16[8,32,1152]{2,1,0:T(8,128)(2,1)S(1)}, bf16[8,32,1152]{2,1,0:T(8,128)(2,1)S(1)}, u32[]{:S(2)}, u32[]{:S(2)}) collective-permute-start(bf16[8,32,1152]{2,1,0:T(8,128)(2,1)S(1)} %all_to_all.10.refs_0_), channel_id=1, source_target_pairs={{0,64},{64,128},{128,192},{192,0},{256,320},{320,384},{384,448},{4... | collective-permute-start | bytes 1769480 | tf_op jit(solution)/shard_map/ppermute | solution.py:304
  80.8 10.5 %all-to-all-done.row_ref = bf16[32,32,288]{2,1,0:T(8,128)(2,1)S(1)} async-done(((bf16[32,32,288]{2,1,0:T(8,128)(2,1)}), bf16[32,32,288]{2,1,0:T(8,128)(2,1)S(1)}, u32[]{:S(2)}, u32[]{:S(2)}) %all-to-all-start) | async-done | bytes 589856 | tf_op jit(solution)/shard_map/all_to_all | solution.py:301
  91.3 4.0 %collective-permute-done.2.refs_3_ = bf16[8,32,1152]{2,1,0:T(8,128)(2,1)S(1)} collective-permute-done((bf16[8,32,1152]{2,1,0:T(8,128)(2,1)S(1)}, bf16[8,32,1152]{2,1,0:T(8,128)(2,1)S(1)}, u32[]{:S(2)}, u32[]{:S(2)}) %collective-permute-start.2) | collective-permute-done | bytes 589856 | tf_op jit(solution)/shard_map/ppermute | solution.py:304
  95.2 4.1 %collective-permute-done.1.refs_2_ = bf16[8,32,1152]{2,1,0:T(8,128)(2,1)S(1)} collective-permute-done((bf16[8,32,1152]{2,1,0:T(8,128)(2,1)S(1)}, bf16[8,32,1152]{2,1,0:T(8,128)(2,1)S(1)}, u32[]{:S(2)}, u32[]{:S(2)}) %collective-permute-start.1) | collective-permute-done | bytes 589856 | tf_op jit(solution)/shard_map/ppermute | solution.py:304
  99.3 13.5 %collective-permute-done.refs_1_ = bf16[8,32,1152]{2,1,0:T(8,128)(2,1)S(1)} collective-permute-done((bf16[8,32,1152]{2,1,0:T(8,128)(2,1)S(1)}, bf16[8,32,1152]{2,1,0:T(8,128)(2,1)S(1)}, u32[]{:S(2)}, u32[]{:S(2)}) %collective-permute-start) | collective-permute-done | bytes 589856 | tf_op jit(solution)/shard_map/ppermute | solution.py:304
  112.8 1.1 shard_map.129
  113.9 3.6 %collective-permute-start.3 = (bf16[96,1152]{1,0:T(8,128)(2,1)S(1)}, bf16[96,1152]{1,0:T(8,128)(2,1)S(1)}, u32[]{:S(2)}, u32[]{:S(2)}) collective-permute-start(bf16[96,1152]{1,0:T(8,128)(2,1)S(1)} %get-tuple-element.13), channel_id=1, source_target_pairs={{0,256},{64,320},{128,384},{192,448},{256,512},{320,576},{384,640}... | collective-permute-start | bytes 663560 | tf_op jit(solution)/shard_map/ppermute | solution.py:309
  117.4 2.9 %collective-permute-start.4 = (bf16[96,1152]{1,0:T(8,128)(2,1)S(1)}, bf16[96,1152]{1,0:T(8,128)(2,1)S(1)}, u32[]{:S(2)}, u32[]{:S(2)}) collective-permute-start(bf16[96,1152]{1,0:T(8,128)(2,1)S(1)} %get-tuple-element.14), channel_id=1, source_target_pairs={{0,512},{64,576},{128,640},{192,704},{256,0},{320,64},{384,128},{4... | collective-permute-start | bytes 663560 | tf_op jit(solution)/shard_map/ppermute | solution.py:309
  120.4 3.4 %collective-permute-done.3 = bf16[96,1152]{1,0:T(8,128)(2,1)S(1)} collective-permute-done((bf16[96,1152]{1,0:T(8,128)(2,1)S(1)}, bf16[96,1152]{1,0:T(8,128)(2,1)S(1)}, u32[]{:S(2)}, u32[]{:S(2)}) %collective-permute-start.3) | collective-permute-done | bytes 221216 | tf_op jit(solution)/shard_map/ppermute | solution.py:309
  123.8 5.2 %collective-permute-done.4 = bf16[96,1152]{1,0:T(8,128)(2,1)S(1)} collective-permute-done((bf16[96,1152]{1,0:T(8,128)(2,1)S(1)}, bf16[96,1152]{1,0:T(8,128)(2,1)S(1)}, u32[]{:S(2)}, u32[]{:S(2)}) %collective-permute-start.4) | collective-permute-done | bytes 221216 | tf_op jit(solution)/shard_map/ppermute | solution.py:309
  129.1 0.8 negate_multiply_fusion
Async XLA Ops:
  66.9 24.3 %all-to-all-start = ((bf16[32,32,288]{2,1,0:T(8,128)(2,1)}), bf16[32,32,288]{2,1,0:T(8,128)(2,1)S(1)}, u32[]{:S(2)}, u32[]{:S(2)}) async-start(bf16[32,32,288]{2,1,0:T(8,128)(2,1)} %get-tuple-element.10), calls=%async_computation | async-start | bytes 1572864 | tf_op jit(solution)/shard_map/all_to_all | solution.py:301
  71.4 23.8 %collective-permute-start.2 = (bf16[8,32,1152]{2,1,0:T(8,128)(2,1)S(1)}, bf16[8,32,1152]{2,1,0:T(8,128)(2,1)S(1)}, u32[]{:S(2)}, u32[]{:S(2)}) collective-permute-start(bf16[8,32,1152]{2,1,0:T(8,128)(2,1)S(1)} %all_to_all.10.refs_0_), channel_id=1, source_target_pairs={{0,192},{64,0},{128,64},{192,128},{256,448},{320,256},{384,320},{4... | collective-permute-start | bytes 1769480 | tf_op jit(solution)/shard_map/ppermute | solution.py:304
  75.8 23.5 %collective-permute-start.1 = (bf16[8,32,1152]{2,1,0:T(8,128)(2,1)S(1)}, bf16[8,32,1152]{2,1,0:T(8,128)(2,1)S(1)}, u32[]{:S(2)}, u32[]{:S(2)}) collective-permute-start(bf16[8,32,1152]{2,1,0:T(8,128)(2,1)S(1)} %all_to_all.10.refs_0_), channel_id=1, source_target_pairs={{0,128},{64,192},{128,0},{192,64},{256,384},{320,448},{384,256},{4... | collective-permute-start | bytes 1769480 | tf_op jit(solution)/shard_map/ppermute | solution.py:304
  78.3 34.5 %collective-permute-start = (bf16[8,32,1152]{2,1,0:T(8,128)(2,1)S(1)}, bf16[8,32,1152]{2,1,0:T(8,128)(2,1)S(1)}, u32[]{:S(2)}, u32[]{:S(2)}) collective-permute-start(bf16[8,32,1152]{2,1,0:T(8,128)(2,1)S(1)} %all_to_all.10.refs_0_), channel_id=1, source_target_pairs={{0,64},{64,128},{128,192},{192,0},{256,320},{320,384},{384,448},{4... | collective-permute-start | bytes 1769480 | tf_op jit(solution)/shard_map/ppermute | solution.py:304
  113.9 10.0 %collective-permute-start.3 = (bf16[96,1152]{1,0:T(8,128)(2,1)S(1)}, bf16[96,1152]{1,0:T(8,128)(2,1)S(1)}, u32[]{:S(2)}, u32[]{:S(2)}) collective-permute-start(bf16[96,1152]{1,0:T(8,128)(2,1)S(1)} %get-tuple-element.13), channel_id=1, source_target_pairs={{0,256},{64,320},{128,384},{192,448},{256,512},{320,576},{384,640}... | collective-permute-start | bytes 663560 | tf_op jit(solution)/shard_map/ppermute | solution.py:309
  117.4 11.6 %collective-permute-start.4 = (bf16[96,1152]{1,0:T(8,128)(2,1)S(1)}, bf16[96,1152]{1,0:T(8,128)(2,1)S(1)}, u32[]{:S(2)}, u32[]{:S(2)}) collective-permute-start(bf16[96,1152]{1,0:T(8,128)(2,1)S(1)} %get-tuple-element.14), channel_id=1, source_target_pairs={{0,512},{64,576},{128,640},{192,704},{256,0},{320,64},{384,128},{4... | collective-permute-start | bytes 663560 | tf_op jit(solution)/shard_map/ppermute | solution.py:309

commit v4 on v3

--- a/solution.py
+++ b/solution.py
@@ -79,7 +79,9 @@
     )
     lane = (second >> 3) * 16 + third
     width = cells.shape[-1]
-    hot = (lax.broadcasted_iota(jnp.int32, (ROWS, width), 0) == row).astype(jnp.bfloat16)
+    row_id = lax.broadcasted_iota(jnp.int32, (ROWS, width), 0).astype(jnp.bfloat16)
+    one, zero = jnp.ones((), jnp.bfloat16), jnp.zeros((), jnp.bfloat16)
+    hot = jnp.where(row_id == row.astype(jnp.bfloat16), one, zero)
     picked = dot(amplitudes, hot)
     mask = lax.broadcasted_iota(jnp.int32, (64, width), 0) == lane
     parts = []
@@ -96,12 +98,13 @@
 
 def amplitude_kernel(pv_hbm, pc_hbm, count_hbm, ve_hbm, ce_hbm, valence_hbm, conduction_hbm,
                      lane_hbm, row_hbm, same_hbm, swap_hbm, last_hbm, g_hbm,
-                     out_ref, pv_ref, pc_ref, count_ref, ve_ref, ce_ref, valence_ref,
+                     col_ref, rows_ref, pv_ref, pc_ref, count_ref, ve_ref, ce_ref, valence_ref,
                      conduction_ref, lane_ref, row_ref, same_ref, swap_ref, last_ref, g_ref,
-                     wide, amp, flat, ordered, sems):
+                     wide, amp, flat, sems):
     slots = 2
-    sub = out_ref.shape[2] // 3
-    n_xy = out_ref.shape[1] // (2 * slots)
+    n_xy, doubled, wide_sub = rows_ref.shape
+    sub = wide_sub // 3
+    width = col_ref.shape[2]
     sources = (pv_hbm, pc_hbm, conduction_hbm, valence_hbm, lane_hbm, row_hbm, same_hbm,
                swap_hbm, last_hbm, g_hbm, count_hbm, ve_hbm, ce_hbm)
     targets = (pv_ref, pc_ref, conduction_ref, valence_ref, lane_ref, row_ref, same_ref,
@@ -165,18 +168,13 @@
     lax.fori_loop(0, flat.shape[1] // CHUNK, pick, 0, unroll=3)
     for place in range(n_xy):
         starts = [(z * n_xy + place) * sub for z in range(3)]
-        block = jnp.concatenate([flat[0:4, at:at + sub] for at in starts], axis=1)
-        for at, (lane, size) in enumerate(lane_tiles(3 * sub)):
-            part = block[:, lane:lane + size]
-            if size < LANES:
-                part = jnp.concatenate(
-                    [part, jnp.zeros((4, LANES - size), jnp.float32)], axis=1)
-            ordered[at, pl.ds(place, 4, stride=n_xy), :] = part
-    for at, (lane, size) in enumerate(lane_tiles(3 * sub)):
-        out_ref[0, :, lane:lane + size] = ordered[at, :, :size].astype(jnp.bfloat16)
-
-
-def amplitudes_of(pv, pc, count, ve, ce, valence, conduction, g_index, n_xy, wide_sub):
+        block = jnp.concatenate([flat[0:doubled, at:at + sub] for at in starts], axis=1)
+        rows_ref[place] = block.astype(jnp.bfloat16)
+    for target in range(col_ref.shape[0]):
+        col_ref[target] = flat[0:doubled, target * width:(target + 1) * width].astype(jnp.bfloat16)
+
+
+def amplitudes_of(pv, pc, count, ve, ce, valence, conduction, g_index, n_xy, wide_sub, n_gcol):
     hbm = pl.BlockSpec(memory_space=pltpu.HBM)
     consts = [jnp.asarray(table) for table in tables()]
     g_rows = g_index.reshape(-1, LANES)
@@ -184,16 +182,17 @@
     doubled = 2 * pv.shape[0]
     return pl.pallas_call(
         amplitude_kernel,
-        out_shape=jax.ShapeDtypeStruct((1, doubled * n_xy, wide_sub), jnp.bfloat16),
+        out_shape=(
+            jax.ShapeDtypeStruct((n_gcol, doubled, g_index.shape[0] // n_gcol), jnp.bfloat16),
+            jax.ShapeDtypeStruct((n_xy, doubled, wide_sub), jnp.bfloat16)),
         in_specs=[hbm] * 13,
-        out_specs=pl.BlockSpec(memory_space=pltpu.VMEM),
+        out_specs=(pl.BlockSpec(memory_space=pltpu.VMEM),) * 2,
         scratch_shapes=[pltpu.SMEM(a.shape, a.dtype) for a in (pv, pc, count, ve, ce)]
         + [pltpu.VMEM(a.shape, a.dtype) for a in arrays]
         + [
             pltpu.VMEM((4, 8 * ROWS, LANES), jnp.float32),
             pltpu.VMEM((ROWS, ROWS), jnp.bfloat16),
             pltpu.VMEM((8, g_index.shape[0]), jnp.float32),
-            pltpu.VMEM((-(-wide_sub // LANES), doubled * n_xy, LANES), jnp.float32),
             pltpu.SemaphoreType.DMA((13,)),
         ],
         compiler_params=pltpu.CompilerParams(vmem_limit_bytes=60 * 1024 * 1024),
@@ -201,57 +200,52 @@
     )(pv, pc, count, ve, ce, *arrays)
 
 
-def deal_kernel(all_ref, rows_ref, col_ref, wide):
-    n_xy, depth, wide_sub = rows_ref.shape
-    sub = wide_sub // 3
-    blocks = col_ref.shape[2] // sub
+def spread_kernel(in_ref, first_ref, out_ref, wide):
+    del first_ref
+    n_gcol, doubled, width = in_ref.shape
+    for at in range(n_gcol):
+        block = in_ref[at].astype(jnp.float32)
+        for lane in range(width // LANES):
+            wide[lane, pl.ds(at, doubled, stride=n_gcol), :] = block[
+                :, lane * LANES:(lane + 1) * LANES]
+    for lane in range(width // LANES):
+        block = wide[lane].astype(jnp.bfloat16)
+        for target in range(out_ref.shape[0]):
+            out_ref[target, :, lane * LANES:(lane + 1) * LANES] = block
+
+
+def spread(col, first, n_grow):
+    n_gcol, doubled, width = col.shape
+    vmem = pl.BlockSpec(memory_space=pltpu.VMEM)
+    return pl.pallas_call(
+        spread_kernel,
+        out_shape=jax.ShapeDtypeStruct((n_grow, n_gcol * doubled, width), jnp.bfloat16),
+        in_specs=[vmem, pl.BlockSpec(memory_space=pl.ANY)],
+        out_specs=vmem,
+        scratch_shapes=[pltpu.VMEM((width // LANES, n_gcol * doubled, LANES), jnp.float32)],
+        compiler_params=pltpu.CompilerParams(vmem_limit_bytes=16 * 1024 * 1024),
+        cost_estimate=pl.CostEstimate(flops=10**6, bytes_accessed=2 * 10**6, transcendentals=0),
+    )(col, first)
+
+
+def tile_kernel(row_ref, *refs):
+    col_refs, own_ref, sent_refs = refs[:NX], refs[NX], refs[NX + 1:-2]
+    wide, total = refs[-2:]
+    n_grow, depth, width = col_refs[0].shape
+    n_gcol, stride, wide_sub = row_ref.shape
+    doubled = depth // n_gcol
     tiles = lane_tiles(wide_sub)
     for at, (lane, size) in enumerate(tiles):
-        block = all_ref[:, :, lane:lane + size].astype(jnp.float32)
-        wide[at, :, :size] = block.reshape(n_xy * depth, size)
-    for place in range(n_xy):
-        for at, (lane, size) in enumerate(tiles):
-            rows = wide[at, pl.ds(place, depth, stride=n_xy), :]
-            rows_ref[place, :, lane:lane + size] = rows[:, :size].astype(jnp.bfloat16)
-    mine = position("gcol") * blocks
-    parts = []
-    for at in range(blocks):
-        layer, place = (mine + at) // n_xy, (mine + at) % n_xy
-        rows = jnp.concatenate(
-            [wide[tile, pl.ds(place, depth, stride=n_xy), :] for tile in range(len(tiles))],
-            axis=1)[:, :wide_sub]
-        part = jnp.where(layer == 1, rows[:, sub:2 * sub], rows[:, :sub])
-        parts.append(jnp.where(layer == 2, rows[:, 2 * sub:], part))
-    whole = jnp.concatenate(parts, axis=1).astype(jnp.bfloat16)
-    for target in range(col_ref.shape[0]):
-        col_ref[target] = whole
-
-
-def deal(gathered, n_xy, width, n_grow):
-    n_gcol, rows, wide_sub = gathered.shape
-    depth = n_gcol * rows // n_xy
-    vmem = pl.BlockSpec(memory_space=pltpu.VMEM)
-    return pl.pallas_call(
-        deal_kernel,
-        out_shape=(jax.ShapeDtypeStruct((n_xy, depth, wide_sub), jnp.bfloat16),
-                   jax.ShapeDtypeStruct((n_grow, depth, width), jnp.bfloat16)),
-        in_specs=[vmem],
-        out_specs=(vmem, vmem),
-        scratch_shapes=[pltpu.VMEM((-(-wide_sub // LANES), n_gcol * rows, LANES), jnp.float32)],
-        compiler_params=pltpu.CompilerParams(vmem_limit_bytes=24 * 1024 * 1024),
-        cost_estimate=pl.CostEstimate(flops=10**6, bytes_accessed=2 * 10**6, transcendentals=0),
-    )(gathered)
-
-
-def tile_kernel(row_ref, *refs):
-    col_refs, own_ref, sent_refs, total = refs[:NX], refs[NX], refs[NX + 1:-1], refs[-1]
-    n_grow, depth, width = col_refs[0].shape
-    wide_sub = row_ref.shape[2]
+        block = row_ref[:, :, lane:lane + size].astype(jnp.float32)
+        wide[at, :, :size] = block.reshape(n_gcol * stride, size)
     mine = position("pair") % NX
     value = None
     for step, col_ref in enumerate(col_refs):
-        source = (mine + (NX - step)) % NX
-        left = row_ref[pl.ds(source * n_grow, n_grow)].reshape(n_grow * depth, wide_sub)
+        first = (mine + (NX - step)) % NX * (n_grow * doubled)
+        left = jnp.concatenate(
+            [jnp.concatenate([wide[at, pl.ds(first + place, n_gcol, stride=stride), :]
+                              for place in range(n_grow * doubled)], axis=0)
+             for at in range(len(tiles))], axis=1)[:, :wide_sub].astype(jnp.bfloat16)
         term = lax.dot_general(
             left, col_ref[...].reshape(n_grow * depth, width), (((0,), (0,)), ((), ())),
             preferred_element_type=jnp.float32)
@@ -266,7 +260,7 @@
 
 
 def tile(row, cols, n_z):
-    n_xy, depth, wide_sub = row.shape
+    n_gcol, rows, wide_sub = row.shape
     width = cols[0].shape[2]
     sub = wide_sub // n_z
     vmem = pl.BlockSpec(memory_space=pltpu.VMEM)
@@ -276,10 +270,11 @@
         + [jax.ShapeDtypeStruct((sub, width), jnp.bfloat16)] * (n_z - 1),
         in_specs=[vmem] * (1 + NX),
         out_specs=[vmem] * n_z,
-        scratch_shapes=[pltpu.VMEM((wide_sub, width), jnp.float32)],
+        scratch_shapes=[pltpu.VMEM((-(-wide_sub // LANES), n_gcol * rows, LANES), jnp.float32),
+                        pltpu.VMEM((wide_sub, width), jnp.float32)],
         compiler_params=pltpu.CompilerParams(vmem_limit_bytes=40 * 1024 * 1024),
         cost_estimate=pl.CostEstimate(
-            flops=2 * n_xy * depth * wide_sub * width, bytes_accessed=5 * 10**6, transcendentals=0),
+            flops=2 * n_gcol * rows * wide_sub * width, bytes_accessed=5 * 10**6, transcendentals=0),
     )(row, *cols)
 
 
@@ -293,13 +288,13 @@
     n_xy = NX * n_grow
     xy_groups = [[(z * NX + x) * n_grow + y for x in range(NX) for y in range(n_grow)]
                  for z in range(n_z)]
-    mine = amplitudes_of(
+    col, row = amplitudes_of(
         pair_valence, pair_conduction, pair_count, valence_energy, conduction_energy,
-        valence, conduction, g_index, n_xy, n_z * sub)
-    mine = lax.all_gather(mine, "gcol", axis=0, tiled=True)
-    row, col = deal(mine, n_xy, width, n_grow)
+        valence, conduction, g_index, n_xy, n_z * sub, n_gcol)
     row = lax.all_to_all(row, ("pair", "grow"), 0, 0, tiled=True, axis_index_groups=xy_groups)
+    col = spread(lax.all_to_all(col, "gcol", 0, 0, tiled=True), row, n_grow)
     col = lax.all_to_all(col, "grow", 0, 0, tiled=True)
+    row = lax.all_gather(row.reshape(1, -1, n_z * sub), "gcol", axis=0, tiled=True)
     cols = [col] + [
         lax.ppermute(col, "pair", [(z * NX + x, z * NX + (x + step) % NX)
                                    for z in range(n_z) for x in range(NX)])

time: 130 us -> 129 us (level)
  blocking collectives: 52.7 us -> 88.7 us
  waiting for transfers between devices: 40.7 us -> 10.7 us
  starting transfers between devices: 20.3 us -> 14.4 us
  Pallas kernels: 13.2 us -> 11 us
    all_to_all x0 -> x2, blocking collectives: none -> 46.5 us  [the longest x1 26.9 us: local(): col = spread(lax.all_to_all(col, 'gcol', 0, 0, tiled=True), row, n_grow)]
    ppermute x3, waiting for transfers between devices: 21.5 us -> 1.97 us  [local(): lax.ppermute(col, 'pair', [(z * NX + x, z * NX + (x + step) % NX) for z i...]
    all_to_all x1 -> x0, waiting for transfers between devices: 10.5 us -> none  [local(): lax.all_to_all(row, ('pair', 'grow'), 0, 0, tiled=True, axis_index_groups...]
    all_gather x1, blocking collectives: 29 us -> 22.6 us  [local(): lax.all_gather(row.reshape(1, -1, n_z * sub), 'gcol', axis=0, tiled=True)]
    all_to_all x1 -> x0, starting transfers between devices: 4.48 us -> none  [local(): lax.all_to_all(row, ('pair', 'grow'), 0, 0, tiled=True, axis_index_groups...]
    all_to_all x1, blocking collectives: 23.7 us -> 19.6 us  [local(): col = lax.all_to_all(col, 'grow', 0, 0, tiled=True)]
    pallas_call x2, Pallas kernels: 12.2 us -> 9.46 us  [the longest x1 9.35 us: amplitudes_of(): pl.pallas_call(amplitude_kernel, out_shape=(jax.ShapeDtypeStruct((n_gcol,...]
    ppermute x3, starting transfers between devices: 9.33 us -> 7.85 us  [local(): lax.ppermute(col, 'pair', [(z * NX + x, z * NX + (x + step) % NX) for z i...]
  transfers between devices with their start and end apart: 6 -> 5, of which waited for: 6 -> 3; matrix products, arithmetic and copies ran while one was open for 0% -> 1% of each run, Pallas kernels for 0% -> 0%
where the time goes in v4:
time: 129 us; the launch traced here: 128 us
  blocking collectives  88.7 us (69%)
  starting transfers between devices  14.4 us (11%)
  Pallas kernels  11 us (9%)
  waiting for transfers between devices  10.7 us (8%)
  local copies, waits for them, and re-layouts  1.59 us (1%)
    all_to_all x1, blocking collectives, local(): col = spread(lax.all_to_all(col, 'gcol', 0, 0, tiled=True), row, n_grow)  26.9 us
    all_gather x1, blocking collectives, local(): lax.all_gather(row.reshape(1, -1, n_z * sub), 'gcol', axis=0, tiled=True)  22.6 us
    all_to_all x1, blocking collectives, local(): col = lax.all_to_all(col, 'grow', 0, 0, tiled=True)  19.6 us
    all_to_all x1, blocking collectives, local(): lax.all_to_all(row, ('pair', 'grow'), 0, 0, tiled=True, axis_index_groups...  19.5 us
    pallas_call x1, Pallas kernels, amplitudes_of(): pl.pallas_call(amplitude_kernel, out_shape=(jax.ShapeDtypeStruct((n_gcol,...  9.35 us
    ppermute x2, waiting for transfers between devices, local(): lax.ppermute(block, 'pair', [(z * NX + x, (z + step) % n_z * NX + x) for...  8.68 us
    ppermute x3, starting transfers between devices, local(): lax.ppermute(col, 'pair', [(z * NX + x, z * NX + (x + step) % NX) for z i...  7.85 us
    ppermute x2, starting transfers between devices, local(): lax.ppermute(block, 'pair', [(z * NX + x, (z + step) % n_z * NX + x) for...  6.56 us
  transfers between devices with their start and end apart: 5, of which 3 were waited for; matrix products, arithmetic and copies ran while one was open for 1% of the time, Pallas kernels for 0%

profile of v4, /device:TPU:1, one launch (start us, length us, event | category | flops | bytes accessed | tf_op | source)
XLA Modules:
  0.0 128.0 jit_solution(7495718006996509537)
XLA Ops:
  0.7 9.3 %shard_map.127 = (bf16[8,4,1152]{2,1,0:T(4,128)(2,1)}, bf16[32,4,288]{2,1,0:T(4,128)(2,1)}) custom-call(s32[2]{0:T(128)} %pv_hbm.1, s32[2]{0:T(128)} %pc_hbm.1, s32[1]{0:T(128)S(6)} %copy.16.count_hbm, f32[48]{0:T(128)} %ve_hbm.1, f32[16]{0:T(128)} %ce_hbm.1, bf16[48,32768]{1,0:T(8,128)(2,1)} %valence_hbm.1, bf16[16,32768]{1,0:T(8,128)(2,1)} %conduction_hbm.1, ...), custom_call_target="tpu_custom_call" | custom-call | flops 4000000000 | bytes 5000000 | tf_op jit(solution)/shard_map/pallas_call | solution.py:183
  10.0 19.5 %all_to_all.15.first_ref = bf16[32,4,288]{2,1,0:T(4,128)(2,1)S(1)} all-to-all(bf16[32,4,288]{2,1,0:T(4,128)(2,1)} %get-tuple-element.10), channel_id=1, replica_groups={{0,8,16,24,32,40,48,56,64,72,80,88,96,104,112,120,128,136,144,152,160,1..., dimensions={0} | all-to-all | bytes 147456 | tf_op jit(solution)/shard_map/all_to_all | solution.py:294
  29.5 26.9 %all_to_all.16.in_ref = bf16[8,4,1152]{2,1,0:T(4,128)(2,1)S(1)} all-to-all(bf16[8,4,1152]{2,1,0:T(4,128)(2,1)} %get-tuple-element.11), channel_id=1, replica_groups=mesh['pair'=12,'grow'=8,'gcol'=8] {'gcol'}, dimensions={0} | all-to-all | bytes 147456 | tf_op jit(solution)/shard_map/all_to_all | solution.py:295
  56.5 0.1 shard_map.128
  56.6 19.6 %all_to_all.17.refs_0_ = bf16[8,32,1152]{2,1,0:T(8,128)(2,1)S(1)} all-to-all(bf16[8,32,1152]{2,1,0:T(8,128)(2,1)S(1)} %shard_map.128), channel_id=1, replica_groups=mesh['pair'=12,'grow'=8,'gcol'=8] {'grow'}, dimensions={0} | all-to-all | bytes 1179648 | tf_op jit(solution)/shard_map/all_to_all | solution.py:296
  76.2 2.8 %collective-permute-start.2 = (bf16[8,32,1152]{2,1,0:T(8,128)(2,1)S(1)}, bf16[8,32,1152]{2,1,0:T(8,128)(2,1)S(1)}, u32[]{:S(2)}, u32[]{:S(2)}) collective-permute-start(bf16[8,32,1152]{2,1,0:T(8,128)(2,1)S(1)} %all_to_all.17.refs_0_), channel_id=1, source_target_pairs={{0,192},{64,0},{128,64},{192,128},{256,448},{320,256},{384,320},{4... | collective-permute-start | bytes 1769480 | tf_op jit(solution)/shard_map/ppermute | solution.py:299
  79.0 3.2 %collective-permute-start.1 = (bf16[8,32,1152]{2,1,0:T(8,128)(2,1)S(1)}, bf16[8,32,1152]{2,1,0:T(8,128)(2,1)S(1)}, u32[]{:S(2)}, u32[]{:S(2)}) collective-permute-start(bf16[8,32,1152]{2,1,0:T(8,128)(2,1)S(1)} %all_to_all.17.refs_0_), channel_id=1, source_target_pairs={{0,128},{64,192},{128,0},{192,64},{256,384},{320,448},{384,256},{4... | collective-permute-start | bytes 1769480 | tf_op jit(solution)/shard_map/ppermute | solution.py:299
  82.2 1.9 %collective-permute-start = (bf16[8,32,1152]{2,1,0:T(8,128)(2,1)S(1)}, bf16[8,32,1152]{2,1,0:T(8,128)(2,1)S(1)}, u32[]{:S(2)}, u32[]{:S(2)}) collective-permute-start(bf16[8,32,1152]{2,1,0:T(8,128)(2,1)S(1)} %all_to_all.17.refs_0_), channel_id=1, source_target_pairs={{0,64},{64,128},{128,192},{192,0},{256,320},{320,384},{384,448},{4... | collective-permute-start | bytes 1769480 | tf_op jit(solution)/shard_map/ppermute | solution.py:299
  84.1 0.1 reshape.7
  84.2 0.1 copy.14
  84.3 22.6 %all_gather.3 = bf16[8,128,288]{1,2,0:T(8,128)(2,1)} all-gather(bf16[1,128,288]{1,2,0:T(8,128)(2,1)S(1)} %copy.14), channel_id=1, replica_groups=mesh['pair'=12,'grow'=8,'gcol'=8] {'gcol'}, dimensions={0}, use_global_device_ids=true | all-gather | bytes 663552 | tf_op jit(solution)/shard_map/all_gather | solution.py:297
  106.9 1.4 %copy.15.row_ref = bf16[8,128,288]{2,1,0:T(8,128)(2,1)S(1)} copy(bf16[8,128,288]{1,2,0:T(8,128)(2,1)} %all_gather.3) | data formatting | bytes 1179648 | tf_op jit(solution)/shard_map/all_gather | solution.py:297
  108.3 0.0 collective-permute-done.2.refs_3_
  108.3 0.0 collective-permute-done.1.refs_2_
  108.4 2.0 %collective-permute-done.refs_1_ = bf16[8,32,1152]{2,1,0:T(8,128)(2,1)S(1)} collective-permute-done((bf16[8,32,1152]{2,1,0:T(8,128)(2,1)S(1)}, bf16[8,32,1152]{2,1,0:T(8,128)(2,1)S(1)}, u32[]{:S(2)}, u32[]{:S(2)}) %collective-permute-start) | collective-permute-done | bytes 589856 | tf_op jit(solution)/shard_map/ppermute | solution.py:299
  110.3 1.6 %shard_map.129 = (f32[96,1152]{1,0:T(8,128)S(1)}, bf16[96,1152]{1,0:T(8,128)(2,1)S(1)}, bf16[96,1152]{1,0:T(8,128)(2,1)S(1)}) custom-call(bf16[8,128,288]{2,1,0:T(8,128)(2,1)S(1)} %copy.15.row_ref, bf16[8,32,1152]{2,1,0:T(8,128)(2,1)S(1)} %all_to_all.17.refs_0_, bf16[8,32,1152]{2,1,0:T(8,128)(2,1)S(1)} %collective-permute-done.refs_1_, ...), custom_call_target="tpu_custom_call" | custom-call | flops 679477248 | bytes 5000000 | tf_op jit(solution)/shard_map/pallas_call | solution.py:267
  111.9 3.5 %collective-permute-start.3 = (bf16[96,1152]{1,0:T(8,128)(2,1)S(1)}, bf16[96,1152]{1,0:T(8,128)(2,1)S(1)}, u32[]{:S(2)}, u32[]{:S(2)}) collective-permute-start(bf16[96,1152]{1,0:T(8,128)(2,1)S(1)} %get-tuple-element.13), channel_id=1, source_target_pairs={{0,256},{64,320},{128,384},{192,448},{256,512},{320,576},{384,640}... | collective-permute-start | bytes 663560 | tf_op jit(solution)/shard_map/ppermute | solution.py:304
  115.4 3.1 %collective-permute-start.4 = (bf16[96,1152]{1,0:T(8,128)(2,1)S(1)}, bf16[96,1152]{1,0:T(8,128)(2,1)S(1)}, u32[]{:S(2)}, u32[]{:S(2)}) collective-permute-start(bf16[96,1152]{1,0:T(8,128)(2,1)S(1)} %get-tuple-element.14), channel_id=1, source_target_pairs={{0,512},{64,576},{128,640},{192,704},{256,0},{320,64},{384,128},{4... | collective-permute-start | bytes 663560 | tf_op jit(solution)/shard_map/ppermute | solution.py:304
  118.5 3.5 %collective-permute-done.3 = bf16[96,1152]{1,0:T(8,128)(2,1)S(1)} collective-permute-done((bf16[96,1152]{1,0:T(8,128)(2,1)S(1)}, bf16[96,1152]{1,0:T(8,128)(2,1)S(1)}, u32[]{:S(2)}, u32[]{:S(2)}) %collective-permute-start.3) | collective-permute-done | bytes 221216 | tf_op jit(solution)/shard_map/ppermute | solution.py:304
  122.0 5.2 %collective-permute-done.4 = bf16[96,1152]{1,0:T(8,128)(2,1)S(1)} collective-permute-done((bf16[96,1152]{1,0:T(8,128)(2,1)S(1)}, bf16[96,1152]{1,0:T(8,128)(2,1)S(1)}, u32[]{:S(2)}, u32[]{:S(2)}) %collective-permute-start.4) | collective-permute-done | bytes 221216 | tf_op jit(solution)/shard_map/ppermute | solution.py:304
  127.2 0.8 negate_multiply_fusion
Async XLA Ops:
  76.2 32.1 %collective-permute-start.2 = (bf16[8,32,1152]{2,1,0:T(8,128)(2,1)S(1)}, bf16[8,32,1152]{2,1,0:T(8,128)(2,1)S(1)}, u32[]{:S(2)}, u32[]{:S(2)}) collective-permute-start(bf16[8,32,1152]{2,1,0:T(8,128)(2,1)S(1)} %all_to_all.17.refs_0_), channel_id=1, source_target_pairs={{0,192},{64,0},{128,64},{192,128},{256,448},{320,256},{384,320},{4... | collective-permute-start | bytes 1769480 | tf_op jit(solution)/shard_map/ppermute | solution.py:299
  79.0 29.3 %collective-permute-start.1 = (bf16[8,32,1152]{2,1,0:T(8,128)(2,1)S(1)}, bf16[8,32,1152]{2,1,0:T(8,128)(2,1)S(1)}, u32[]{:S(2)}, u32[]{:S(2)}) collective-permute-start(bf16[8,32,1152]{2,1,0:T(8,128)(2,1)S(1)} %all_to_all.17.refs_0_), channel_id=1, source_target_pairs={{0,128},{64,192},{128,0},{192,64},{256,384},{320,448},{384,256},{4... | collective-permute-start | bytes 1769480 | tf_op jit(solution)/shard_map/ppermute | solution.py:299
  82.2 28.1 %collective-permute-start = (bf16[8,32,1152]{2,1,0:T(8,128)(2,1)S(1)}, bf16[8,32,1152]{2,1,0:T(8,128)(2,1)S(1)}, u32[]{:S(2)}, u32[]{:S(2)}) collective-permute-start(bf16[8,32,1152]{2,1,0:T(8,128)(2,1)S(1)} %all_to_all.17.refs_0_), channel_id=1, source_target_pairs={{0,64},{64,128},{128,192},{192,0},{256,320},{320,384},{384,448},{4... | collective-permute-start | bytes 1769480 | tf_op jit(solution)/shard_map/ppermute | solution.py:299
  111.9 10.0 %collective-permute-start.3 = (bf16[96,1152]{1,0:T(8,128)(2,1)S(1)}, bf16[96,1152]{1,0:T(8,128)(2,1)S(1)}, u32[]{:S(2)}, u32[]{:S(2)}) collective-permute-start(bf16[96,1152]{1,0:T(8,128)(2,1)S(1)} %get-tuple-element.13), channel_id=1, source_target_pairs={{0,256},{64,320},{128,384},{192,448},{256,512},{320,576},{384,640}... | collective-permute-start | bytes 663560 | tf_op jit(solution)/shard_map/ppermute | solution.py:304
  115.4 11.8 %collective-permute-start.4 = (bf16[96,1152]{1,0:T(8,128)(2,1)S(1)}, bf16[96,1152]{1,0:T(8,128)(2,1)S(1)}, u32[]{:S(2)}, u32[]{:S(2)}) collective-permute-start(bf16[96,1152]{1,0:T(8,128)(2,1)S(1)} %get-tuple-element.14), channel_id=1, source_target_pairs={{0,512},{64,576},{128,640},{192,704},{256,0},{320,64},{384,128},{4... | collective-permute-start | bytes 663560 | tf_op jit(solution)/shard_map/ppermute | solution.py:304

commit v5 on v4

--- a/solution.py
+++ b/solution.py
@@ -100,7 +100,7 @@
                      lane_hbm, row_hbm, same_hbm, swap_hbm, last_hbm, g_hbm,
                      col_ref, rows_ref, pv_ref, pc_ref, count_ref, ve_ref, ce_ref, valence_ref,
                      conduction_ref, lane_ref, row_ref, same_ref, swap_ref, last_ref, g_ref,
-                     wide, amp, flat, sems):
+                     wide, amp, flat, ordered, sems):
     slots = 2
     n_xy, doubled, wide_sub = rows_ref.shape
     sub = wide_sub // 3
@@ -170,8 +170,13 @@
         starts = [(z * n_xy + place) * sub for z in range(3)]
         block = jnp.concatenate([flat[0:doubled, at:at + sub] for at in starts], axis=1)
         rows_ref[place] = block.astype(jnp.bfloat16)
-    for target in range(col_ref.shape[0]):
-        col_ref[target] = flat[0:doubled, target * width:(target + 1) * width].astype(jnp.bfloat16)
+    targets = flat.shape[1] // width
+    for at in range(width // LANES):
+        for target in range(targets):
+            lane = target * width + at * LANES
+            ordered[at, pl.ds(target, doubled, stride=targets), :] = flat[
+                0:doubled, lane:lane + LANES]
+        col_ref[0, :, at * LANES:(at + 1) * LANES] = ordered[at].astype(jnp.bfloat16)
 
 
 def amplitudes_of(pv, pc, count, ve, ce, valence, conduction, g_index, n_xy, wide_sub, n_gcol):
@@ -180,10 +185,11 @@
     g_rows = g_index.reshape(-1, LANES)
     arrays = [valence, conduction, *consts, g_rows]
     doubled = 2 * pv.shape[0]
+    width = g_index.shape[0] // n_gcol
     return pl.pallas_call(
         amplitude_kernel,
         out_shape=(
-            jax.ShapeDtypeStruct((n_gcol, doubled, g_index.shape[0] // n_gcol), jnp.bfloat16),
+            jax.ShapeDtypeStruct((1, doubled * n_gcol, width), jnp.bfloat16),
             jax.ShapeDtypeStruct((n_xy, doubled, wide_sub), jnp.bfloat16)),
         in_specs=[hbm] * 13,
         out_specs=(pl.BlockSpec(memory_space=pltpu.VMEM),) * 2,
@@ -193,6 +199,7 @@
             pltpu.VMEM((4, 8 * ROWS, LANES), jnp.float32),
             pltpu.VMEM((ROWS, ROWS), jnp.bfloat16),
             pltpu.VMEM((8, g_index.shape[0]), jnp.float32),
+            pltpu.VMEM((width // LANES, doubled * n_gcol, LANES), jnp.float32),
             pltpu.SemaphoreType.DMA((13,)),
         ],
         compiler_params=pltpu.CompilerParams(vmem_limit_bytes=60 * 1024 * 1024),
@@ -202,27 +209,27 @@
 
 def spread_kernel(in_ref, first_ref, out_ref, wide):
     del first_ref
-    n_gcol, doubled, width = in_ref.shape
-    for at in range(n_gcol):
-        block = in_ref[at].astype(jnp.float32)
-        for lane in range(width // LANES):
-            wide[lane, pl.ds(at, doubled, stride=n_gcol), :] = block[
-                :, lane * LANES:(lane + 1) * LANES]
-    for lane in range(width // LANES):
-        block = wide[lane].astype(jnp.bfloat16)
+    n_gcol, depth, width = in_ref.shape
+    mine = position("gcol")
+    for at in range(width // LANES):
+        lanes = slice(at * LANES, (at + 1) * LANES)
+        wide[at] = in_ref[:, :, lanes].astype(jnp.float32).reshape(n_gcol * depth, LANES)
+        block = jnp.concatenate(
+            [wide[at, pl.ds(row * n_gcol + mine, n_gcol, stride=depth), :]
+             for row in range(depth // n_gcol)], axis=0).astype(jnp.bfloat16)
         for target in range(out_ref.shape[0]):
-            out_ref[target, :, lane * LANES:(lane + 1) * LANES] = block
+            out_ref[target, :, lanes] = block
 
 
 def spread(col, first, n_grow):
-    n_gcol, doubled, width = col.shape
+    n_gcol, depth, width = col.shape
     vmem = pl.BlockSpec(memory_space=pltpu.VMEM)
     return pl.pallas_call(
         spread_kernel,
-        out_shape=jax.ShapeDtypeStruct((n_grow, n_gcol * doubled, width), jnp.bfloat16),
+        out_shape=jax.ShapeDtypeStruct((n_grow, depth, width), jnp.bfloat16),
         in_specs=[vmem, pl.BlockSpec(memory_space=pl.ANY)],
         out_specs=vmem,
-        scratch_shapes=[pltpu.VMEM((width // LANES, n_gcol * doubled, LANES), jnp.float32)],
+        scratch_shapes=[pltpu.VMEM((width // LANES, n_gcol * depth, LANES), jnp.float32)],
         compiler_params=pltpu.CompilerParams(vmem_limit_bytes=16 * 1024 * 1024),
         cost_estimate=pl.CostEstimate(flops=10**6, bytes_accessed=2 * 10**6, transcendentals=0),
     )(col, first)
@@ -292,7 +299,7 @@
         pair_valence, pair_conduction, pair_count, valence_energy, conduction_energy,
         valence, conduction, g_index, n_xy, n_z * sub, n_gcol)
     row = lax.all_to_all(row, ("pair", "grow"), 0, 0, tiled=True, axis_index_groups=xy_groups)
-    col = spread(lax.all_to_all(col, "gcol", 0, 0, tiled=True), row, n_grow)
+    col = spread(lax.all_gather(col, "gcol", axis=0, tiled=True), row, n_grow)
     col = lax.all_to_all(col, "grow", 0, 0, tiled=True)
     row = lax.all_gather(row.reshape(1, -1, n_z * sub), "gcol", axis=0, tiled=True)
     cols = [col] + [

time: 129 us -> 127 us (0.984)
  blocking collectives: 88.7 us -> 73.2 us
  starting transfers between devices: 14.4 us -> 26 us
  waiting for transfers between devices: 10.7 us -> 12.7 us
    all_to_all x2 -> x0, blocking collectives: 46.5 us -> none  [the longest x1 26.9 us: local(): col = spread(lax.all_to_all(col, 'gcol', 0, 0, tiled=True), row, n_grow)]
    all_gather x0 -> x1, blocking collectives: none -> 27.4 us  [local(): col = spread(lax.all_gather(col, 'gcol', axis=0, tiled=True), row, n_grow)]
    all_to_all x0 -> x1, starting transfers between devices: none -> 10.5 us  [local(): lax.all_to_all(row, ('pair', 'grow'), 0, 0, tiled=True, axis_index_groups...]
    all_to_all x1, blocking collectives: 19.6 us -> 25.1 us  [local(): col = lax.all_to_all(col, 'grow', 0, 0, tiled=True)]
    ppermute x3, waiting for transfers between devices: 1.97 us -> 4.06 us  [local(): lax.ppermute(col, 'pair', [(z * NX + x, z * NX + (x + step) % NX) for z i...]
    all_gather x1, blocking collectives: 22.6 us -> 20.7 us  [local(): lax.all_gather(row.reshape(1, -1, n_z * sub), 'gcol', axis=0, tiled=True)]
    ppermute x3, starting transfers between devices: 7.85 us -> 9.28 us  [local(): lax.ppermute(col, 'pair', [(z * NX + x, z * NX + (x + step) % NX) for z i...]
  transfers between devices with their start and end apart: 5 -> 6, of which waited for: 3 -> 3; matrix products, arithmetic and copies ran while one was open for 1% -> 1% of each run, Pallas kernels for 0% -> 0%
where the time goes in v5:
time: 127 us; the launch traced here: 126 us
  blocking collectives  73.2 us (58%)
  starting transfers between devices  26 us (20%)
  waiting for transfers between devices  12.7 us (10%)
  Pallas kernels  11.2 us (9%)
  local copies, waits for them, and re-layouts  1.59 us (1%)
    all_gather x1, blocking collectives, local(): col = spread(lax.all_gather(col, 'gcol', axis=0, tiled=True), row, n_grow)  27.4 us
    all_to_all x1, blocking collectives, local(): col = lax.all_to_all(col, 'grow', 0, 0, tiled=True)  25.1 us
    all_gather x1, blocking collectives, local(): lax.all_gather(row.reshape(1, -1, n_z * sub), 'gcol', axis=0, tiled=True)  20.7 us
    all_to_all x1, starting transfers between devices, local(): lax.all_to_all(row, ('pair', 'grow'), 0, 0, tiled=True, axis_index_groups...  10.5 us
    pallas_call x1, Pallas kernels, amplitudes_of(): pl.pallas_call(amplitude_kernel, out_shape=(jax.ShapeDtypeStruct((1, doub...  9.36 us
    ppermute x3, starting transfers between devices, local(): lax.ppermute(col, 'pair', [(z * NX + x, z * NX + (x + step) % NX) for z i...  9.28 us
    ppermute x2, waiting for transfers between devices, local(): lax.ppermute(block, 'pair', [(z * NX + x, (z + step) % n_z * NX + x) for...  8.67 us
    ppermute x2, starting transfers between devices, local(): lax.ppermute(block, 'pair', [(z * NX + x, (z + step) % n_z * NX + x) for...  6.18 us
  transfers between devices with their start and end apart: 6, of which 3 were waited for; matrix products, arithmetic and copies ran while one was open for 1% of the time, Pallas kernels for 0%

profile of v5, /device:TPU:1, one launch (start us, length us, event | category | flops | bytes accessed | tf_op | source)
XLA Modules:
  0.0 126.2 jit_solution(16110984048268550495)
XLA Ops:
  0.7 9.4 %shard_map.127 = (bf16[1,32,1152]{2,1,0:T(8,128)(2,1)}, bf16[32,4,288]{2,1,0:T(4,128)(2,1)}) custom-call(s32[2]{0:T(128)} %pv_hbm.1, s32[2]{0:T(128)} %pc_hbm.1, s32[1]{0:T(128)S(6)} %copy.16.count_hbm, f32[48]{0:T(128)} %ve_hbm.1, f32[16]{0:T(128)} %ce_hbm.1, bf16[48,32768]{1,0:T(8,128)(2,1)} %valence_hbm.1, bf16[16,32768]{1,0:T(8,128)(2,1)} %conduction_hbm.1, ...), custom_call_target="tpu_custom_call" | custom-call | flops 4000000000 | bytes 5000000 | tf_op jit(solution)/shard_map/pallas_call | solution.py:189
  10.0 10.5 %all-to-all-start = ((bf16[32,4,288]{2,1,0:T(4,128)(2,1)}), bf16[32,4,288]{2,1,0:T(4,128)(2,1)S(1)}, u32[]{:S(2)}, u32[]{:S(2)}) async-start(bf16[32,4,288]{2,1,0:T(4,128)(2,1)} %get-tuple-element.10), calls=%async_computation | async-start | bytes 196608 | tf_op jit(solution)/shard_map/all_to_all | solution.py:301
  20.5 27.4 %all_gather.7.in_ref = bf16[8,32,1152]{2,1,0:T(8,128)(2,1)S(1)} all-gather(bf16[1,32,1152]{2,1,0:T(8,128)(2,1)} %get-tuple-element.11), channel_id=1, replica_groups=mesh['pair'=12,'grow'=8,'gcol'=8] {'gcol'}, dimensions={0}, use_global_device_ids=true | all-gather | bytes 663552 | tf_op jit(solution)/shard_map/all_gather | solution.py:302
  47.9 0.0 all-to-all-done.first_ref
  47.9 0.2 shard_map.128
  48.1 25.1 %all_to_all.10.refs_0_ = bf16[8,32,1152]{2,1,0:T(8,128)(2,1)S(1)} all-to-all(bf16[8,32,1152]{2,1,0:T(8,128)(2,1)S(1)} %shard_map.128), channel_id=1, replica_groups=mesh['pair'=12,'grow'=8,'gcol'=8] {'grow'}, dimensions={0} | all-to-all | bytes 1179648 | tf_op jit(solution)/shard_map/all_to_all | solution.py:303
  73.3 4.4 %collective-permute-start.2 = (bf16[8,32,1152]{2,1,0:T(8,128)(2,1)S(1)}, bf16[8,32,1152]{2,1,0:T(8,128)(2,1)S(1)}, u32[]{:S(2)}, u32[]{:S(2)}) collective-permute-start(bf16[8,32,1152]{2,1,0:T(8,128)(2,1)S(1)} %all_to_all.10.refs_0_), channel_id=1, source_target_pairs={{0,192},{64,0},{128,64},{192,128},{256,448},{320,256},{384,320},{4... | collective-permute-start | bytes 1769480 | tf_op jit(solution)/shard_map/ppermute | solution.py:306
  77.6 2.4 %collective-permute-start.1 = (bf16[8,32,1152]{2,1,0:T(8,128)(2,1)S(1)}, bf16[8,32,1152]{2,1,0:T(8,128)(2,1)S(1)}, u32[]{:S(2)}, u32[]{:S(2)}) collective-permute-start(bf16[8,32,1152]{2,1,0:T(8,128)(2,1)S(1)} %all_to_all.10.refs_0_), channel_id=1, source_target_pairs={{0,128},{64,192},{128,0},{192,64},{256,384},{320,448},{384,256},{4... | collective-permute-start | bytes 1769480 | tf_op jit(solution)/shard_map/ppermute | solution.py:306
  80.1 2.5 %collective-permute-start = (bf16[8,32,1152]{2,1,0:T(8,128)(2,1)S(1)}, bf16[8,32,1152]{2,1,0:T(8,128)(2,1)S(1)}, u32[]{:S(2)}, u32[]{:S(2)}) collective-permute-start(bf16[8,32,1152]{2,1,0:T(8,128)(2,1)S(1)} %all_to_all.10.refs_0_), channel_id=1, source_target_pairs={{0,64},{64,128},{128,192},{192,0},{256,320},{320,384},{384,448},{4... | collective-permute-start | bytes 1769480 | tf_op jit(solution)/shard_map/ppermute | solution.py:306
  82.6 0.1 reshape.7
  82.6 0.1 copy.14
  82.7 20.7 %all_gather.6 = bf16[8,128,288]{1,2,0:T(8,128)(2,1)} all-gather(bf16[1,128,288]{1,2,0:T(8,128)(2,1)S(1)} %copy.14), channel_id=1, replica_groups=mesh['pair'=12,'grow'=8,'gcol'=8] {'gcol'}, dimensions={0}, use_global_device_ids=true | all-gather | bytes 663552 | tf_op jit(solution)/shard_map/all_gather | solution.py:304
  103.4 1.4 %copy.15.row_ref = bf16[8,128,288]{2,1,0:T(8,128)(2,1)S(1)} copy(bf16[8,128,288]{1,2,0:T(8,128)(2,1)} %all_gather.6) | data formatting | bytes 1179648 | tf_op jit(solution)/shard_map/all_gather | solution.py:304
  104.8 0.0 collective-permute-done.2.refs_3_
  104.8 0.0 collective-permute-done.1.refs_2_
  104.9 4.1 %collective-permute-done.refs_1_ = bf16[8,32,1152]{2,1,0:T(8,128)(2,1)S(1)} collective-permute-done((bf16[8,32,1152]{2,1,0:T(8,128)(2,1)S(1)}, bf16[8,32,1152]{2,1,0:T(8,128)(2,1)S(1)}, u32[]{:S(2)}, u32[]{:S(2)}) %collective-permute-start) | collective-permute-done | bytes 589856 | tf_op jit(solution)/shard_map/ppermute | solution.py:306
  108.9 1.6 %shard_map.129 = (f32[96,1152]{1,0:T(8,128)S(1)}, bf16[96,1152]{1,0:T(8,128)(2,1)S(1)}, bf16[96,1152]{1,0:T(8,128)(2,1)S(1)}) custom-call(bf16[8,128,288]{2,1,0:T(8,128)(2,1)S(1)} %copy.15.row_ref, bf16[8,32,1152]{2,1,0:T(8,128)(2,1)S(1)} %all_to_all.10.refs_0_, bf16[8,32,1152]{2,1,0:T(8,128)(2,1)S(1)} %collective-permute-done.refs_1_, ...), custom_call_target="tpu_custom_call" | custom-call | flops 679477248 | bytes 5000000 | tf_op jit(solution)/shard_map/pallas_call | solution.py:274
  110.5 3.7 %collective-permute-start.3 = (bf16[96,1152]{1,0:T(8,128)(2,1)S(1)}, bf16[96,1152]{1,0:T(8,128)(2,1)S(1)}, u32[]{:S(2)}, u32[]{:S(2)}) collective-permute-start(bf16[96,1152]{1,0:T(8,128)(2,1)S(1)} %get-tuple-element.13), channel_id=1, source_target_pairs={{0,256},{64,320},{128,384},{192,448},{256,512},{320,576},{384,640}... | collective-permute-start | bytes 663560 | tf_op jit(solution)/shard_map/ppermute | solution.py:311
  114.2 2.5 %collective-permute-start.4 = (bf16[96,1152]{1,0:T(8,128)(2,1)S(1)}, bf16[96,1152]{1,0:T(8,128)(2,1)S(1)}, u32[]{:S(2)}, u32[]{:S(2)}) collective-permute-start(bf16[96,1152]{1,0:T(8,128)(2,1)S(1)} %get-tuple-element.14), channel_id=1, source_target_pairs={{0,512},{64,576},{128,640},{192,704},{256,0},{320,64},{384,128},{4... | collective-permute-start | bytes 663560 | tf_op jit(solution)/shard_map/ppermute | solution.py:311
  116.7 3.1 %collective-permute-done.3 = bf16[96,1152]{1,0:T(8,128)(2,1)S(1)} collective-permute-done((bf16[96,1152]{1,0:T(8,128)(2,1)S(1)}, bf16[96,1152]{1,0:T(8,128)(2,1)S(1)}, u32[]{:S(2)}, u32[]{:S(2)}) %collective-permute-start.3) | collective-permute-done | bytes 221216 | tf_op jit(solution)/shard_map/ppermute | solution.py:311
  119.8 5.6 %collective-permute-done.4 = bf16[96,1152]{1,0:T(8,128)(2,1)S(1)} collective-permute-done((bf16[96,1152]{1,0:T(8,128)(2,1)S(1)}, bf16[96,1152]{1,0:T(8,128)(2,1)S(1)}, u32[]{:S(2)}, u32[]{:S(2)}) %collective-permute-start.4) | collective-permute-done | bytes 221216 | tf_op jit(solution)/shard_map/ppermute | solution.py:311
  125.4 0.8 negate_multiply_fusion
Async XLA Ops:
  10.0 37.9 %all-to-all-start = ((bf16[32,4,288]{2,1,0:T(4,128)(2,1)}), bf16[32,4,288]{2,1,0:T(4,128)(2,1)S(1)}, u32[]{:S(2)}, u32[]{:S(2)}) async-start(bf16[32,4,288]{2,1,0:T(4,128)(2,1)} %get-tuple-element.10), calls=%async_computation | async-start | bytes 196608 | tf_op jit(solution)/shard_map/all_to_all | solution.py:301
  73.3 31.6 %collective-permute-start.2 = (bf16[8,32,1152]{2,1,0:T(8,128)(2,1)S(1)}, bf16[8,32,1152]{2,1,0:T(8,128)(2,1)S(1)}, u32[]{:S(2)}, u32[]{:S(2)}) collective-permute-start(bf16[8,32,1152]{2,1,0:T(8,128)(2,1)S(1)} %all_to_all.10.refs_0_), channel_id=1, source_target_pairs={{0,192},{64,0},{128,64},{192,128},{256,448},{320,256},{384,320},{4... | collective-permute-start | bytes 1769480 | tf_op jit(solution)/shard_map/ppermute | solution.py:306
  77.6 27.2 %collective-permute-start.1 = (bf16[8,32,1152]{2,1,0:T(8,128)(2,1)S(1)}, bf16[8,32,1152]{2,1,0:T(8,128)(2,1)S(1)}, u32[]{:S(2)}, u32[]{:S(2)}) collective-permute-start(bf16[8,32,1152]{2,1,0:T(8,128)(2,1)S(1)} %all_to_all.10.refs_0_), channel_id=1, source_target_pairs={{0,128},{64,192},{128,0},{192,64},{256,384},{320,448},{384,256},{4... | collective-permute-start | bytes 1769480 | tf_op jit(solution)/shard_map/ppermute | solution.py:306
  80.1 28.9 %collective-permute-start = (bf16[8,32,1152]{2,1,0:T(8,128)(2,1)S(1)}, bf16[8,32,1152]{2,1,0:T(8,128)(2,1)S(1)}, u32[]{:S(2)}, u32[]{:S(2)}) collective-permute-start(bf16[8,32,1152]{2,1,0:T(8,128)(2,1)S(1)} %all_to_all.10.refs_0_), channel_id=1, source_target_pairs={{0,64},{64,128},{128,192},{192,0},{256,320},{320,384},{384,448},{4... | collective-permute-start | bytes 1769480 | tf_op jit(solution)/shard_map/ppermute | solution.py:306
  110.5 9.3 %collective-permute-start.3 = (bf16[96,1152]{1,0:T(8,128)(2,1)S(1)}, bf16[96,1152]{1,0:T(8,128)(2,1)S(1)}, u32[]{:S(2)}, u32[]{:S(2)}) collective-permute-start(bf16[96,1152]{1,0:T(8,128)(2,1)S(1)} %get-tuple-element.13), channel_id=1, source_target_pairs={{0,256},{64,320},{128,384},{192,448},{256,512},{320,576},{384,640}... | collective-permute-start | bytes 663560 | tf_op jit(solution)/shard_map/ppermute | solution.py:311
  114.2 11.2 %collective-permute-start.4 = (bf16[96,1152]{1,0:T(8,128)(2,1)S(1)}, bf16[96,1152]{1,0:T(8,128)(2,1)S(1)}, u32[]{:S(2)}, u32[]{:S(2)}) collective-permute-start(bf16[96,1152]{1,0:T(8,128)(2,1)S(1)} %get-tuple-element.14), channel_id=1, source_target_pairs={{0,512},{64,576},{128,640},{192,704},{256,0},{320,64},{384,128},{4... | collective-permute-start | bytes 663560 | tf_op jit(solution)/shard_map/ppermute | solution.py:311

commit v6 on v5

--- a/solution.py
+++ b/solution.py
@@ -207,8 +207,8 @@
     )(pv, pc, count, ve, ce, *arrays)
 
 
-def spread_kernel(in_ref, first_ref, out_ref, wide):
-    del first_ref
+def spread_kernel(in_ref, row_ref, out_ref, same_ref, wide):
+    del row_ref, same_ref
     n_gcol, depth, width = in_ref.shape
     mine = position("gcol")
     for at in range(width // LANES):
@@ -221,40 +221,40 @@
             out_ref[target, :, lanes] = block
 
 
-def spread(col, first, n_grow):
+def spread(col, row, copies):
     n_gcol, depth, width = col.shape
     vmem = pl.BlockSpec(memory_space=pltpu.VMEM)
     return pl.pallas_call(
         spread_kernel,
-        out_shape=jax.ShapeDtypeStruct((n_grow, depth, width), jnp.bfloat16),
+        out_shape=(jax.ShapeDtypeStruct((copies, depth, width), jnp.bfloat16),
+                   jax.ShapeDtypeStruct(row.shape, row.dtype)),
         in_specs=[vmem, pl.BlockSpec(memory_space=pl.ANY)],
-        out_specs=vmem,
+        out_specs=(vmem, pl.BlockSpec(memory_space=pl.ANY)),
+        input_output_aliases={1: 1},
         scratch_shapes=[pltpu.VMEM((width // LANES, n_gcol * depth, LANES), jnp.float32)],
         compiler_params=pltpu.CompilerParams(vmem_limit_bytes=16 * 1024 * 1024),
         cost_estimate=pl.CostEstimate(flops=10**6, bytes_accessed=2 * 10**6, transcendentals=0),
-    )(col, first)
-
-
-def tile_kernel(row_ref, *refs):
-    col_refs, own_ref, sent_refs = refs[:NX], refs[NX], refs[NX + 1:-2]
-    wide, total = refs[-2:]
-    n_grow, depth, width = col_refs[0].shape
+    )(col, row)
+
+
+def tile_kernel(row_ref, col_ref, own_ref, *refs):
+    sent_refs, (wide, total) = refs[:-2], refs[-2:]
+    n_xy, depth, width = col_ref.shape
     n_gcol, stride, wide_sub = row_ref.shape
-    doubled = depth // n_gcol
     tiles = lane_tiles(wide_sub)
     for at, (lane, size) in enumerate(tiles):
         block = row_ref[:, :, lane:lane + size].astype(jnp.float32)
         wide[at, :, :size] = block.reshape(n_gcol * stride, size)
-    mine = position("pair") % NX
     value = None
-    for step, col_ref in enumerate(col_refs):
-        first = (mine + (NX - step)) % NX * (n_grow * doubled)
+    for source in range(NX):
+        lefts = range(source * stride // NX, (source + 1) * stride // NX)
         left = jnp.concatenate(
-            [jnp.concatenate([wide[at, pl.ds(first + place, n_gcol, stride=stride), :]
-                              for place in range(n_grow * doubled)], axis=0)
+            [jnp.concatenate([wide[at, pl.ds(place, n_gcol, stride=stride), :]
+                              for place in lefts], axis=0)
              for at in range(len(tiles))], axis=1)[:, :wide_sub].astype(jnp.bfloat16)
+        right = col_ref[source * n_xy // NX:(source + 1) * n_xy // NX]
         term = lax.dot_general(
-            left, col_ref[...].reshape(n_grow * depth, width), (((0,), (0,)), ((), ())),
+            left, right.reshape(n_xy // NX * depth, width), (((0,), (0,)), ((), ())),
             preferred_element_type=jnp.float32)
         value = term if value is None else value + term
     total[...] = value
@@ -266,23 +266,23 @@
         sent_ref[...] = total[pl.ds(pl.multiple_of(target * sub, 8), sub), :].astype(jnp.bfloat16)
 
 
-def tile(row, cols, n_z):
+def tile(row, col, n_z):
     n_gcol, rows, wide_sub = row.shape
-    width = cols[0].shape[2]
+    width = col.shape[2]
     sub = wide_sub // n_z
     vmem = pl.BlockSpec(memory_space=pltpu.VMEM)
     return pl.pallas_call(
         tile_kernel,
         out_shape=[jax.ShapeDtypeStruct((sub, width), jnp.float32)]
         + [jax.ShapeDtypeStruct((sub, width), jnp.bfloat16)] * (n_z - 1),
-        in_specs=[vmem] * (1 + NX),
+        in_specs=[vmem] * 2,
         out_specs=[vmem] * n_z,
         scratch_shapes=[pltpu.VMEM((-(-wide_sub // LANES), n_gcol * rows, LANES), jnp.float32),
                         pltpu.VMEM((wide_sub, width), jnp.float32)],
         compiler_params=pltpu.CompilerParams(vmem_limit_bytes=40 * 1024 * 1024),
         cost_estimate=pl.CostEstimate(
             flops=2 * n_gcol * rows * wide_sub * width, bytes_accessed=5 * 10**6, transcendentals=0),
-    )(row, *cols)
+    )(row, col)
 
 
 def local(valence, conduction, valence_energy, conduction_energy, pair_valence, pair_conduction,
@@ -299,14 +299,10 @@
         pair_valence, pair_conduction, pair_count, valence_energy, conduction_energy,
         valence, conduction, g_index, n_xy, n_z * sub, n_gcol)
     row = lax.all_to_all(row, ("pair", "grow"), 0, 0, tiled=True, axis_index_groups=xy_groups)
-    col = spread(lax.all_gather(col, "gcol", axis=0, tiled=True), row, n_grow)
-    col = lax.all_to_all(col, "grow", 0, 0, tiled=True)
+    col, row = spread(lax.all_gather(col, "gcol", axis=0, tiled=True), row, n_xy)
+    col = lax.all_to_all(col, ("pair", "grow"), 0, 0, tiled=True, axis_index_groups=xy_groups)
     row = lax.all_gather(row.reshape(1, -1, n_z * sub), "gcol", axis=0, tiled=True)
-    cols = [col] + [
-        lax.ppermute(col, "pair", [(z * NX + x, z * NX + (x + step) % NX)
-                                   for z in range(n_z) for x in range(NX)])
-        for step in range(1, NX)]
-    own, *sent = tile(row, cols, n_z)
+    own, *sent = tile(row, col, n_z)
     for step, block in enumerate(sent, 1):
         own = own + lax.ppermute(block, "pair", [(z * NX + x, (z + step) % n_z * NX + x)
                                                  for z in range(n_z) for x in range(NX)])

time: 127 us -> 131 us (1.031)
  waiting for transfers between devices: 12.7 us -> 41.3 us
  blocking collectives: 73.2 us -> 46.6 us
  local copies, waits for them, and re-layouts: 1.59 us -> 3 us
    all_to_all x0 -> x1, waiting for transfers between devices: none -> 33.7 us  [local(): lax.all_to_all(col, ('pair', 'grow'), 0, 0, tiled=True, axis_index_groups...]
    all_to_all x1 -> x0, blocking collectives: 25.1 us -> none  [local(): col = lax.all_to_all(col, 'grow', 0, 0, tiled=True)]
    ppermute x3 -> x0, starting transfers between devices: 9.28 us -> none  [local(): lax.ppermute(col, 'pair', [(z * NX + x, z * NX + (x + step) % NX) for z i...]
    all_to_all x0 -> x1, starting transfers between devices: none -> 9.17 us  [local(): lax.all_to_all(col, ('pair', 'grow'), 0, 0, tiled=True, axis_index_groups...]
    ppermute x3 -> x0, waiting for transfers between devices: 4.06 us -> none  [local(): lax.ppermute(col, 'pair', [(z * NX + x, z * NX + (x + step) % NX) for z i...]
    all_gather x1, blocking collectives: 20.7 us -> 19 us  [local(): lax.all_gather(row.reshape(1, -1, n_z * sub), 'gcol', axis=0, tiled=True)]
    unnamed x0 -> x2, local copies, waits for them, and re-layouts: none -> 1.4 us
  transfers between devices with their start and end apart: 6 -> 4, of which waited for: 3 -> 3; matrix products, arithmetic and copies ran while one was open for 1% -> 1% of each run, Pallas kernels for 0% -> 0%
where the time goes in v6:
time: 131 us; the launch traced here: 130 us
  blocking collectives  46.6 us (36%)
  waiting for transfers between devices  41.3 us (32%)
  starting transfers between devices  25.9 us (20%)
  Pallas kernels  11.5 us (9%)
  local copies, waits for them, and re-layouts  3 us (2%)
    all_to_all x1, waiting for transfers between devices, local(): lax.all_to_all(col, ('pair', 'grow'), 0, 0, tiled=True, axis_index_groups...  33.7 us
    all_gather x1, blocking collectives, local(): lax.all_gather(col, 'gcol', axis=0, tiled=True)  27.6 us
    all_gather x1, blocking collectives, local(): lax.all_gather(row.reshape(1, -1, n_z * sub), 'gcol', axis=0, tiled=True)  19 us
    all_to_all x1, starting transfers between devices, local(): lax.all_to_all(row, ('pair', 'grow'), 0, 0, tiled=True, axis_index_groups...  10.5 us
    pallas_call x1, Pallas kernels, amplitudes_of(): pl.pallas_call(amplitude_kernel, out_shape=(jax.ShapeDtypeStruct((1, doub...  9.36 us
    all_to_all x1, starting transfers between devices, local(): lax.all_to_all(col, ('pair', 'grow'), 0, 0, tiled=True, axis_index_groups...  9.17 us
    ppermute x2, waiting for transfers between devices, local(): lax.ppermute(block, 'pair', [(z * NX + x, (z + step) % n_z * NX + x) for...  7.6 us
    ppermute x2, starting transfers between devices, local(): lax.ppermute(block, 'pair', [(z * NX + x, (z + step) % n_z * NX + x) for...  6.18 us
  transfers between devices with their start and end apart: 4, of which 3 were waited for; matrix products, arithmetic and copies ran while one was open for 1% of the time, Pallas kernels for 0%

profile of v6, /device:TPU:1, one launch (start us, length us, event | category | flops | bytes accessed | tf_op | source)
XLA Modules:
  0.0 129.9 jit_solution(6239943342746845881)
XLA Ops:
  0.7 9.4 %shard_map.127 = (bf16[1,32,1152]{2,1,0:T(8,128)(2,1)}, bf16[32,4,288]{2,1,0:T(4,128)(2,1)}) custom-call(s32[2]{0:T(128)} %pv_hbm.1, s32[2]{0:T(128)} %pc_hbm.1, s32[1]{0:T(128)S(6)} %copy.18.count_hbm, f32[48]{0:T(128)} %ve_hbm.1, f32[16]{0:T(128)} %ce_hbm.1, bf16[48,32768]{1,0:T(8,128)(2,1)} %valence_hbm.1, bf16[16,32768]{1,0:T(8,128)(2,1)} %conduction_hbm.1, ...), custom_call_target="tpu_custom_call" | custom-call | flops 4000000000 | bytes 5000000 | tf_op jit(solution)/shard_map/pallas_call | solution.py:189
  10.0 10.5 %all-to-all-start = ((bf16[32,4,288]{2,1,0:T(4,128)(2,1)}), bf16[32,4,288]{2,1,0:T(4,128)(2,1)S(1)}, u32[]{:S(2)}, u32[]{:S(2)}) async-start(bf16[32,4,288]{2,1,0:T(4,128)(2,1)} %get-tuple-element.13), calls=%async_computation | async-start | bytes 196608 | tf_op jit(solution)/shard_map/all_to_all | solution.py:301
  20.5 27.6 %all_gather.6.in_ref = bf16[8,32,1152]{2,1,0:T(8,128)(2,1)S(1)} all-gather(bf16[1,32,1152]{2,1,0:T(8,128)(2,1)} %get-tuple-element.12), channel_id=1, replica_groups=mesh['pair'=12,'grow'=8,'gcol'=8] {'gcol'}, dimensions={0}, use_global_device_ids=true | all-gather | bytes 663552 | tf_op jit(solution)/shard_map/all_gather | solution.py:302
  48.1 0.0 all-to-all-done.row_ref
  48.1 0.5 shard_map.128
  48.6 0.0 copy-start
  48.6 1.4 %copy-done = bf16[32,32,1152]{2,1,0:T(8,128)(2,1)} copy-done((bf16[32,32,1152]{2,1,0:T(8,128)(2,1)}, bf16[32,32,1152]{2,1,0:T(8,128)(2,1)S(1)}, u32[]{:S(2)}) %copy-start) | copy-done | bytes 2359320
  50.0 9.2 %all-to-all-start.1 = ((bf16[32,32,1152]{2,1,0:T(8,128)(2,1)}), bf16[32,32,1152]{2,1,0:T(8,128)(2,1)S(1)}, u32[]{:S(2)}, u32[]{:S(2)}) async-start(bf16[32,32,1152]{2,1,0:T(8,128)(2,1)} %copy-done), calls=%async_computation.1 | async-start | bytes 4718592 | tf_op jit(solution)/shard_map/all_to_all | solution.py:303
  59.2 0.1 reshape.7
  59.2 0.1 copy.15
  59.4 19.0 %all_gather.7 = bf16[8,128,288]{1,2,0:T(8,128)(2,1)} all-gather(bf16[1,128,288]{1,2,0:T(8,128)(2,1)S(1)} %copy.15), channel_id=1, replica_groups=mesh['pair'=12,'grow'=8,'gcol'=8] {'gcol'}, dimensions={0}, use_global_device_ids=true | all-gather | bytes 663552 | tf_op jit(solution)/shard_map/all_gather | solution.py:304
  78.4 1.4 %copy.16.row_ref = bf16[8,128,288]{2,1,0:T(8,128)(2,1)S(1)} copy(bf16[8,128,288]{1,2,0:T(8,128)(2,1)} %all_gather.7) | data formatting | bytes 1179648 | tf_op jit(solution)/shard_map/all_gather | solution.py:304
  79.8 33.7 %all-to-all-done.1.col_ref = bf16[32,32,1152]{2,1,0:T(8,128)(2,1)S(1)} async-done(((bf16[32,32,1152]{2,1,0:T(8,128)(2,1)}), bf16[32,32,1152]{2,1,0:T(8,128)(2,1)S(1)}, u32[]{:S(2)}, u32[]{:S(2)}) %all-to-all-start.1) | async-done | bytes 2359328 | tf_op jit(solution)/shard_map/all_to_all | solution.py:303
  113.6 1.7 %shard_map.129 = (f32[96,1152]{1,0:T(8,128)S(1)}, bf16[96,1152]{1,0:T(8,128)(2,1)S(1)}, bf16[96,1152]{1,0:T(8,128)(2,1)S(1)}) custom-call(bf16[8,128,288]{2,1,0:T(8,128)(2,1)S(1)} %copy.16.row_ref, bf16[32,32,1152]{2,1,0:T(8,128)(2,1)S(1)} %all-to-all-done.1.col_ref), custom_call_target="tpu_custom_call" | custom-call | flops 679477248 | bytes 5000000 | tf_op jit(solution)/shard_map/pallas_call | solution.py:274
  115.3 3.7 %collective-permute-start = (bf16[96,1152]{1,0:T(8,128)(2,1)S(1)}, bf16[96,1152]{1,0:T(8,128)(2,1)S(1)}, u32[]{:S(2)}, u32[]{:S(2)}) collective-permute-start(bf16[96,1152]{1,0:T(8,128)(2,1)S(1)} %get-tuple-element.17), channel_id=1, source_target_pairs={{0,256},{64,320},{128,384},{192,448},{256,512},{320,576},{384,640}... | collective-permute-start | bytes 663560 | tf_op jit(solution)/shard_map/ppermute | solution.py:307
  119.0 2.5 %collective-permute-start.1 = (bf16[96,1152]{1,0:T(8,128)(2,1)S(1)}, bf16[96,1152]{1,0:T(8,128)(2,1)S(1)}, u32[]{:S(2)}, u32[]{:S(2)}) collective-permute-start(bf16[96,1152]{1,0:T(8,128)(2,1)S(1)} %get-tuple-element.18), channel_id=1, source_target_pairs={{0,512},{64,576},{128,640},{192,704},{256,0},{320,64},{384,128},{4... | collective-permute-start | bytes 663560 | tf_op jit(solution)/shard_map/ppermute | solution.py:307
  121.5 1.4 %collective-permute-done = bf16[96,1152]{1,0:T(8,128)(2,1)S(1)} collective-permute-done((bf16[96,1152]{1,0:T(8,128)(2,1)S(1)}, bf16[96,1152]{1,0:T(8,128)(2,1)S(1)}, u32[]{:S(2)}, u32[]{:S(2)}) %collective-permute-start) | collective-permute-done | bytes 221216 | tf_op jit(solution)/shard_map/ppermute | solution.py:307
  122.8 6.2 %collective-permute-done.1 = bf16[96,1152]{1,0:T(8,128)(2,1)S(1)} collective-permute-done((bf16[96,1152]{1,0:T(8,128)(2,1)S(1)}, bf16[96,1152]{1,0:T(8,128)(2,1)S(1)}, u32[]{:S(2)}, u32[]{:S(2)}) %collective-permute-start.1) | collective-permute-done | bytes 221216 | tf_op jit(solution)/shard_map/ppermute | solution.py:307
  129.1 0.8 negate_multiply_fusion
Async XLA Ops:
  10.0 38.1 %all-to-all-start = ((bf16[32,4,288]{2,1,0:T(4,128)(2,1)}), bf16[32,4,288]{2,1,0:T(4,128)(2,1)S(1)}, u32[]{:S(2)}, u32[]{:S(2)}) async-start(bf16[32,4,288]{2,1,0:T(4,128)(2,1)} %get-tuple-element.13), calls=%async_computation | async-start | bytes 196608 | tf_op jit(solution)/shard_map/all_to_all | solution.py:301
  48.6 1.4 %copy-start = (bf16[32,32,1152]{2,1,0:T(8,128)(2,1)}, bf16[32,32,1152]{2,1,0:T(8,128)(2,1)S(1)}, u32[]{:S(2)}) copy-start(bf16[32,32,1152]{2,1,0:T(8,128)(2,1)S(1)} %get-tuple-element.15) | copy-start | bytes 7077892
  50.0 63.6 %all-to-all-start.1 = ((bf16[32,32,1152]{2,1,0:T(8,128)(2,1)}), bf16[32,32,1152]{2,1,0:T(8,128)(2,1)S(1)}, u32[]{:S(2)}, u32[]{:S(2)}) async-start(bf16[32,32,1152]{2,1,0:T(8,128)(2,1)} %copy-done), calls=%async_computation.1 | async-start | bytes 4718592 | tf_op jit(solution)/shard_map/all_to_all | solution.py:303
  115.3 7.6 %collective-permute-start = (bf16[96,1152]{1,0:T(8,128)(2,1)S(1)}, bf16[96,1152]{1,0:T(8,128)(2,1)S(1)}, u32[]{:S(2)}, u32[]{:S(2)}) collective-permute-start(bf16[96,1152]{1,0:T(8,128)(2,1)S(1)} %get-tuple-element.17), channel_id=1, source_target_pairs={{0,256},{64,320},{128,384},{192,448},{256,512},{320,576},{384,640}... | collective-permute-start | bytes 663560 | tf_op jit(solution)/shard_map/ppermute | solution.py:307
  119.0 10.1 %collective-permute-start.1 = (bf16[96,1152]{1,0:T(8,128)(2,1)S(1)}, bf16[96,1152]{1,0:T(8,128)(2,1)S(1)}, u32[]{:S(2)}, u32[]{:S(2)}) collective-permute-start(bf16[96,1152]{1,0:T(8,128)(2,1)S(1)} %get-tuple-element.18), channel_id=1, source_target_pairs={{0,512},{64,576},{128,640},{192,704},{256,0},{320,64},{384,128},{4... | collective-permute-start | bytes 663560 | tf_op jit(solution)/shard_map/ppermute | solution.py:307

commit v7 on v5

--- a/solution.py
+++ b/solution.py
@@ -1,3 +1,5 @@
+import functools
+
 import numpy as np
 import ml_dtypes
 
@@ -12,7 +14,7 @@
 NX = 4
 LANES = 128
 ROWS = 256
-CHUNK = 384
+CHUNK = 768
 
 
 def split(table):
@@ -113,21 +115,23 @@
               for at, (source, target) in enumerate(zip(sources, targets))]
     for copy in copies:
         copy.start()
-    for copy in copies[:4]:
+    for copy in copies[:3]:
         copy.wait()
-    picks = [(valence_ref, pv_ref[slot]) for slot in range(slots)]
-    picks += [(conduction_ref, pc_ref[slot]) for slot in range(slots)]
-
-    def widen(tile, carry):
+
+    def widen(picks, tile, carry):
         lanes = pl.ds(pl.multiple_of(tile * LANES, LANES), LANES)
         rows = pl.ds(pl.multiple_of(tile * 8, 8), 8)
-        for at, (ref, band) in enumerate(picks):
+        for at, ref, band in picks:
             start = pl.multiple_of(band // 16 * 16, 16)
             block = ref[pl.ds(start, 16), lanes].astype(jnp.float32)
             wide[at, rows, :] = jnp.where(band % 16 >= 8, block[8:], block[:8])
         return carry
 
-    lax.fori_loop(0, ROWS, widen, 0, unroll=8)
+    picks = [(slots + slot, conduction_ref, pc_ref[slot]) for slot in range(slots)]
+    lax.fori_loop(0, ROWS, functools.partial(widen, picks), 0, unroll=16)
+    copies[3].wait()
+    picks = [(slot, valence_ref, pv_ref[slot]) for slot in range(slots)]
+    lax.fori_loop(0, ROWS, functools.partial(widen, picks), 0, unroll=16)
     for copy in copies[4:]:
         copy.wait()
 
@@ -165,7 +169,7 @@
         flat[0:4, lanes] = select(cells, amp[...])
         return carry
 
-    lax.fori_loop(0, flat.shape[1] // CHUNK, pick, 0, unroll=3)
+    lax.fori_loop(0, flat.shape[1] // CHUNK, pick, 0, unroll=4)
     for place in range(n_xy):
         starts = [(z * n_xy + place) * sub for z in range(3)]
         block = jnp.concatenate([flat[0:doubled, at:at + sub] for at in starts], axis=1)

time: 127 us -> 124 us (0.976)
  Pallas kernels: 11.2 us -> 9.15 us
    pallas_call x1, Pallas kernels: 9.36 us -> 7.32 us  [amplitudes_of(): pl.pallas_call(amplitude_kernel, out_shape=(jax.ShapeDtypeStruct((1, doub...]
where the time goes in v7:
time: 124 us
  blocking collectives  73.1 us (59%)
  starting transfers between devices  26 us (21%)
  waiting for transfers between devices  12.6 us (10%)
  Pallas kernels  9.15 us (7%)
  local copies, waits for them, and re-layouts  1.59 us (1%)
    all_gather x1, blocking collectives, local(): col = spread(lax.all_gather(col, 'gcol', axis=0, tiled=True), row, n_grow)  27.6 us
    all_to_all x1, blocking collectives, local(): col = lax.all_to_all(col, 'grow', 0, 0, tiled=True)  24.8 us
    all_gather x1, blocking collectives, local(): lax.all_gather(row.reshape(1, -1, n_z * sub), 'gcol', axis=0, tiled=True)  20.8 us
    all_to_all x1, starting transfers between devices, local(): lax.all_to_all(row, ('pair', 'grow'), 0, 0, tiled=True, axis_index_groups...  10.5 us
    ppermute x3, starting transfers between devices, local(): lax.ppermute(col, 'pair', [(z * NX + x, z * NX + (x + step) % NX) for z i...  9.28 us
    ppermute x2, waiting for transfers between devices, local(): lax.ppermute(block, 'pair', [(z * NX + x, (z + step) % n_z * NX + x) for...  8.63 us
    pallas_call x1, Pallas kernels, amplitudes_of(): pl.pallas_call(amplitude_kernel, out_shape=(jax.ShapeDtypeStruct((1, doub...  7.32 us
    ppermute x2, starting transfers between devices, local(): lax.ppermute(block, 'pair', [(z * NX + x, (z + step) % n_z * NX + x) for...  6.18 us
  transfers between devices with their start and end apart: 6, of which 3 were waited for; matrix products, arithmetic and copies ran while one was open for 1% of the time, Pallas kernels for 0%

profile of v7, /device:TPU:1, one launch (start us, length us, event | category | flops | bytes accessed | tf_op | source)
XLA Modules:
  0.0 124.1 jit_solution(3077862028130596616)
XLA Ops:
  0.7 7.3 %shard_map.127 = (bf16[1,32,1152]{2,1,0:T(8,128)(2,1)}, bf16[32,4,288]{2,1,0:T(4,128)(2,1)}) custom-call(s32[2]{0:T(128)} %pv_hbm.1, s32[2]{0:T(128)} %pc_hbm.1, s32[1]{0:T(128)S(6)} %copy.16.count_hbm, f32[48]{0:T(128)} %ve_hbm.1, f32[16]{0:T(128)} %ce_hbm.1, bf16[48,32768]{1,0:T(8,128)(2,1)} %valence_hbm.1, bf16[16,32768]{1,0:T(8,128)(2,1)} %conduction_hbm.1, ...), custom_call_target="tpu_custom_call" | custom-call | flops 4000000000 | bytes 5000000 | tf_op jit(solution)/shard_map/pallas_call | solution.py:193
  8.0 10.5 %all-to-all-start = ((bf16[32,4,288]{2,1,0:T(4,128)(2,1)}), bf16[32,4,288]{2,1,0:T(4,128)(2,1)S(1)}, u32[]{:S(2)}, u32[]{:S(2)}) async-start(bf16[32,4,288]{2,1,0:T(4,128)(2,1)} %get-tuple-element.10), calls=%async_computation | async-start | bytes 196608 | tf_op jit(solution)/shard_map/all_to_all | solution.py:305
  18.5 27.6 %all_gather.7.in_ref = bf16[8,32,1152]{2,1,0:T(8,128)(2,1)S(1)} all-gather(bf16[1,32,1152]{2,1,0:T(8,128)(2,1)} %get-tuple-element.11), channel_id=1, replica_groups=mesh['pair'=12,'grow'=8,'gcol'=8] {'gcol'}, dimensions={0}, use_global_device_ids=true | all-gather | bytes 663552 | tf_op jit(solution)/shard_map/all_gather | solution.py:306
  46.1 0.0 all-to-all-done.first_ref
  46.1 0.2 shard_map.128
  46.3 24.8 %all_to_all.10.refs_0_ = bf16[8,32,1152]{2,1,0:T(8,128)(2,1)S(1)} all-to-all(bf16[8,32,1152]{2,1,0:T(8,128)(2,1)S(1)} %shard_map.128), channel_id=1, replica_groups=mesh['pair'=12,'grow'=8,'gcol'=8] {'grow'}, dimensions={0} | all-to-all | bytes 1179648 | tf_op jit(solution)/shard_map/all_to_all | solution.py:307
  71.1 4.4 %collective-permute-start.2 = (bf16[8,32,1152]{2,1,0:T(8,128)(2,1)S(1)}, bf16[8,32,1152]{2,1,0:T(8,128)(2,1)S(1)}, u32[]{:S(2)}, u32[]{:S(2)}) collective-permute-start(bf16[8,32,1152]{2,1,0:T(8,128)(2,1)S(1)} %all_to_all.10.refs_0_), channel_id=1, source_target_pairs={{0,192},{64,0},{128,64},{192,128},{256,448},{320,256},{384,320},{4... | collective-permute-start | bytes 1769480 | tf_op jit(solution)/shard_map/ppermute | solution.py:310
  75.5 2.4 %collective-permute-start.1 = (bf16[8,32,1152]{2,1,0:T(8,128)(2,1)S(1)}, bf16[8,32,1152]{2,1,0:T(8,128)(2,1)S(1)}, u32[]{:S(2)}, u32[]{:S(2)}) collective-permute-start(bf16[8,32,1152]{2,1,0:T(8,128)(2,1)S(1)} %all_to_all.10.refs_0_), channel_id=1, source_target_pairs={{0,128},{64,192},{128,0},{192,64},{256,384},{320,448},{384,256},{4... | collective-permute-start | bytes 1769480 | tf_op jit(solution)/shard_map/ppermute | solution.py:310
  77.9 2.5 %collective-permute-start = (bf16[8,32,1152]{2,1,0:T(8,128)(2,1)S(1)}, bf16[8,32,1152]{2,1,0:T(8,128)(2,1)S(1)}, u32[]{:S(2)}, u32[]{:S(2)}) collective-permute-start(bf16[8,32,1152]{2,1,0:T(8,128)(2,1)S(1)} %all_to_all.10.refs_0_), channel_id=1, source_target_pairs={{0,64},{64,128},{128,192},{192,0},{256,320},{320,384},{384,448},{4... | collective-permute-start | bytes 1769480 | tf_op jit(solution)/shard_map/ppermute | solution.py:310
  80.4 0.1 reshape.7
  80.5 0.1 copy.14
  80.6 20.8 %all_gather.6 = bf16[8,128,288]{1,2,0:T(8,128)(2,1)} all-gather(bf16[1,128,288]{1,2,0:T(8,128)(2,1)S(1)} %copy.14), channel_id=1, replica_groups=mesh['pair'=12,'grow'=8,'gcol'=8] {'gcol'}, dimensions={0}, use_global_device_ids=true | all-gather | bytes 663552 | tf_op jit(solution)/shard_map/all_gather | solution.py:308
  101.4 1.4 %copy.15.row_ref = bf16[8,128,288]{2,1,0:T(8,128)(2,1)S(1)} copy(bf16[8,128,288]{1,2,0:T(8,128)(2,1)} %all_gather.6) | data formatting | bytes 1179648 | tf_op jit(solution)/shard_map/all_gather | solution.py:308
  102.8 0.0 collective-permute-done.2.refs_3_
  102.8 0.0 collective-permute-done.1.refs_2_
  102.8 4.0 %collective-permute-done.refs_1_ = bf16[8,32,1152]{2,1,0:T(8,128)(2,1)S(1)} collective-permute-done((bf16[8,32,1152]{2,1,0:T(8,128)(2,1)S(1)}, bf16[8,32,1152]{2,1,0:T(8,128)(2,1)S(1)}, u32[]{:S(2)}, u32[]{:S(2)}) %collective-permute-start) | collective-permute-done | bytes 589856 | tf_op jit(solution)/shard_map/ppermute | solution.py:310
  106.8 1.6 %shard_map.129 = (f32[96,1152]{1,0:T(8,128)S(1)}, bf16[96,1152]{1,0:T(8,128)(2,1)S(1)}, bf16[96,1152]{1,0:T(8,128)(2,1)S(1)}) custom-call(bf16[8,128,288]{2,1,0:T(8,128)(2,1)S(1)} %copy.15.row_ref, bf16[8,32,1152]{2,1,0:T(8,128)(2,1)S(1)} %all_to_all.10.refs_0_, bf16[8,32,1152]{2,1,0:T(8,128)(2,1)S(1)} %collective-permute-done.refs_1_, ...), custom_call_target="tpu_custom_call" | custom-call | flops 679477248 | bytes 5000000 | tf_op jit(solution)/shard_map/pallas_call | solution.py:278
  108.4 3.8 %collective-permute-start.3 = (bf16[96,1152]{1,0:T(8,128)(2,1)S(1)}, bf16[96,1152]{1,0:T(8,128)(2,1)S(1)}, u32[]{:S(2)}, u32[]{:S(2)}) collective-permute-start(bf16[96,1152]{1,0:T(8,128)(2,1)S(1)} %get-tuple-element.13), channel_id=1, source_target_pairs={{0,256},{64,320},{128,384},{192,448},{256,512},{320,576},{384,640}... | collective-permute-start | bytes 663560 | tf_op jit(solution)/shard_map/ppermute | solution.py:315
  112.2 2.4 %collective-permute-start.4 = (bf16[96,1152]{1,0:T(8,128)(2,1)S(1)}, bf16[96,1152]{1,0:T(8,128)(2,1)S(1)}, u32[]{:S(2)}, u32[]{:S(2)}) collective-permute-start(bf16[96,1152]{1,0:T(8,128)(2,1)S(1)} %get-tuple-element.14), channel_id=1, source_target_pairs={{0,512},{64,576},{128,640},{192,704},{256,0},{320,64},{384,128},{4... | collective-permute-start | bytes 663560 | tf_op jit(solution)/shard_map/ppermute | solution.py:315
  114.6 3.1 %collective-permute-done.3 = bf16[96,1152]{1,0:T(8,128)(2,1)S(1)} collective-permute-done((bf16[96,1152]{1,0:T(8,128)(2,1)S(1)}, bf16[96,1152]{1,0:T(8,128)(2,1)S(1)}, u32[]{:S(2)}, u32[]{:S(2)}) %collective-permute-start.3) | collective-permute-done | bytes 221216 | tf_op jit(solution)/shard_map/ppermute | solution.py:315
  117.7 5.5 %collective-permute-done.4 = bf16[96,1152]{1,0:T(8,128)(2,1)S(1)} collective-permute-done((bf16[96,1152]{1,0:T(8,128)(2,1)S(1)}, bf16[96,1152]{1,0:T(8,128)(2,1)S(1)}, u32[]{:S(2)}, u32[]{:S(2)}) %collective-permute-start.4) | collective-permute-done | bytes 221216 | tf_op jit(solution)/shard_map/ppermute | solution.py:315
  123.2 0.8 negate_multiply_fusion
Async XLA Ops:
  8.0 38.1 %all-to-all-start = ((bf16[32,4,288]{2,1,0:T(4,128)(2,1)}), bf16[32,4,288]{2,1,0:T(4,128)(2,1)S(1)}, u32[]{:S(2)}, u32[]{:S(2)}) async-start(bf16[32,4,288]{2,1,0:T(4,128)(2,1)} %get-tuple-element.10), calls=%async_computation | async-start | bytes 196608 | tf_op jit(solution)/shard_map/all_to_all | solution.py:305
  71.1 31.7 %collective-permute-start.2 = (bf16[8,32,1152]{2,1,0:T(8,128)(2,1)S(1)}, bf16[8,32,1152]{2,1,0:T(8,128)(2,1)S(1)}, u32[]{:S(2)}, u32[]{:S(2)}) collective-permute-start(bf16[8,32,1152]{2,1,0:T(8,128)(2,1)S(1)} %all_to_all.10.refs_0_), channel_id=1, source_target_pairs={{0,192},{64,0},{128,64},{192,128},{256,448},{320,256},{384,320},{4... | collective-permute-start | bytes 1769480 | tf_op jit(solution)/shard_map/ppermute | solution.py:310
  75.5 27.3 %collective-permute-start.1 = (bf16[8,32,1152]{2,1,0:T(8,128)(2,1)S(1)}, bf16[8,32,1152]{2,1,0:T(8,128)(2,1)S(1)}, u32[]{:S(2)}, u32[]{:S(2)}) collective-permute-start(bf16[8,32,1152]{2,1,0:T(8,128)(2,1)S(1)} %all_to_all.10.refs_0_), channel_id=1, source_target_pairs={{0,128},{64,192},{128,0},{192,64},{256,384},{320,448},{384,256},{4... | collective-permute-start | bytes 1769480 | tf_op jit(solution)/shard_map/ppermute | solution.py:310
  77.9 28.9 %collective-permute-start = (bf16[8,32,1152]{2,1,0:T(8,128)(2,1)S(1)}, bf16[8,32,1152]{2,1,0:T(8,128)(2,1)S(1)}, u32[]{:S(2)}, u32[]{:S(2)}) collective-permute-start(bf16[8,32,1152]{2,1,0:T(8,128)(2,1)S(1)} %all_to_all.10.refs_0_), channel_id=1, source_target_pairs={{0,64},{64,128},{128,192},{192,0},{256,320},{320,384},{384,448},{4... | collective-permute-start | bytes 1769480 | tf_op jit(solution)/shard_map/ppermute | solution.py:310
  108.4 9.3 %collective-permute-start.3 = (bf16[96,1152]{1,0:T(8,128)(2,1)S(1)}, bf16[96,1152]{1,0:T(8,128)(2,1)S(1)}, u32[]{:S(2)}, u32[]{:S(2)}) collective-permute-start(bf16[96,1152]{1,0:T(8,128)(2,1)S(1)} %get-tuple-element.13), channel_id=1, source_target_pairs={{0,256},{64,320},{128,384},{192,448},{256,512},{320,576},{384,640}... | collective-permute-start | bytes 663560 | tf_op jit(solution)/shard_map/ppermute | solution.py:315
  112.2 11.1 %collective-permute-start.4 = (bf16[96,1152]{1,0:T(8,128)(2,1)S(1)}, bf16[96,1152]{1,0:T(8,128)(2,1)S(1)}, u32[]{:S(2)}, u32[]{:S(2)}) collective-permute-start(bf16[96,1152]{1,0:T(8,128)(2,1)S(1)} %get-tuple-element.14), channel_id=1, source_target_pairs={{0,512},{64,576},{128,640},{192,704},{256,0},{320,64},{384,128},{4... | collective-permute-start | bytes 663560 | tf_op jit(solution)/shard_map/ppermute | solution.py:315

commit v8 on v7

--- a/solution.py
+++ b/solution.py
@@ -84,11 +84,14 @@
     row_id = lax.broadcasted_iota(jnp.int32, (ROWS, width), 0).astype(jnp.bfloat16)
     one, zero = jnp.ones((), jnp.bfloat16), jnp.zeros((), jnp.bfloat16)
     hot = jnp.where(row_id == row.astype(jnp.bfloat16), one, zero)
-    picked = dot(amplitudes, hot)
-    mask = lax.broadcasted_iota(jnp.int32, (64, width), 0) == lane
+    picked = dot(amplitudes, hot).astype(jnp.bfloat16)
+    mask = lax.broadcasted_iota(jnp.int32, (64, width), 0).astype(jnp.bfloat16) == lane.astype(
+        jnp.bfloat16)
     parts = []
     for part in range(4):
-        block = jnp.where(mask, picked[part * 64:part * 64 + 64], 0.0)
+        block = jnp.where(mask, picked[part * 64:part * 64 + 64], zero)
+        block = block[:32] + block[32:]
+        block = (block[:16] + block[16:]).astype(jnp.float32)
         total = jnp.sum(block, axis=0, keepdims=True)
         parts.append(total * sign if part % 2 else total)
     return jnp.concatenate(parts, axis=0)
@@ -102,10 +105,12 @@
                      lane_hbm, row_hbm, same_hbm, swap_hbm, last_hbm, g_hbm,
                      col_ref, rows_ref, pv_ref, pc_ref, count_ref, ve_ref, ce_ref, valence_ref,
                      conduction_ref, lane_ref, row_ref, same_ref, swap_ref, last_ref, g_ref,
-                     wide, amp, flat, ordered, sems):
+                     wide, amp, flat, placed, ordered, sems):
     slots = 2
-    n_xy, doubled, wide_sub = rows_ref.shape
+    members, doubled, double_sub = rows_ref.shape
+    wide_sub = double_sub // 2
     sub = wide_sub // 3
+    n_xy = placed.shape[0]
     width = col_ref.shape[2]
     sources = (pv_hbm, pc_hbm, conduction_hbm, valence_hbm, lane_hbm, row_hbm, same_hbm,
                swap_hbm, last_hbm, g_hbm, count_hbm, ve_hbm, ce_hbm)
@@ -173,7 +178,15 @@
     for place in range(n_xy):
         starts = [(z * n_xy + place) * sub for z in range(3)]
         block = jnp.concatenate([flat[0:doubled, at:at + sub] for at in starts], axis=1)
-        rows_ref[place] = block.astype(jnp.bfloat16)
+        placed[place, 0:doubled, 0:wide_sub] = block
+    n_grow = members // 2
+    low = position("pair") % NX // 2 * 2
+    for member in range(members):
+        own = low + member // n_grow
+        near = placed[own * n_grow + member % n_grow]
+        far = placed[(NX - 1 - own) * n_grow + member % n_grow]
+        rows_ref[member] = jnp.concatenate(
+            [near[0:doubled, 0:wide_sub], far[0:doubled, 0:wide_sub]], axis=1).astype(jnp.bfloat16)
     targets = flat.shape[1] // width
     for at in range(width // LANES):
         for target in range(targets):
@@ -194,7 +207,7 @@
         amplitude_kernel,
         out_shape=(
             jax.ShapeDtypeStruct((1, doubled * n_gcol, width), jnp.bfloat16),
-            jax.ShapeDtypeStruct((n_xy, doubled, wide_sub), jnp.bfloat16)),
+            jax.ShapeDtypeStruct((n_xy * 2 // NX, doubled, 2 * wide_sub), jnp.bfloat16)),
         in_specs=[hbm] * 13,
         out_specs=(pl.BlockSpec(memory_space=pltpu.VMEM),) * 2,
         scratch_shapes=[pltpu.SMEM(a.shape, a.dtype) for a in (pv, pc, count, ve, ce)]
@@ -203,6 +216,7 @@
             pltpu.VMEM((4, 8 * ROWS, LANES), jnp.float32),
             pltpu.VMEM((ROWS, ROWS), jnp.bfloat16),
             pltpu.VMEM((8, g_index.shape[0]), jnp.float32),
+            pltpu.VMEM((n_xy, 8, wide_sub), jnp.float32),
             pltpu.VMEM((width // LANES, doubled * n_gcol, LANES), jnp.float32),
             pltpu.SemaphoreType.DMA((13,)),
         ],
@@ -240,52 +254,53 @@
 
 
 def tile_kernel(row_ref, *refs):
-    col_refs, own_ref, sent_refs = refs[:NX], refs[NX], refs[NX + 1:-2]
+    col_refs, own_ref, sent_refs = refs[:2], refs[2], refs[3:-2]
     wide, total = refs[-2:]
     n_grow, depth, width = col_refs[0].shape
-    n_gcol, stride, wide_sub = row_ref.shape
-    doubled = depth // n_gcol
-    tiles = lane_tiles(wide_sub)
+    n_gcol, stride, double_sub = row_ref.shape
+    tiles = lane_tiles(double_sub)
     for at, (lane, size) in enumerate(tiles):
         block = row_ref[:, :, lane:lane + size].astype(jnp.float32)
         wide[at, :, :size] = block.reshape(n_gcol * stride, size)
-    mine = position("pair") % NX
+    mine = position("pair") % 2
     value = None
     for step, col_ref in enumerate(col_refs):
-        first = (mine + (NX - step)) % NX * (n_grow * doubled)
+        first = (mine + step) % 2 * (stride // 2)
         left = jnp.concatenate(
             [jnp.concatenate([wide[at, pl.ds(first + place, n_gcol, stride=stride), :]
-                              for place in range(n_grow * doubled)], axis=0)
-             for at in range(len(tiles))], axis=1)[:, :wide_sub].astype(jnp.bfloat16)
+                              for place in range(stride // 2)], axis=0)
+             for at in range(len(tiles))], axis=1)[:, :double_sub].astype(jnp.bfloat16)
         term = lax.dot_general(
             left, col_ref[...].reshape(n_grow * depth, width), (((0,), (0,)), ((), ())),
             preferred_element_type=jnp.float32)
         value = term if value is None else value + term
     total[...] = value
     sub = own_ref.shape[0]
+    layers = double_sub // (2 * sub)
     layer = position("pair") // NX
-    own_ref[...] = total[pl.ds(pl.multiple_of(layer * sub, 8), sub), :]
-    for at, sent_ref in enumerate(sent_refs):
-        target = (layer + at + 1) % (len(sent_refs) + 1)
-        sent_ref[...] = total[pl.ds(pl.multiple_of(target * sub, 8), sub), :].astype(jnp.bfloat16)
+    for at, out_ref in enumerate((own_ref, *sent_refs)):
+        row = at // layers * layers + (layer + at) % layers
+        block = total[pl.ds(pl.multiple_of(row * sub, 8), sub), :]
+        out_ref[...] = block.astype(out_ref.dtype)
 
 
 def tile(row, cols, n_z):
-    n_gcol, rows, wide_sub = row.shape
+    n_gcol, rows, double_sub = row.shape
     width = cols[0].shape[2]
-    sub = wide_sub // n_z
+    sub = double_sub // (2 * n_z)
     vmem = pl.BlockSpec(memory_space=pltpu.VMEM)
     return pl.pallas_call(
         tile_kernel,
         out_shape=[jax.ShapeDtypeStruct((sub, width), jnp.float32)]
-        + [jax.ShapeDtypeStruct((sub, width), jnp.bfloat16)] * (n_z - 1),
-        in_specs=[vmem] * (1 + NX),
-        out_specs=[vmem] * n_z,
-        scratch_shapes=[pltpu.VMEM((-(-wide_sub // LANES), n_gcol * rows, LANES), jnp.float32),
-                        pltpu.VMEM((wide_sub, width), jnp.float32)],
+        + [jax.ShapeDtypeStruct((sub, width), jnp.bfloat16)] * (2 * n_z - 1),
+        in_specs=[vmem] * 3,
+        out_specs=[vmem] * (2 * n_z),
+        scratch_shapes=[pltpu.VMEM((-(-double_sub // LANES), n_gcol * rows, LANES), jnp.float32),
+                        pltpu.VMEM((double_sub, width), jnp.float32)],
         compiler_params=pltpu.CompilerParams(vmem_limit_bytes=40 * 1024 * 1024),
         cost_estimate=pl.CostEstimate(
-            flops=2 * n_gcol * rows * wide_sub * width, bytes_accessed=5 * 10**6, transcendentals=0),
+            flops=2 * n_gcol * rows * double_sub * width, bytes_accessed=5 * 10**6,
+            transcendentals=0),
     )(row, *cols)
 
 
@@ -297,23 +312,22 @@
     width = total_g // n_gcol
     sub = total_g // (n_pair * n_grow)
     n_xy = NX * n_grow
-    xy_groups = [[(z * NX + x) * n_grow + y for x in range(NX) for y in range(n_grow)]
-                 for z in range(n_z)]
+    near_groups = [[(z * NX + 2 * half + x) * n_grow + y for x in range(2) for y in range(n_grow)]
+                   for z in range(n_z) for half in range(NX // 2)]
     col, row = amplitudes_of(
         pair_valence, pair_conduction, pair_count, valence_energy, conduction_energy,
         valence, conduction, g_index, n_xy, n_z * sub, n_gcol)
-    row = lax.all_to_all(row, ("pair", "grow"), 0, 0, tiled=True, axis_index_groups=xy_groups)
+    row = lax.all_to_all(row, ("pair", "grow"), 0, 0, tiled=True, axis_index_groups=near_groups)
     col = spread(lax.all_gather(col, "gcol", axis=0, tiled=True), row, n_grow)
     col = lax.all_to_all(col, "grow", 0, 0, tiled=True)
-    row = lax.all_gather(row.reshape(1, -1, n_z * sub), "gcol", axis=0, tiled=True)
-    cols = [col] + [
-        lax.ppermute(col, "pair", [(z * NX + x, z * NX + (x + step) % NX)
-                                   for z in range(n_z) for x in range(NX)])
-        for step in range(1, NX)]
-    own, *sent = tile(row, cols, n_z)
-    for step, block in enumerate(sent, 1):
-        own = own + lax.ppermute(block, "pair", [(z * NX + x, (z + step) % n_z * NX + x)
-                                                 for z in range(n_z) for x in range(NX)])
+    row = lax.all_gather(row.reshape(1, -1, 2 * n_z * sub), "gcol", axis=0, tiled=True)
+    devices = [(z, x) for z in range(n_z) for x in range(NX)]
+    beside = lax.ppermute(col, "pair", [(z * NX + x, z * NX + (x ^ 1)) for z, x in devices])
+    own, *sent = tile(row, [col, beside], n_z)
+    for at, block in enumerate(sent, 1):
+        own = own + lax.ppermute(block, "pair", [
+            (z * NX + x, (z + at) % n_z * NX + (NX - 1 - x if at >= n_z else x))
+            for z, x in devices])
     total_slots = pair_valence.shape[0] * n_pair * n_grow * n_gcol
     return -own / jnp.sqrt(jnp.float32(total_slots))
 

time: 124 us -> 123 us (level); the launches traced: 124 us -> 122 us
  waiting for transfers between devices: 12.6 us -> 8.29 us
  starting transfers between devices: 26 us -> 30.2 us
  local copies, waits for them, and re-layouts: 1.59 us -> 0.04 us
    ppermute x5 -> x6, starting transfers between devices: 15.5 us -> 21.5 us  [the longest x5 18.5 us: local(): lax.ppermute(block, 'pair', [(z * NX + x, (z + at) % n_z * NX + (NX - 1 -...]
    ppermute x5 -> x6, waiting for transfers between devices: 12.6 us -> 8.28 us  [the longest x5 8.28 us: local(): lax.ppermute(block, 'pair', [(z * NX + x, (z + at) % n_z * NX + (NX - 1 -...]
    all_to_all x1, starting transfers between devices: 10.5 us -> 8.7 us  [local(): lax.all_to_all(row, ('pair', 'grow'), 0, 0, tiled=True, axis_index_groups...]
    all_gather x1 -> x0, local copies, waits for them, and re-layouts: 1.42 us -> none  [local(): lax.all_gather(row.reshape(1, -1, n_z * sub), 'gcol', axis=0, tiled=True)]
    all_gather x1, blocking collectives: 20.8 us -> 19.4 us  [local(): lax.all_gather(row.reshape(1, -1, 2 * n_z * sub), 'gcol', axis=0, tiled=T...]
  transfers between devices with their start and end apart: 6 -> 7, of which waited for: 3 -> 2; matrix products, arithmetic and copies ran while one was open for 1% -> 0% of each run, Pallas kernels for 0% -> 0%
where the time goes in v8:
time: 123 us; the launch traced here: 122 us
  blocking collectives  72.2 us (59%)
  starting transfers between devices  30.2 us (25%)
  Pallas kernels  9.19 us (7%)
  waiting for transfers between devices  8.29 us (7%)
    all_gather x1, blocking collectives, local(): col = spread(lax.all_gather(col, 'gcol', axis=0, tiled=True), row, n_grow)  27.6 us
    all_to_all x1, blocking collectives, local(): col = lax.all_to_all(col, 'grow', 0, 0, tiled=True)  25.2 us
    all_gather x1, blocking collectives, local(): lax.all_gather(row.reshape(1, -1, 2 * n_z * sub), 'gcol', axis=0, tiled=T...  19.4 us
    ppermute x5, starting transfers between devices, local(): lax.ppermute(block, 'pair', [(z * NX + x, (z + at) % n_z * NX + (NX - 1 -...  18.5 us
    all_to_all x1, starting transfers between devices, local(): lax.all_to_all(row, ('pair', 'grow'), 0, 0, tiled=True, axis_index_groups...  8.7 us
    ppermute x5, waiting for transfers between devices, local(): lax.ppermute(block, 'pair', [(z * NX + x, (z + at) % n_z * NX + (NX - 1 -...  8.28 us
    pallas_call x1, Pallas kernels, amplitudes_of(): pl.pallas_call(amplitude_kernel, out_shape=(jax.ShapeDtypeStruct((1, doub...  7.19 us
    ppermute x1, starting transfers between devices, local(): lax.ppermute(col, 'pair', [(z * NX + x, z * NX + (x ^ 1)) for z, x in dev...  3.08 us
  transfers between devices with their start and end apart: 7, of which 2 were waited for; matrix products, arithmetic and copies ran while one was open for 0% of the time, Pallas kernels for 0%

profile of v8, /device:TPU:1, one launch (start us, length us, event | category | flops | bytes accessed | tf_op | source)
XLA Modules:
  0.0 121.6 jit_solution(6737383941546264855)
XLA Ops:
  0.7 7.2 %shard_map.127 = (bf16[1,32,1152]{2,1,0:T(8,128)(2,1)}, bf16[16,4,576]{2,1,0:T(4,128)(2,1)}) custom-call(s32[2]{0:T(128)} %pv_hbm.1, s32[2]{0:T(128)} %pc_hbm.1, s32[1]{0:T(128)S(6)} %copy.14.count_hbm, f32[48]{0:T(128)} %ve_hbm.1, f32[16]{0:T(128)} %ce_hbm.1, bf16[48,32768]{1,0:T(8,128)(2,1)} %valence_hbm.1, bf16[16,32768]{1,0:T(8,128)(2,1)} %conduction_hbm.1, ...), custom_call_target="tpu_custom_call" | custom-call | flops 4000000000 | bytes 5000000 | tf_op jit(solution)/shard_map/pallas_call | solution.py:206
  7.8 8.7 %all-to-all-start = ((bf16[16,4,576]{2,1,0:T(4,128)(2,1)}), bf16[16,4,576]{2,1,0:T(4,128)(2,1)S(1)}, u32[]{:S(2)}, u32[]{:S(2)}) async-start(bf16[16,4,576]{2,1,0:T(4,128)(2,1)} %get-tuple-element.13), calls=%async_computation | async-start | bytes 163840 | tf_op jit(solution)/shard_map/all_to_all | solution.py:320
  16.6 27.6 %all_gather.7.in_ref = bf16[8,32,1152]{2,1,0:T(8,128)(2,1)S(1)} all-gather(bf16[1,32,1152]{2,1,0:T(8,128)(2,1)} %get-tuple-element.14), channel_id=1, replica_groups=mesh['pair'=12,'grow'=8,'gcol'=8] {'gcol'}, dimensions={0}, use_global_device_ids=true | all-gather | bytes 663552 | tf_op jit(solution)/shard_map/all_gather | solution.py:321
  44.2 0.0 all-to-all-done.first_ref
  44.2 0.2 shard_map.128
  44.4 25.2 %all_to_all.10.refs_0_ = bf16[8,32,1152]{2,1,0:T(8,128)(2,1)S(1)} all-to-all(bf16[8,32,1152]{2,1,0:T(8,128)(2,1)S(1)} %shard_map.128), channel_id=1, replica_groups=mesh['pair'=12,'grow'=8,'gcol'=8] {'grow'}, dimensions={0} | all-to-all | bytes 1179648 | tf_op jit(solution)/shard_map/all_to_all | solution.py:322
  69.6 3.1 %collective-permute-start = (bf16[8,32,1152]{2,1,0:T(8,128)(2,1)S(1)}, bf16[8,32,1152]{2,1,0:T(8,128)(2,1)S(1)}, u32[]{:S(2)}, u32[]{:S(2)}) collective-permute-start(bf16[8,32,1152]{2,1,0:T(8,128)(2,1)S(1)} %all_to_all.10.refs_0_), channel_id=1, source_target_pairs={{0,64},{64,0},{128,192},{192,128},{256,320},{320,256},{384,448},{4... | collective-permute-start | bytes 1769480 | tf_op jit(solution)/shard_map/ppermute | solution.py:325
  72.7 19.4 %all_gather.6.row_ref = bf16[8,64,576]{2,1,0:T(8,128)(2,1)S(1)} all-gather(bf16[1,64,576]{2,1,0:T(8,128)(2,1)S(1)} %reshape.7), channel_id=1, replica_groups=mesh['pair'=12,'grow'=8,'gcol'=8] {'gcol'}, dimensions={0}, use_global_device_ids=true | all-gather | bytes 663552 | tf_op jit(solution)/shard_map/all_gather | solution.py:323
  92.1 0.0 collective-permute-done.refs_1_
  92.1 1.8 %shard_map.129 = (f32[96,1152]{1,0:T(8,128)S(1)}, bf16[96,1152]{1,0:T(8,128)(2,1)S(1)}, bf16[96,1152]{1,0:T(8,128)(2,1)S(1)}, bf16[96,1152]{1,0:T(8,128)(2,1)S(1...) custom-call(bf16[8,64,576]{2,1,0:T(8,128)(2,1)S(1)} %all_gather.6.row_ref, ...), custom_call_target="tpu_custom_call" | custom-call | flops 679477248 | bytes 5000000 | tf_op jit(solution)/shard_map/pallas_call | solution.py:292
  93.9 4.0 %collective-permute-start.1 = (bf16[96,1152]{1,0:T(8,128)(2,1)S(1)}, bf16[96,1152]{1,0:T(8,128)(2,1)S(1)}, u32[]{:S(2)}, u32[]{:S(2)}) collective-permute-start(bf16[96,1152]{1,0:T(8,128)(2,1)S(1)} %get-tuple-element.16), channel_id=1, source_target_pairs={{0,256},{64,320},{128,384},{192,448},{256,512},{320,576},{384,640}... | collective-permute-start | bytes 663560 | tf_op jit(solution)/shard_map/ppermute | solution.py:328
  97.9 3.0 %collective-permute-start.2 = (bf16[96,1152]{1,0:T(8,128)(2,1)S(1)}, bf16[96,1152]{1,0:T(8,128)(2,1)S(1)}, u32[]{:S(2)}, u32[]{:S(2)}) collective-permute-start(bf16[96,1152]{1,0:T(8,128)(2,1)S(1)} %get-tuple-element.17), channel_id=1, source_target_pairs={{0,512},{64,576},{128,640},{192,704},{256,0},{320,64},{384,128},{4... | collective-permute-start | bytes 663560 | tf_op jit(solution)/shard_map/ppermute | solution.py:328
  100.9 3.2 %collective-permute-start.3 = (bf16[96,1152]{1,0:T(8,128)(2,1)S(1)}, bf16[96,1152]{1,0:T(8,128)(2,1)S(1)}, u32[]{:S(2)}, u32[]{:S(2)}) collective-permute-start(bf16[96,1152]{1,0:T(8,128)(2,1)S(1)} %get-tuple-element.18), channel_id=1, source_target_pairs={{0,192},{64,128},{128,64},{192,0},{256,448},{320,384},{384,320},{4... | collective-permute-start | bytes 663560 | tf_op jit(solution)/shard_map/ppermute | solution.py:328
  104.1 3.4 %collective-permute-start.4 = (bf16[96,1152]{1,0:T(8,128)(2,1)S(1)}, bf16[96,1152]{1,0:T(8,128)(2,1)S(1)}, u32[]{:S(2)}, u32[]{:S(2)}) collective-permute-start(bf16[96,1152]{1,0:T(8,128)(2,1)S(1)} %get-tuple-element.19), channel_id=1, source_target_pairs={{0,448},{64,384},{128,320},{192,256},{256,704},{320,640},{384,576}... | collective-permute-start | bytes 663560 | tf_op jit(solution)/shard_map/ppermute | solution.py:328
  107.5 4.8 %collective-permute-start.5 = (bf16[96,1152]{1,0:T(8,128)(2,1)S(1)}, bf16[96,1152]{1,0:T(8,128)(2,1)S(1)}, u32[]{:S(2)}, u32[]{:S(2)}) collective-permute-start(bf16[96,1152]{1,0:T(8,128)(2,1)S(1)} %get-tuple-element.20), channel_id=1, source_target_pairs={{0,704},{64,640},{128,576},{192,512},{256,192},{320,128},{384,64},... | collective-permute-start | bytes 663560 | tf_op jit(solution)/shard_map/ppermute | solution.py:328
  112.4 0.0 collective-permute-done.1
  112.4 0.0 collective-permute-done.2
  112.4 0.0 collective-permute-done.3
  112.4 2.8 %collective-permute-done.4 = bf16[96,1152]{1,0:T(8,128)(2,1)S(1)} collective-permute-done((bf16[96,1152]{1,0:T(8,128)(2,1)S(1)}, bf16[96,1152]{1,0:T(8,128)(2,1)S(1)}, u32[]{:S(2)}, u32[]{:S(2)}) %collective-permute-start.4) | collective-permute-done | bytes 221216 | tf_op jit(solution)/shard_map/ppermute | solution.py:328
  115.2 5.5 %collective-permute-done.5 = bf16[96,1152]{1,0:T(8,128)(2,1)S(1)} collective-permute-done((bf16[96,1152]{1,0:T(8,128)(2,1)S(1)}, bf16[96,1152]{1,0:T(8,128)(2,1)S(1)}, u32[]{:S(2)}, u32[]{:S(2)}) %collective-permute-start.5) | collective-permute-done | bytes 221216 | tf_op jit(solution)/shard_map/ppermute | solution.py:328
  120.7 0.9 negate_multiply_fusion
  (1 shorter events, 0.0 us)
Async XLA Ops:
  7.8 36.3 %all-to-all-start = ((bf16[16,4,576]{2,1,0:T(4,128)(2,1)}), bf16[16,4,576]{2,1,0:T(4,128)(2,1)S(1)}, u32[]{:S(2)}, u32[]{:S(2)}) async-start(bf16[16,4,576]{2,1,0:T(4,128)(2,1)} %get-tuple-element.13), calls=%async_computation | async-start | bytes 163840 | tf_op jit(solution)/shard_map/all_to_all | solution.py:320
  69.6 22.5 %collective-permute-start = (bf16[8,32,1152]{2,1,0:T(8,128)(2,1)S(1)}, bf16[8,32,1152]{2,1,0:T(8,128)(2,1)S(1)}, u32[]{:S(2)}, u32[]{:S(2)}) collective-permute-start(bf16[8,32,1152]{2,1,0:T(8,128)(2,1)S(1)} %all_to_all.10.refs_0_), channel_id=1, source_target_pairs={{0,64},{64,0},{128,192},{192,128},{256,320},{320,256},{384,448},{4... | collective-permute-start | bytes 1769480 | tf_op jit(solution)/shard_map/ppermute | solution.py:325
  93.9 18.5 %collective-permute-start.1 = (bf16[96,1152]{1,0:T(8,128)(2,1)S(1)}, bf16[96,1152]{1,0:T(8,128)(2,1)S(1)}, u32[]{:S(2)}, u32[]{:S(2)}) collective-permute-start(bf16[96,1152]{1,0:T(8,128)(2,1)S(1)} %get-tuple-element.16), channel_id=1, source_target_pairs={{0,256},{64,320},{128,384},{192,448},{256,512},{320,576},{384,640}... | collective-permute-start | bytes 663560 | tf_op jit(solution)/shard_map/ppermute | solution.py:328
  97.9 14.5 %collective-permute-start.2 = (bf16[96,1152]{1,0:T(8,128)(2,1)S(1)}, bf16[96,1152]{1,0:T(8,128)(2,1)S(1)}, u32[]{:S(2)}, u32[]{:S(2)}) collective-permute-start(bf16[96,1152]{1,0:T(8,128)(2,1)S(1)} %get-tuple-element.17), channel_id=1, source_target_pairs={{0,512},{64,576},{128,640},{192,704},{256,0},{320,64},{384,128},{4... | collective-permute-start | bytes 663560 | tf_op jit(solution)/shard_map/ppermute | solution.py:328
  100.9 11.5 %collective-permute-start.3 = (bf16[96,1152]{1,0:T(8,128)(2,1)S(1)}, bf16[96,1152]{1,0:T(8,128)(2,1)S(1)}, u32[]{:S(2)}, u32[]{:S(2)}) collective-permute-start(bf16[96,1152]{1,0:T(8,128)(2,1)S(1)} %get-tuple-element.18), channel_id=1, source_target_pairs={{0,192},{64,128},{128,64},{192,0},{256,448},{320,384},{384,320},{4... | collective-permute-start | bytes 663560 | tf_op jit(solution)/shard_map/ppermute | solution.py:328
  104.1 11.1 %collective-permute-start.4 = (bf16[96,1152]{1,0:T(8,128)(2,1)S(1)}, bf16[96,1152]{1,0:T(8,128)(2,1)S(1)}, u32[]{:S(2)}, u32[]{:S(2)}) collective-permute-start(bf16[96,1152]{1,0:T(8,128)(2,1)S(1)} %get-tuple-element.19), channel_id=1, source_target_pairs={{0,448},{64,384},{128,320},{192,256},{256,704},{320,640},{384,576}... | collective-permute-start | bytes 663560 | tf_op jit(solution)/shard_map/ppermute | solution.py:328
  107.5 13.2 %collective-permute-start.5 = (bf16[96,1152]{1,0:T(8,128)(2,1)S(1)}, bf16[96,1152]{1,0:T(8,128)(2,1)S(1)}, u32[]{:S(2)}, u32[]{:S(2)}) collective-permute-start(bf16[96,1152]{1,0:T(8,128)(2,1)S(1)} %get-tuple-element.20), channel_id=1, source_target_pairs={{0,704},{64,640},{128,576},{192,512},{256,192},{320,128},{384,64},... | collective-permute-start | bytes 663560 | tf_op jit(solution)/shard_map/ppermute | solution.py:328

commit v9 on v8

--- a/solution.py
+++ b/solution.py
@@ -179,12 +179,10 @@
         starts = [(z * n_xy + place) * sub for z in range(3)]
         block = jnp.concatenate([flat[0:doubled, at:at + sub] for at in starts], axis=1)
         placed[place, 0:doubled, 0:wide_sub] = block
-    n_grow = members // 2
-    low = position("pair") % NX // 2 * 2
+    parity = position("grow") % 2
     for member in range(members):
-        own = low + member // n_grow
-        near = placed[own * n_grow + member % n_grow]
-        far = placed[(NX - 1 - own) * n_grow + member % n_grow]
+        near = placed[2 * member + parity]
+        far = placed[2 * member + 1 - parity]
         rows_ref[member] = jnp.concatenate(
             [near[0:doubled, 0:wide_sub], far[0:doubled, 0:wide_sub]], axis=1).astype(jnp.bfloat16)
     targets = flat.shape[1] // width
@@ -207,7 +205,7 @@
         amplitude_kernel,
         out_shape=(
             jax.ShapeDtypeStruct((1, doubled * n_gcol, width), jnp.bfloat16),
-            jax.ShapeDtypeStruct((n_xy * 2 // NX, doubled, 2 * wide_sub), jnp.bfloat16)),
+            jax.ShapeDtypeStruct((n_xy // 2, doubled, 2 * wide_sub), jnp.bfloat16)),
         in_specs=[hbm] * 13,
         out_specs=(pl.BlockSpec(memory_space=pltpu.VMEM),) * 2,
         scratch_shapes=[pltpu.SMEM(a.shape, a.dtype) for a in (pv, pc, count, ve, ce)]
@@ -254,24 +252,24 @@
 
 
 def tile_kernel(row_ref, *refs):
-    col_refs, own_ref, sent_refs = refs[:2], refs[2], refs[3:-2]
+    col_refs, own_ref, sent_refs = refs[:NX], refs[NX], refs[NX + 1:-2]
     wide, total = refs[-2:]
-    n_grow, depth, width = col_refs[0].shape
+    n_half, depth, width = col_refs[0].shape
     n_gcol, stride, double_sub = row_ref.shape
     tiles = lane_tiles(double_sub)
     for at, (lane, size) in enumerate(tiles):
         block = row_ref[:, :, lane:lane + size].astype(jnp.float32)
         wide[at, :, :size] = block.reshape(n_gcol * stride, size)
-    mine = position("pair") % 2
+    mine = position("pair") % NX
     value = None
     for step, col_ref in enumerate(col_refs):
-        first = (mine + step) % 2 * (stride // 2)
+        first = (mine + (NX - step)) % NX * (stride // NX)
         left = jnp.concatenate(
             [jnp.concatenate([wide[at, pl.ds(first + place, n_gcol, stride=stride), :]
-                              for place in range(stride // 2)], axis=0)
+                              for place in range(stride // NX)], axis=0)
              for at in range(len(tiles))], axis=1)[:, :double_sub].astype(jnp.bfloat16)
         term = lax.dot_general(
-            left, col_ref[...].reshape(n_grow * depth, width), (((0,), (0,)), ((), ())),
+            left, col_ref[...].reshape(n_half * depth, width), (((0,), (0,)), ((), ())),
             preferred_element_type=jnp.float32)
         value = term if value is None else value + term
     total[...] = value
@@ -293,7 +291,7 @@
         tile_kernel,
         out_shape=[jax.ShapeDtypeStruct((sub, width), jnp.float32)]
         + [jax.ShapeDtypeStruct((sub, width), jnp.bfloat16)] * (2 * n_z - 1),
-        in_specs=[vmem] * 3,
+        in_specs=[vmem] * (1 + NX),
         out_specs=[vmem] * (2 * n_z),
         scratch_shapes=[pltpu.VMEM((-(-double_sub // LANES), n_gcol * rows, LANES), jnp.float32),
                         pltpu.VMEM((double_sub, width), jnp.float32)],
@@ -312,22 +310,26 @@
     width = total_g // n_gcol
     sub = total_g // (n_pair * n_grow)
     n_xy = NX * n_grow
-    near_groups = [[(z * NX + 2 * half + x) * n_grow + y for x in range(2) for y in range(n_grow)]
-                   for z in range(n_z) for half in range(NX // 2)]
+    halves_y = [list(range(parity, n_grow, 2)) for parity in range(2)]
+    near_groups = [[(z * NX + x) * n_grow + y for x in range(NX) for y in half]
+                   for z in range(n_z) for half in halves_y]
     col, row = amplitudes_of(
         pair_valence, pair_conduction, pair_count, valence_energy, conduction_energy,
         valence, conduction, g_index, n_xy, n_z * sub, n_gcol)
     row = lax.all_to_all(row, ("pair", "grow"), 0, 0, tiled=True, axis_index_groups=near_groups)
-    col = spread(lax.all_gather(col, "gcol", axis=0, tiled=True), row, n_grow)
-    col = lax.all_to_all(col, "grow", 0, 0, tiled=True)
+    col = spread(lax.all_gather(col, "gcol", axis=0, tiled=True), row, n_grow // 2)
+    col = lax.all_to_all(col, "grow", 0, 0, tiled=True, axis_index_groups=halves_y)
     row = lax.all_gather(row.reshape(1, -1, 2 * n_z * sub), "gcol", axis=0, tiled=True)
-    devices = [(z, x) for z in range(n_z) for x in range(NX)]
-    beside = lax.ppermute(col, "pair", [(z * NX + x, z * NX + (x ^ 1)) for z, x in devices])
-    own, *sent = tile(row, [col, beside], n_z)
+    cols = [col] + [
+        lax.ppermute(col, "pair", [(z * NX + x, z * NX + (x + step) % NX)
+                                   for z in range(n_z) for x in range(NX)])
+        for step in range(1, NX)]
+    own, *sent = tile(row, cols, n_z)
     for at, block in enumerate(sent, 1):
-        own = own + lax.ppermute(block, "pair", [
-            (z * NX + x, (z + at) % n_z * NX + (NX - 1 - x if at >= n_z else x))
-            for z, x in devices])
+        own = own + lax.ppermute(block, ("pair", "grow"), [
+            ((z * NX + x) * n_grow + y,
+             ((z + at) % n_z * NX + x) * n_grow + (y ^ 1 if at >= n_z else y))
+            for z in range(n_z) for x in range(NX) for y in range(n_grow)])
     total_slots = pair_valence.shape[0] * n_pair * n_grow * n_gcol
     return -own / jnp.sqrt(jnp.float32(total_slots))
 

time: 123 us -> 123 us (level); the launches traced: 122 us -> 123 us
  starting transfers between devices: 30.2 us -> 36.4 us
  blocking collectives: 72.2 us -> 66.6 us
    all_to_all x1, blocking collectives: 25.2 us -> 16.6 us  [local(): lax.all_to_all(col, 'grow', 0, 0, tiled=True, axis_index_groups=halves_y)]
    ppermute x6 -> x8, starting transfers between devices: 21.5 us -> 26.2 us  [the longest x5 16.9 us: local(): lax.ppermute(block, ('pair', 'grow'), [((z * NX + x) * n_grow + y, ((z +...]
    all_gather x1, blocking collectives: 19.4 us -> 22.2 us  [local(): lax.all_gather(row.reshape(1, -1, 2 * n_z * sub), 'gcol', axis=0, tiled=T...]
    all_to_all x1, starting transfers between devices: 8.7 us -> 10.2 us  [local(): lax.all_to_all(row, ('pair', 'grow'), 0, 0, tiled=True, axis_index_groups...]
    ppermute x6 -> x8, waiting for transfers between devices: 8.28 us -> 8.94 us  [the longest x5 8.94 us: local(): lax.ppermute(block, ('pair', 'grow'), [((z * NX + x) * n_grow + y, ((z +...]
  transfers between devices with their start and end apart: 7 -> 9, of which waited for: 2 -> 2; matrix products, arithmetic and copies ran while one was open for 0% -> 0% of each run, Pallas kernels for 0% -> 0%
where the time goes in v9:
time: 123 us
  blocking collectives  66.6 us (54%)
  starting transfers between devices  36.4 us (30%)
  Pallas kernels  9.25 us (8%)
  waiting for transfers between devices  8.95 us (7%)
    all_gather x1, blocking collectives, local(): lax.all_gather(col, 'gcol', axis=0, tiled=True)  27.8 us
    all_gather x1, blocking collectives, local(): lax.all_gather(row.reshape(1, -1, 2 * n_z * sub), 'gcol', axis=0, tiled=T...  22.2 us
    ppermute x5, starting transfers between devices, local(): lax.ppermute(block, ('pair', 'grow'), [((z * NX + x) * n_grow + y, ((z +...  16.9 us
    all_to_all x1, blocking collectives, local(): lax.all_to_all(col, 'grow', 0, 0, tiled=True, axis_index_groups=halves_y)  16.6 us
    all_to_all x1, starting transfers between devices, local(): lax.all_to_all(row, ('pair', 'grow'), 0, 0, tiled=True, axis_index_groups...  10.2 us
    ppermute x3, starting transfers between devices, local(): lax.ppermute(col, 'pair', [(z * NX + x, z * NX + (x + step) % NX) for z i...  9.27 us
    ppermute x5, waiting for transfers between devices, local(): lax.ppermute(block, ('pair', 'grow'), [((z * NX + x) * n_grow + y, ((z +...  8.94 us
    pallas_call x1, Pallas kernels, amplitudes_of(): pl.pallas_call(amplitude_kernel, out_shape=(jax.ShapeDtypeStruct((1, doub...  7.19 us
  transfers between devices with their start and end apart: 9, of which 2 were waited for; matrix products, arithmetic and copies ran while one was open for 0% of the time, Pallas kernels for 0%

profile of v9, /device:TPU:1, one launch (start us, length us, event | category | flops | bytes accessed | tf_op | source)
XLA Modules:
  0.0 123.0 jit_solution(1066833805469092698)
XLA Ops:
  0.7 7.2 %shard_map.127 = (bf16[1,32,1152]{2,1,0:T(8,128)(2,1)}, bf16[16,4,576]{2,1,0:T(4,128)(2,1)}) custom-call(s32[2]{0:T(128)} %pv_hbm.1, s32[2]{0:T(128)} %pc_hbm.1, s32[1]{0:T(128)S(6)} %copy.14.count_hbm, f32[48]{0:T(128)} %ve_hbm.1, f32[16]{0:T(128)} %ce_hbm.1, bf16[48,32768]{1,0:T(8,128)(2,1)} %valence_hbm.1, bf16[16,32768]{1,0:T(8,128)(2,1)} %conduction_hbm.1, ...), custom_call_target="tpu_custom_call" | custom-call | flops 4000000000 | bytes 5000000 | tf_op jit(solution)/shard_map/pallas_call | solution.py:204
  7.8 10.2 %all-to-all-start = ((bf16[16,4,576]{2,1,0:T(4,128)(2,1)}), bf16[16,4,576]{2,1,0:T(4,128)(2,1)S(1)}, u32[]{:S(2)}, u32[]{:S(2)}) async-start(bf16[16,4,576]{2,1,0:T(4,128)(2,1)} %get-tuple-element.13), calls=%async_computation | async-start | bytes 163840 | tf_op jit(solution)/shard_map/all_to_all | solution.py:319
  18.1 27.8 %all_gather.7.in_ref = bf16[8,32,1152]{2,1,0:T(8,128)(2,1)S(1)} all-gather(bf16[1,32,1152]{2,1,0:T(8,128)(2,1)} %get-tuple-element.14), channel_id=1, replica_groups=mesh['pair'=12,'grow'=8,'gcol'=8] {'gcol'}, dimensions={0}, use_global_device_ids=true | all-gather | bytes 663552 | tf_op jit(solution)/shard_map/all_gather | solution.py:320
  45.8 0.0 all-to-all-done.first_ref
  45.8 0.2 shard_map.128
  46.1 16.6 %all_to_all.10.refs_0_ = bf16[4,32,1152]{2,1,0:T(8,128)(2,1)S(1)} all-to-all(bf16[4,32,1152]{2,1,0:T(8,128)(2,1)S(1)} %shard_map.128), channel_id=1, replica_groups={{0,16,32,48},{8,24,40,56},{1,17,33,49},{9,25,41,57},{2,18,34,50},{10,26..., dimensions={0} | all-to-all | bytes 589824 | tf_op jit(solution)/shard_map/all_to_all | solution.py:321
  62.7 4.3 %collective-permute-start.2 = (bf16[4,32,1152]{2,1,0:T(8,128)(2,1)S(1)}, bf16[4,32,1152]{2,1,0:T(8,128)(2,1)S(1)}, u32[]{:S(2)}, u32[]{:S(2)}) collective-permute-start(bf16[4,32,1152]{2,1,0:T(8,128)(2,1)S(1)} %all_to_all.10.refs_0_), channel_id=1, source_target_pairs={{0,192},{64,0},{128,64},{192,128},{256,448},{320,256},{384,320},{4... | collective-permute-start | bytes 884744 | tf_op jit(solution)/shard_map/ppermute | solution.py:324
  67.0 2.5 %collective-permute-start.1 = (bf16[4,32,1152]{2,1,0:T(8,128)(2,1)S(1)}, bf16[4,32,1152]{2,1,0:T(8,128)(2,1)S(1)}, u32[]{:S(2)}, u32[]{:S(2)}) collective-permute-start(bf16[4,32,1152]{2,1,0:T(8,128)(2,1)S(1)} %all_to_all.10.refs_0_), channel_id=1, source_target_pairs={{0,128},{64,192},{128,0},{192,64},{256,384},{320,448},{384,256},{4... | collective-permute-start | bytes 884744 | tf_op jit(solution)/shard_map/ppermute | solution.py:324
  69.5 2.5 %collective-permute-start = (bf16[4,32,1152]{2,1,0:T(8,128)(2,1)S(1)}, bf16[4,32,1152]{2,1,0:T(8,128)(2,1)S(1)}, u32[]{:S(2)}, u32[]{:S(2)}) collective-permute-start(bf16[4,32,1152]{2,1,0:T(8,128)(2,1)S(1)} %all_to_all.10.refs_0_), channel_id=1, source_target_pairs={{0,64},{64,128},{128,192},{192,0},{256,320},{320,384},{384,448},{4... | collective-permute-start | bytes 884744 | tf_op jit(solution)/shard_map/ppermute | solution.py:324
  72.0 22.2 %all_gather.6.row_ref = bf16[8,64,576]{2,1,0:T(8,128)(2,1)S(1)} all-gather(bf16[1,64,576]{2,1,0:T(8,128)(2,1)S(1)} %reshape.7), channel_id=1, replica_groups=mesh['pair'=12,'grow'=8,'gcol'=8] {'gcol'}, dimensions={0}, use_global_device_ids=true | all-gather | bytes 663552 | tf_op jit(solution)/shard_map/all_gather | solution.py:322
  94.2 0.0 collective-permute-done.2.refs_3_
  94.2 0.0 collective-permute-done.1.refs_2_
  94.2 0.0 collective-permute-done.refs_1_
  94.3 1.9 %shard_map.129 = (f32[96,1152]{1,0:T(8,128)S(1)}, bf16[96,1152]{1,0:T(8,128)(2,1)S(1)}, bf16[96,1152]{1,0:T(8,128)(2,1)S(1)}, bf16[96,1152]{1,0:T(8,128)(2,1)S(1...) custom-call(bf16[8,64,576]{2,1,0:T(8,128)(2,1)S(1)} %all_gather.6.row_ref, ...), custom_call_target="tpu_custom_call" | custom-call | flops 679477248 | bytes 5000000 | tf_op jit(solution)/shard_map/pallas_call | solution.py:290
  96.1 3.2 %collective-permute-start.3 = (bf16[96,1152]{1,0:T(8,128)(2,1)S(1)}, bf16[96,1152]{1,0:T(8,128)(2,1)S(1)}, u32[]{:S(2)}, u32[]{:S(2)}) collective-permute-start(bf16[96,1152]{1,0:T(8,128)(2,1)S(1)} %get-tuple-element.16), channel_id=1, source_target_pairs={{0,256},{8,264},{16,272},{24,280},{32,288},{40,296},{48,304},{56,3... | collective-permute-start | bytes 663560 | tf_op jit(solution)/shard_map/ppermute | solution.py:329
  99.3 4.2 %collective-permute-start.4 = (bf16[96,1152]{1,0:T(8,128)(2,1)S(1)}, bf16[96,1152]{1,0:T(8,128)(2,1)S(1)}, u32[]{:S(2)}, u32[]{:S(2)}) collective-permute-start(bf16[96,1152]{1,0:T(8,128)(2,1)S(1)} %get-tuple-element.17), channel_id=1, source_target_pairs={{0,512},{8,520},{16,528},{24,536},{32,544},{40,552},{48,560},{56,5... | collective-permute-start | bytes 663560 | tf_op jit(solution)/shard_map/ppermute | solution.py:329
  103.5 2.5 %collective-permute-start.5 = (bf16[96,1152]{1,0:T(8,128)(2,1)S(1)}, bf16[96,1152]{1,0:T(8,128)(2,1)S(1)}, u32[]{:S(2)}, u32[]{:S(2)}) collective-permute-start(bf16[96,1152]{1,0:T(8,128)(2,1)S(1)} %get-tuple-element.18), channel_id=1, source_target_pairs={{0,8},{8,0},{16,24},{24,16},{32,40},{40,32},{48,56},{56,48},{64,72... | collective-permute-start | bytes 663560 | tf_op jit(solution)/shard_map/ppermute | solution.py:329
  106.0 2.8 %collective-permute-start.6 = (bf16[96,1152]{1,0:T(8,128)(2,1)S(1)}, bf16[96,1152]{1,0:T(8,128)(2,1)S(1)}, u32[]{:S(2)}, u32[]{:S(2)}) collective-permute-start(bf16[96,1152]{1,0:T(8,128)(2,1)S(1)} %get-tuple-element.19), channel_id=1, source_target_pairs={{0,264},{8,256},{16,280},{24,272},{32,296},{40,288},{48,312},{56,3... | collective-permute-start | bytes 663560 | tf_op jit(solution)/shard_map/ppermute | solution.py:329
  108.8 4.3 %collective-permute-start.7 = (bf16[96,1152]{1,0:T(8,128)(2,1)S(1)}, bf16[96,1152]{1,0:T(8,128)(2,1)S(1)}, u32[]{:S(2)}, u32[]{:S(2)}) collective-permute-start(bf16[96,1152]{1,0:T(8,128)(2,1)S(1)} %get-tuple-element.20), channel_id=1, source_target_pairs={{0,520},{8,512},{16,536},{24,528},{32,552},{40,544},{48,568},{56,5... | collective-permute-start | bytes 663560 | tf_op jit(solution)/shard_map/ppermute | solution.py:329
  113.1 0.0 collective-permute-done.3
  113.1 0.0 collective-permute-done.4
  113.1 0.0 collective-permute-done.5
  113.1 3.3 %collective-permute-done.6 = bf16[96,1152]{1,0:T(8,128)(2,1)S(1)} collective-permute-done((bf16[96,1152]{1,0:T(8,128)(2,1)S(1)}, bf16[96,1152]{1,0:T(8,128)(2,1)S(1)}, u32[]{:S(2)}, u32[]{:S(2)}) %collective-permute-start.6) | collective-permute-done | bytes 221216 | tf_op jit(solution)/shard_map/ppermute | solution.py:329
  116.5 5.6 %collective-permute-done.7 = bf16[96,1152]{1,0:T(8,128)(2,1)S(1)} collective-permute-done((bf16[96,1152]{1,0:T(8,128)(2,1)S(1)}, bf16[96,1152]{1,0:T(8,128)(2,1)S(1)}, u32[]{:S(2)}, u32[]{:S(2)}) %collective-permute-start.7) | collective-permute-done | bytes 221216 | tf_op jit(solution)/shard_map/ppermute | solution.py:329
  122.1 0.9 negate_multiply_fusion
  (1 shorter events, 0.0 us)
Async XLA Ops:
  7.8 38.0 %all-to-all-start = ((bf16[16,4,576]{2,1,0:T(4,128)(2,1)}), bf16[16,4,576]{2,1,0:T(4,128)(2,1)S(1)}, u32[]{:S(2)}, u32[]{:S(2)}) async-start(bf16[16,4,576]{2,1,0:T(4,128)(2,1)} %get-tuple-element.13), calls=%async_computation | async-start | bytes 163840 | tf_op jit(solution)/shard_map/all_to_all | solution.py:319
  62.7 31.6 %collective-permute-start.2 = (bf16[4,32,1152]{2,1,0:T(8,128)(2,1)S(1)}, bf16[4,32,1152]{2,1,0:T(8,128)(2,1)S(1)}, u32[]{:S(2)}, u32[]{:S(2)}) collective-permute-start(bf16[4,32,1152]{2,1,0:T(8,128)(2,1)S(1)} %all_to_all.10.refs_0_), channel_id=1, source_target_pairs={{0,192},{64,0},{128,64},{192,128},{256,448},{320,256},{384,320},{4... | collective-permute-start | bytes 884744 | tf_op jit(solution)/shard_map/ppermute | solution.py:324
  67.0 27.3 %collective-permute-start.1 = (bf16[4,32,1152]{2,1,0:T(8,128)(2,1)S(1)}, bf16[4,32,1152]{2,1,0:T(8,128)(2,1)S(1)}, u32[]{:S(2)}, u32[]{:S(2)}) collective-permute-start(bf16[4,32,1152]{2,1,0:T(8,128)(2,1)S(1)} %all_to_all.10.refs_0_), channel_id=1, source_target_pairs={{0,128},{64,192},{128,0},{192,64},{256,384},{320,448},{384,256},{4... | collective-permute-start | bytes 884744 | tf_op jit(solution)/shard_map/ppermute | solution.py:324
  69.5 24.8 %collective-permute-start = (bf16[4,32,1152]{2,1,0:T(8,128)(2,1)S(1)}, bf16[4,32,1152]{2,1,0:T(8,128)(2,1)S(1)}, u32[]{:S(2)}, u32[]{:S(2)}) collective-permute-start(bf16[4,32,1152]{2,1,0:T(8,128)(2,1)S(1)} %all_to_all.10.refs_0_), channel_id=1, source_target_pairs={{0,64},{64,128},{128,192},{192,0},{256,320},{320,384},{384,448},{4... | collective-permute-start | bytes 884744 | tf_op jit(solution)/shard_map/ppermute | solution.py:324
  96.1 17.0 %collective-permute-start.3 = (bf16[96,1152]{1,0:T(8,128)(2,1)S(1)}, bf16[96,1152]{1,0:T(8,128)(2,1)S(1)}, u32[]{:S(2)}, u32[]{:S(2)}) collective-permute-start(bf16[96,1152]{1,0:T(8,128)(2,1)S(1)} %get-tuple-element.16), channel_id=1, source_target_pairs={{0,256},{8,264},{16,272},{24,280},{32,288},{40,296},{48,304},{56,3... | collective-permute-start | bytes 663560 | tf_op jit(solution)/shard_map/ppermute | solution.py:329
  99.3 13.8 %collective-permute-start.4 = (bf16[96,1152]{1,0:T(8,128)(2,1)S(1)}, bf16[96,1152]{1,0:T(8,128)(2,1)S(1)}, u32[]{:S(2)}, u32[]{:S(2)}) collective-permute-start(bf16[96,1152]{1,0:T(8,128)(2,1)S(1)} %get-tuple-element.17), channel_id=1, source_target_pairs={{0,512},{8,520},{16,528},{24,536},{32,544},{40,552},{48,560},{56,5... | collective-permute-start | bytes 663560 | tf_op jit(solution)/shard_map/ppermute | solution.py:329
  103.5 9.6 %collective-permute-start.5 = (bf16[96,1152]{1,0:T(8,128)(2,1)S(1)}, bf16[96,1152]{1,0:T(8,128)(2,1)S(1)}, u32[]{:S(2)}, u32[]{:S(2)}) collective-permute-start(bf16[96,1152]{1,0:T(8,128)(2,1)S(1)} %get-tuple-element.18), channel_id=1, source_target_pairs={{0,8},{8,0},{16,24},{24,16},{32,40},{40,32},{48,56},{56,48},{64,72... | collective-permute-start | bytes 663560 | tf_op jit(solution)/shard_map/ppermute | solution.py:329
  106.0 10.5 %collective-permute-start.6 = (bf16[96,1152]{1,0:T(8,128)(2,1)S(1)}, bf16[96,1152]{1,0:T(8,128)(2,1)S(1)}, u32[]{:S(2)}, u32[]{:S(2)}) collective-permute-start(bf16[96,1152]{1,0:T(8,128)(2,1)S(1)} %get-tuple-element.19), channel_id=1, source_target_pairs={{0,264},{8,256},{16,280},{24,272},{32,296},{40,288},{48,312},{56,3... | collective-permute-start | bytes 663560 | tf_op jit(solution)/shard_map/ppermute | solution.py:329
  108.8 13.2 %collective-permute-start.7 = (bf16[96,1152]{1,0:T(8,128)(2,1)S(1)}, bf16[96,1152]{1,0:T(8,128)(2,1)S(1)}, u32[]{:S(2)}, u32[]{:S(2)}) collective-permute-start(bf16[96,1152]{1,0:T(8,128)(2,1)S(1)} %get-tuple-element.20), channel_id=1, source_target_pairs={{0,520},{8,512},{16,536},{24,528},{32,552},{40,544},{48,568},{56,5... | collective-permute-start | bytes 663560 | tf_op jit(solution)/shard_map/ppermute | solution.py:329
